TPU v7x, 128 devices: a whole 4x4x4 slice. The times are simulated.
128 devices in a mesh: pipe: 4 (over z_lo, core), dp: 32 (over z_hi, x, y).
Axes of the slice: x: 4, y: 4, z: 4 (z_hi: 2, z_lo: 2; z = z_hi * 2 + z_lo), core: 2. Of those that a mesh axis runs over, the one named last changes fastest.
Arguments:
- inputs: float32 [2, 64, 88, 400], P(None, 'dp'), may hold values from -6 to 6
- resets: int32 [2, 64], P(None, 'dp'), may hold values from 1 to 87
- in_mask: int32 [2, 64, 400], P(None, 'dp'), may hold values 0 or 1
- mid_mask: int32 [2, 64, 1150], P(None, 'dp'), may hold values 0 or 1
- out_mask: int32 [2, 64, 1150], P(None, 'dp'), may hold values 0 or 1
- w_ih_one: bfloat16 [400, 4600], P(None, 'pipe'), may hold values from -0.3125 to 0.3125
- w_hh_one: bfloat16 [1150, 4600], P(None, 'pipe'), may hold values from -0.1875 to 0.1875
- bias_one: bfloat16 [4600], P('pipe'), may hold values from -3 to 3
- drop_one: int32 [1150, 4600], P(None, 'pipe'), may hold values 0 or 1
- w_ih_two: bfloat16 [1150, 4600], P(None, 'pipe'), may hold values from -0.1875 to 0.1875
- w_hh_two: bfloat16 [1150, 4600], P(None, 'pipe'), may hold values from -0.1875 to 0.1875
- bias_two: bfloat16 [4600], P('pipe'), may hold values from -3 to 3
- drop_two: int32 [1150, 4600], P(None, 'pipe'), may hold values 0 or 1
- cotangent: bfloat16 [2, 64, 88, 1150], P(None, 'dp'), may hold values from -6 to 6
Outputs:
- layer_outputs: bfloat16 [4, 64, 88, 1150], P('pipe', 'dp')
- grad_input: float32 [2, 64, 88, 400], P(None, 'dp', None, 'pipe')
- grad_w_ih_one: float32 [400, 4600], P(None, 'pipe')
- grad_w_hh_one: float32 [1150, 4600], P(None, 'pipe')
- grad_bias_one: float32 [4600], P('pipe')
- grad_w_ih_two: float32 [1150, 4600], P(None, 'pipe')
- grad_w_hh_two: float32 [1150, 4600], P(None, 'pipe')
- grad_bias_two: float32 [4600], P('pipe')
Inputs may be any that keep to these rules, and one draw needn't show every extreme that they name: `resets`: the position in a stream before which its carried state is dropped.
All inputs are finite; a program needn't handle non-finite values. No bound on the sum of `in_mask` or of `mid_mask` or of `out_mask` or of `drop_one` or of `drop_two` on one device may be relied on, other than what follows from the above.
Results may differ from a plain program's by a relative error of at most 0.011.
Values may be sent and summed in bfloat16 or wider, within the bound.
A program may use at most 576 MiB of HBM per device.

v0:
```python
import jax
import jax.numpy as jnp
from jax import lax
from jax.sharding import PartitionSpec as P

SPAN = 44


keep_scale = 4.0 / 3.0
weight_scale = 2.0


def shifted(block, axis, distance):
    devices = range(lax.axis_size(axis))
    route = [(i - distance, i) for i in devices if i - distance in devices]
    return lax.ppermute(block, axis, route)


def partner_2(value, axis, bit):
    mask = 2**bit
    pairs = [(source, source ^ mask) for source in range(lax.axis_size(axis))]
    return lax.ppermute(value, axis, pairs)


def passed_along(value, axis, steps):
    count = lax.axis_size(axis)
    pairs = [(source, (source + steps) % count) for source in range(count)]
    return lax.ppermute(value, axis, pairs)


def split_gates(gates, width):
    gate_in = jax.nn.sigmoid(gates[:, :width])
    gate_forget = jax.nn.sigmoid(gates[:, width : 2 * width])
    gate_cand = jnp.tanh(gates[:, 2 * width : 3 * width])
    gate_out = jax.nn.sigmoid(gates[:, 3 * width :])
    return (gate_in, gate_forget, gate_cand, gate_out)


def recurrence(projected, keep_mask, w_recur, hidden_in, cell_in):
    width = hidden_in.shape[1]

    def advance(carry, items):
        hidden, cell_state = carry
        proj_now, keep_now = items
        keep_col = keep_now[:, None]
        hidden_prev = jnp.where(keep_col, hidden, jnp.zeros_like(hidden))
        cell_prev = jnp.where(keep_col, cell_state, 0.0)
        gates = proj_now + jnp.dot(hidden_prev, w_recur, preferred_element_type=jnp.float32)
        gate_in, gate_forget, gate_cand, gate_out = split_gates(gates, width)
        cell_state = gate_forget * cell_prev + gate_in * gate_cand
        hidden = (gate_out * jnp.tanh(cell_state)).astype(jnp.bfloat16)
        return ((hidden, cell_state), (hidden, gates, cell_state))

    last_pair, emitted = lax.scan(advance, (hidden_in, cell_in), (projected, keep_mask), unroll=4)
    return (emitted[0], emitted[1], emitted[2], last_pair[0], last_pair[1])


def back_steps(gate_values, cells, cell_prev, keep_mask, upstream, w_recur, grad_hidden, grad_cell):
    width = cells.shape[2]

    def retreat(carry, items):
        hidden_back, cell_back = carry
        gates, cell_now, cell_before, keep_now, outer = items
        gate_in, gate_forget, gate_cand, gate_out = split_gates(gates, width)
        cell_tanh = jnp.tanh(cell_now)
        total = hidden_back + outer
        out_grad = total * cell_tanh * gate_out * (1.0 - gate_out)
        cell_total = cell_back + total * gate_out * (1.0 - cell_tanh * cell_tanh)
        in_grad = cell_total * gate_cand * gate_in * (1.0 - gate_in)
        forget_grad = cell_total * cell_before * gate_forget * (1.0 - gate_forget)
        cand_grad = cell_total * gate_in * (1.0 - gate_cand * gate_cand)
        gate_grad = jnp.concatenate([in_grad, forget_grad, cand_grad, out_grad], 1).astype(
            jnp.bfloat16
        )
        hidden_grad = lax.dot_general(
            gate_grad, w_recur, (((1,), (1,)), ((), ())), preferred_element_type=jnp.float32
        )
        keep_col = keep_now[:, None]
        return (
            (
                jnp.where(keep_col, hidden_grad, 0.0),
                jnp.where(keep_col, cell_total * gate_forget, 0.0),
            ),
            gate_grad,
        )

    carry, gate_grads = lax.scan(
        retreat,
        (grad_hidden, grad_cell),
        (gate_values, cells, cell_prev, keep_mask, upstream),
        reverse=True,
        unroll=4,
    )
    return (gate_grads, carry)


def send_down(values):
    return shifted(values, "pipe", 2)


def send_up(values):
    return shifted(values, "pipe", -2)


def two_quarters(values, first, width):
    last = values.ndim - 1
    lower = lax.dynamic_slice_in_dim(values, first * width, width, last)
    upper = lax.dynamic_slice_in_dim(values, (first + 2) % 4 * width, width, last)
    return jnp.stack([lower, upper], 0)


def local(
    inputs,
    resets,
    in_mask,
    mid_mask,
    out_mask,
    w_ih_one,
    w_hh_one,
    bias_one,
    drop_one,
    w_ih_two,
    w_hh_two,
    bias_two,
    drop_two,
    cotangent,
):
    section_index = lax.axis_index("pipe")
    first_section = section_index < 2
    stream_half = section_index % 2
    hidden_size = w_hh_one.shape[0]
    streams = inputs.shape[1]
    length = inputs.shape[2]
    block = SPAN
    blocks = length // block
    rec_first_own = (
        w_hh_one.astype(jnp.float32) * drop_one.astype(jnp.float32) * weight_scale
    ).astype(jnp.bfloat16)
    rec_second_own = (
        w_hh_two.astype(jnp.float32) * drop_two.astype(jnp.float32) * weight_scale
    ).astype(jnp.bfloat16)
    in_first, rec_first, in_second, rec_second, bias_first, bias_second = (
        lax.all_gather(w_ih_one, "pipe", axis=1, tiled=True),
        lax.all_gather(rec_first_own, "pipe", axis=1, tiled=True),
        lax.all_gather(w_ih_two, "pipe", axis=1, tiled=True),
        lax.all_gather(rec_second_own, "pipe", axis=1, tiled=True),
        lax.all_gather(bias_one, "pipe", axis=0, tiled=True),
        lax.all_gather(bias_two, "pipe", axis=0, tiled=True),
    )
    w_recur = jnp.where(first_section, rec_first, rec_second)
    in_width = in_first.shape[0]
    gates_width = in_first.shape[1]

    def mine(array):
        return lax.dynamic_index_in_dim(array, stream_half, 0, keepdims=False)

    keep_in = mine(in_mask).astype(jnp.float32) * keep_scale
    keep_layer = (
        jnp.where(first_section, mine(mid_mask), mine(out_mask)).astype(jnp.float32) * keep_scale
    )
    first_input = (mine(inputs) * keep_in[:, None, :]).astype(jnp.bfloat16)
    cot_mine = mine(cotangent)
    positions = jnp.arange(length, dtype=jnp.int32)
    keep_all = mine(resets)[:, None] != positions[None, :]

    def project(layer_input, w_input, bias):
        return jnp.einsum(
            "sci,ig->csg", layer_input, w_input, preferred_element_type=jnp.float32
        ) + bias.astype(jnp.float32)

    def fwd_first(operands):
        first_block, received, keep_mask, hidden, cell_state = operands
        return recurrence(
            project(first_block, in_first, bias_first), keep_mask, w_recur, hidden, cell_state
        )

    def fwd_second(operands):
        first_block, received, keep_mask, hidden, cell_state = operands
        return recurrence(
            project(received, in_second, bias_second), keep_mask, w_recur, hidden, cell_state
        )

    def fwd_spare(operands):
        first_block, received, keep_mask, hidden, cell_state = operands
        return (
            jnp.zeros((block, streams, hidden_size), jnp.bfloat16),
            jnp.zeros((block, streams, gates_width), jnp.float32),
            jnp.zeros((block, streams, hidden_size), jnp.float32),
            hidden,
            cell_state,
        )

    hidden = jnp.zeros((streams, hidden_size), jnp.bfloat16)
    cell_state = jnp.zeros((streams, hidden_size), jnp.float32)
    received = jnp.zeros((streams, block, hidden_size), jnp.bfloat16)
    saved = []
    sent_blocks = []
    for tick_no in range(blocks + 1):
        branch = jnp.where(first_section, 1 if tick_no < blocks else 0, 2 if tick_no >= 1 else 0)
        begin = min(tick_no, blocks - 1) * block
        first_block = first_input[:, begin : begin + block]
        start = jnp.clip(tick_no - jnp.where(first_section, 0, 1), 0, blocks - 1) * block
        keep_mask = jnp.swapaxes(lax.dynamic_slice_in_dim(keep_all, start, block, 1), 0, 1)
        hiddens, gate_values, cells, hidden_next, cell_next = lax.switch(
            branch,
            [fwd_spare, fwd_first, fwd_second],
            (first_block, received, keep_mask, hidden, cell_state),
        )
        saved.append(
            (first_block, received, keep_mask, hidden, cell_state, hiddens, gate_values, cells)
        )
        hidden, cell_state = (hidden_next, cell_next)
        layer_block = (
            jnp.swapaxes(hiddens, 0, 1).astype(jnp.float32) * keep_layer[:, None, :]
        ).astype(jnp.bfloat16)
        sent_blocks.append(layer_block)
        if tick_no < blocks:
            received = send_down(layer_block)
    layer_outputs = jnp.where(
        first_section, jnp.concatenate(sent_blocks[:blocks], 1), jnp.concatenate(sent_blocks[1:], 1)
    )[None]

    def back_layer(layer_input, w_input, operands):
        (
            first_block,
            received,
            keep_mask,
            hidden_in,
            cell_in,
            hiddens,
            gate_values,
            cells,
            upstream,
            grad_hidden,
            grad_cell,
        ) = operands
        keep_cube = keep_mask[:, :, None]
        hidden_prev = jnp.where(
            keep_cube,
            jnp.concatenate([hidden_in[None], hiddens[:-1]], 0),
            jnp.zeros((), jnp.bfloat16),
        )
        cell_prev = jnp.where(keep_cube, jnp.concatenate([cell_in[None], cells[:-1]], 0), 0.0)
        gate_grads, carry = back_steps(
            gate_values, cells, cell_prev, keep_mask, upstream, w_recur, grad_hidden, grad_cell
        )
        grad_rec = jnp.einsum(
            "csh,csg->hg", hidden_prev, gate_grads, preferred_element_type=jnp.float32
        )
        grad_in = jnp.einsum(
            "sci,csg->ig", layer_input, gate_grads, preferred_element_type=jnp.float32
        )
        grad_bias = jnp.sum(gate_grads.astype(jnp.float32), axis=(0, 1))
        input_grad = jnp.einsum(
            "csg,ig->sci", gate_grads, w_input, preferred_element_type=jnp.float32
        )
        return (grad_in, grad_rec, grad_bias, input_grad, carry[0], carry[1])

    zero_in_first = jnp.zeros((in_width, gates_width), jnp.float32)
    zero_square = jnp.zeros((hidden_size, gates_width), jnp.float32)
    zero_bias = jnp.zeros((gates_width,), jnp.float32)
    zero_first_grad = jnp.zeros((streams, block, in_width), jnp.float32)
    zero_second_grad = jnp.zeros((streams, block, hidden_size), jnp.float32)

    def back_first(operands):
        grad_in, grad_rec, grad_bias, input_grad, hidden_back, cell_back = back_layer(
            operands[0], in_first, operands
        )
        return (
            grad_in,
            grad_rec,
            grad_bias,
            zero_square,
            input_grad,
            zero_second_grad,
            hidden_back,
            cell_back,
        )

    def back_second(operands):
        grad_in, grad_rec, grad_bias, input_grad, hidden_back, cell_back = back_layer(
            operands[1], in_second, operands
        )
        return (
            zero_in_first,
            grad_rec,
            grad_bias,
            grad_in,
            zero_first_grad,
            input_grad,
            hidden_back,
            cell_back,
        )

    def back_spare(operands):
        return (
            zero_in_first,
            zero_square,
            zero_bias,
            zero_square,
            zero_first_grad,
            zero_second_grad,
            operands[9],
            operands[10],
        )

    grad_hidden = jnp.zeros((streams, hidden_size), jnp.float32)
    grad_cell = jnp.zeros((streams, hidden_size), jnp.float32)
    received_grad = jnp.zeros((streams, block, hidden_size), jnp.bfloat16)
    totals = (zero_in_first, zero_square, zero_bias, zero_square)
    input_parts = [None] * blocks
    for turn in range(blocks + 1):
        slot = blocks - turn
        first_block, received, keep_mask, hidden_in, cell_in, hiddens, gate_values, cells = saved[
            slot
        ]
        cot_start = max(slot - 1, 0) * block
        cot_block = cot_mine[:, cot_start : cot_start + block]
        upstream = (
            jnp.where(first_section, received_grad, cot_block).astype(jnp.float32)
            * keep_layer[:, None, :]
        )
        upstream = jnp.swapaxes(upstream, 0, 1)
        branch = jnp.where(first_section, 1 if slot < blocks else 0, 2 if slot >= 1 else 0)
        results = lax.switch(
            branch,
            [back_spare, back_first, back_second],
            (
                first_block,
                received,
                keep_mask,
                hidden_in,
                cell_in,
                hiddens,
                gate_values,
                cells,
                upstream,
                grad_hidden,
                grad_cell,
            ),
        )
        grad_in1, grad_rec, grad_bias, grad_in2, first_grad, second_grad, grad_hidden, grad_cell = (
            results
        )
        totals = (
            totals[0] + grad_in1,
            totals[1] + grad_rec,
            totals[2] + grad_bias,
            totals[3] + grad_in2,
        )
        if slot < blocks:
            input_parts[slot] = first_grad * keep_in[:, None, :]
        if turn < blocks:
            received_grad = send_up(second_grad.astype(jnp.bfloat16))
    quarter_width = gates_width // 4
    partner = section_index + 1 - 2 * stream_half
    own_in = jnp.where(
        first_section, jnp.pad(totals[0], ((0, hidden_size - in_width), (0, 0))), totals[3]
    )
    own_rec = totals[1]
    own_bias = totals[2]
    got_in, got_rec, got_bias = partner_2(
        (
            two_quarters(own_in, partner, quarter_width),
            two_quarters(own_rec, partner, quarter_width),
            two_quarters(own_bias, partner, quarter_width),
        ),
        "pipe",
        0,
    )
    kept_in = two_quarters(own_in, section_index, quarter_width) + got_in
    kept_rec = two_quarters(own_rec, section_index, quarter_width) + got_rec
    kept_bias = two_quarters(own_bias, section_index, quarter_width) + got_bias
    cross_in, cross_rec, cross_bias = passed_along(
        (kept_in[1], kept_rec[1], kept_bias[1]), "pipe", 2
    )
    quarters = (
        jnp.where(first_section, kept_in[0][:in_width], cross_in[:in_width]),
        jnp.where(first_section, kept_rec[0], cross_rec),
        jnp.where(first_section, kept_bias[0], cross_bias),
        jnp.where(first_section, cross_in, kept_in[0]),
        jnp.where(first_section, cross_rec, kept_rec[0]),
        jnp.where(first_section, cross_bias, kept_bias[0]),
    )
    part_a, part_b, part_c, part_d, part_e, part_f = quarters
    summed = lax.psum((part_a, part_b, part_c, part_d, part_e, part_f), "dp")
    grad_w_ih_one = summed[0]
    grad_w_hh_one = summed[1] * drop_one.astype(jnp.float32) * weight_scale
    grad_bias_one = summed[2]
    grad_w_ih_two = summed[3]
    grad_w_hh_two = summed[4] * drop_two.astype(jnp.float32) * weight_scale
    grad_bias_two = summed[5]
    input_full = jnp.concatenate(input_parts, 1)
    halves = (jnp.arange(2) == stream_half).astype(jnp.float32)
    input_term = halves[:, None, None, None] * input_full[None]
    grad_input = lax.psum_scatter(input_term, "pipe", scatter_dimension=3, tiled=True)
    return (
        layer_outputs,
        grad_input,
        grad_w_ih_one,
        grad_w_hh_one,
        grad_bias_one,
        grad_w_ih_two,
        grad_w_hh_two,
        grad_bias_two,
    )


def solution(mesh):
    placed = (
        P(None, "dp", None, None),
        P(None, "dp"),
        P(None, "dp", None),
        P(None, "dp", None),
        P(None, "dp", None),
        P(None, "pipe"),
        P(None, "pipe"),
        P("pipe"),
        P(None, "pipe"),
        P(None, "pipe"),
        P(None, "pipe"),
        P("pipe"),
        P(None, "pipe"),
        P(None, "dp", None, None),
    )
    return jax.shard_map(
        local,
        mesh=mesh,
        in_specs=placed,
        out_specs=(
            P("pipe", "dp", None, None),
            P(None, "dp", None, "pipe"),
            P(None, "pipe"),
            P(None, "pipe"),
            P("pipe"),
            P(None, "pipe"),
            P(None, "pipe"),
            P("pipe"),
        ),
        check_vma=False,
    )
```

profile of v0, /device:TPU:32, one launch (start us, length us, event | category | flops | bytes accessed | tf_op | source)
XLA Modules:
  0.0 3185.1 jit_solution(5531819365426400696)
XLA Ops:
  47.7 10.8 all-reduce.10
  73.4 81.6 %all-gather.11.cloned.1.call-done = bf16[4,1150,1150]{2,1,0:T(8,128)(2,1)} async-done(((bf16[1,1150,1150]{2,1,0:T(8,128)(2,1)}), bf16[4,1150,1150]{2,1,0:T(8,128)(2,1)}) %all-gather.11.cloned.1.call-update) | async-done | bytes 10580016 | tf_op jit(solution)/shard_map/all_gather | solution.py:144
  155.1 102.6 %all-gather.13.cloned.1.call-done = bf16[4,1150,1150]{2,1,0:T(8,128)(2,1)} async-done(((bf16[1,1150,1150]{2,1,0:T(8,128)(2,1)}), bf16[4,1150,1150]{2,1,0:T(8,128)(2,1)}) %all-gather.13.cloned.1.call-update) | async-done | bytes 10580016 | tf_op jit(solution)/shard_map/all_gather | solution.py:146
  257.6 10.3 broadcast_select_fusion.56
  268.0 15.6 reshape.2728
  283.5 76.5 %all-gather.15.cloned.1.call-done = bf16[4,1150,1150]{2,1,0:T(8,128)(2,1)} async-done(((bf16[1,1150,1150]{2,1,0:T(8,128)(2,1)}), bf16[4,1150,1150]{2,1,0:T(8,128)(2,1)}) %all-gather.15.cloned.1.call-update) | async-done | bytes 10580016 | tf_op jit(solution)/shard_map/all_gather | solution.py:145
  360.0 14.7 reshape.2722
  374.7 11.4 conditional.6
  389.3 196.7 %collective-permute-done = bf16[2,44,1150]{2,1,0:T(8,128)(2,1)S(1)} collective-permute-done((bf16[2,44,1150]{2,1,0:T(8,128)(2,1)S(1)}, bf16[2,44,1150]{2,1,0:T(8,128)(2,1)S(1)}, u32[]{:S(2)}, u32[]{:S(2)}) %collective-permute-start) | collective-permute-done | bytes 202432 | tf_op jit(solution)/shard_map/ppermute | solution.py:16
  586.7 203.5 %conditional.7 = (bf16[44,2,1150]{2,1,0:T(2,128)(2,1)}, f32[44,2,4600]{2,1,0:T(2,128)}, f32[44,2,1150]{2,1,0:T(2,128)}, bf16[2,1150]{1,0:T(2,128)(2,1)}, f32[2,1150]{1,0:T(2,128)}, /*index=5*/f32[44,2,1150]{2,0,1:T(8,128)S(1)}) conditional(s32[]{:T(128)} %clamp.13, (bf16[2,1150]{1,0:T(2,128)(2,1)}, ...), branch_computations={%region_7.8_spmd, %region_8.11_spmd, %region_11.14_spmd} | conditional | flops 1016484992 | bytes 123078768 | solution.py:204
  598.4 15.3 copy.325
  613.7 175.3 %while.209 = (s32[]{:T(128)}, bf16[2,1150]{1,0:T(2,128)(2,1)}, f32[2,1150]{1,0:T(2,128)}, bf16[11,4,2,1150]{3,2,1,0:T(2,128)(2,1)}, f32[11,4,2,4600]{3,2,1,0:T(2...) while((s32[]{:T(128)}, bf16[2,1150]{1,0:T(2,128)(2,1)}, ...), condition=%wide.region_13.13_spmd, body=%wide.region_12.12_spmd.sunk | while | flops 85035600 | bytes 85597448 | solution.py:54
  801.8 180.8 %conditional.8 = (bf16[44,2,1150]{2,1,0:T(2,128)(2,1)}, f32[44,2,4600]{2,1,0:T(2,128)}, f32[44,2,1150]{2,1,0:T(2,128)}, f32[44,2,1150]{2,0,1:T(8,128)S(1)}) conditional(s32[]{:T(128)} %clamp.14, () %tuple.230, (bf16[400,4600]{1,0:T(8,128)(2,1)}, bf16[2,44,400]{2,1,0:T(8,128)(2,1)S(1)}, bf16[4600]{0:T(1024)(128)(2,1)}, ...), branch_computations={%region_14.15_spmd, %region_15.18_spmd, %region_18.21_spmd} | conditional | flops 1016484992 | bytes 123078736 | solution.py:204
  812.4 15.3 copy.328
  827.7 153.4 %while.211 = (s32[]{:T(128)}, bf16[2,1150]{1,0:T(2,128)(2,1)S(1)}, f32[2,1150]{1,0:T(2,128)S(1)}, bf16[11,4,2,1150]{3,2,1,0:T(2,128)(2,1)}, f32[11,4,2,4600]{3,2...) while((s32[]{:T(128)}, bf16[2,1150]{1,0:T(2,128)(2,1)S(1)}, ...), condition=%wide.region_20.20_spmd, body=%wide.region_19.19_spmd.sunk | while | flops 85035600 | bytes 85597432 | solution.py:54
  983.3 420.6 %conditional.9 = (f32[400,4600]{1,0:T(8,128)S(1)}, f32[1150,4600]{0,1:T(8,128)}, f32[4600]{0:T(1024)S(1)}, bf16[2,44,1150]{2,1,0:T(8,128)(2,1)S(1)}, f32[2,1150]...) conditional(s32[]{:T(128)} %clamp.14, () %tuple.234, (f32[44,2,4600]{2,1,0:T(2,128)}, ...), branch_computations={%region_21.22_spmd, %region_22.26_spmd, %region_26.30_spmd} | conditional | flops 2879970304 | bytes 218133440 | solution.py:325
  1002.1 15.3 copy.334
  1017.8 339.8 %while.219 = (s32[]{:T(128)}, f32[2,1150]{1,0:T(2,128)S(1)}, f32[2,1150]{1,0:T(2,128)S(1)}, bf16[11,4,2,4600]{3,2,1,0:T(2,128)(2,1)S(1)}, pred[11,4,2]{2,1,0:T(4...) while((s32[]{:T(128)}, f32[2,1150]{1,0:T(2,128)S(1)}, ...), condition=%wide.region_28.28_spmd.clone, body=%wide.region_27.27_spmd.clone.sunk | while | flops 85336912 | bytes 43691392 | solution.py:87
  1359.3 10.0 convolution_bitcast_fusion.11
  1371.9 8.7 convolution_bitcast_fusion.10
  1380.5 22.1 copy.375
  1410.5 420.9 %conditional.10 = (f32[400,4600]{1,0:T(8,128)}, f32[1150,4600]{0,1:T(8,128)}, f32[4600]{0:T(1024)S(1)}, f32[1150,4600]{1,0:T(8,128)}, f32[2,44,400]{2,1,0:T(8,12...) conditional(s32[]{:T(128)} %clamp.13, (f32[2,1150]{1,0:T(2,128)}, ...), branch_computations={%region_30.31_spmd, %region_31.35_spmd, %region_35.39_spmd} | conditional | flops 2879965696 | bytes 175218240 | solution.py:325
  1424.7 15.3 copy.339
  1440.5 339.0 %while.213 = (s32[]{:T(128)}, f32[2,1150]{1,0:T(2,128)S(1)}, f32[2,1150]{1,0:T(2,128)S(1)}, bf16[11,4,2,4600]{3,2,1,0:T(2,128)(2,1)S(1)}, pred[11,4,2]{2,1,0:T(4...) while((s32[]{:T(128)}, f32[2,1150]{1,0:T(2,128)S(1)}, ...), condition=%wide.region_37.37_spmd, body=%wide.region_36.36_spmd.sunk | while | flops 85332304 | bytes 43691380 | solution.py:87
  1781.1 8.7 convolution_bitcast_fusion.3
  1790.5 8.7 convolution_bitcast_fusion.2
  1799.2 22.1 copy.286
  1838.0 27.8 conditional.11
  1838.9 8.5 broadcast_in_dim.1454
  1847.4 9.8 broadcast_in_dim.1454.clone
  1865.8 30.7 add_add_fusion
  1896.6 15.2 dynamic-slice_bitcast_fusion.99
  1911.7 12.8 copy.361
  1924.6 12.7 copy.360
  1937.3 12.2 pad_maximum_fusion.5
  1949.5 12.4 add_add_fusion.1
  1961.9 30.5 add_select_fusion
  1992.4 13.0 constant_dynamic-slice_fusion.15
  2019.5 11.0 pad_maximum_fusion.4
  2045.0 19.0 copy.353
  2078.4 362.6 %collective-permute-start.7 = (f32[1150,1150]{0,1:T(8,128)}, f32[1150,1150]{0,1:T(8,128)}, u32[]{:S(2)}, u32[]{:S(2)}) collective-permute-start(f32[1150,1150]{0,1:T(8,128)} %slice_bitcast_fusion.49), channel_id=1, source_target_pairs={{0,64},{32,96},{64,0},{96,32},{1,65},{33,97},{65,1},{97,33},{2,66}... | collective-permute-start | bytes 15870008 | tf_op jit(solution)/shard_map/ppermute | solution.py:28
  2441.1 18.9 copy.350
  2475.6 92.6 %collective-permute-done.7 = f32[1150,1150]{0,1:T(8,128)} collective-permute-done((f32[1150,1150]{0,1:T(8,128)}, f32[1150,1150]{0,1:T(8,128)}, u32[]{:S(2)}, u32[]{:S(2)}) %collective-permute-start.7) | collective-permute-done | bytes 5290032 | tf_op jit(solution)/shard_map/ppermute | solution.py:28
  2568.2 8.7 fusion.729
  2576.9 104.5 %collective-permute-done.5 = f32[1150,1150]{0,1:T(8,128)} collective-permute-done((f32[1150,1150]{0,1:T(8,128)}, f32[1150,1150]{0,1:T(8,128)}, u32[]{:S(2)}, u32[]{:S(2)}) %collective-permute-start.5) | collective-permute-done | bytes 5290032 | tf_op jit(solution)/shard_map/ppermute | solution.py:28
  2698.5 184.0 %all-reduce.8 = (f32[1150]{0:T(1024)}, f32[1150]{0:T(1024)}) all-reduce(f32[1150]{0:T(1024)S(1)} %get-tuple-element.3447, f32[1150]{0:T(1024)S(1)} %get-tuple-element.3446), channel_id=1, replica_groups=mesh['pipe'=4,'dp'=32] {'dp'}, use_global_device_ids=true, to_apply=%region_51.52 | all-reduce | flops 2300 | bytes 18400 | tf_op jit(solution)/shard_map/psum | solution.py:386
  2884.3 257.9 %all-reduce.16.cloned.1.call-done = (f32[400,1150]{0,1:T(8,128)}, f32[1150,1150]{0,1:T(8,128)}, f32[1150,1150]{0,1:T(8,128)}, f32[1150,1150]{0,1:T(8,128)}) async-done(((f32[400,1150]{0,1:T(8,128)}, f32[1150,1150]{0,1:T(8,128)}, f32[1150,1150]{0,1:T(8,128)}, f32[1150,1150]{0,1:T(8,128)}), (f32[400,1150]{0,1:T(8,128)}, f32[1150,1150]{0,1:T(8,128)}, f32[1150,1150]{0,1:T(8,128)}, ...) | async-done | bytes 17710016 | tf_op jit(solution)/shard_map/psum | solution.py:386
  3145.2 11.9 multiply_multiply_fusion
  (1055 shorter events, 1240.8 us)
Async XLA Ops:
  7.2 380.9 %copy-start = (bf16[2,2,88,1150]{3,2,1,0:T(8,128)(2,1)S(1)}, bf16[2,2,88,1150]{3,2,1,0:T(8,128)(2,1)}, u32[]{:S(2)}) copy-start(bf16[2,2,88,1150]{3,2,1,0:T(8,128)(2,1)} %param.69) | copy-start | bytes 2428804
  7.2 53.4 %all-gather.9.cloned.1.call-start = ((), (), s32[]{:S(2)}) async-start(), calls=%async_computation | async-start | bytes 4608000 | tf_op jit(solution)/shard_map/all_gather | solution.py:143
  7.9 147.1 %all-gather.11.cloned.1.call-start = ((), (), s32[]{:S(2)}) async-start(), calls=%async_computation.1 | async-start | bytes 13271040 | tf_op jit(solution)/shard_map/all_gather | solution.py:144
  24.2 233.4 %all-gather.13.cloned.1.call-start = ((), (), s32[]{:S(2)}) async-start(), calls=%async_computation.2 | async-start | bytes 13271040 | tf_op jit(solution)/shard_map/all_gather | solution.py:146
  35.3 11.9 copy-start.71
  35.3 12.1 copy-start.72
  35.3 23.2 copy-start.75
  35.3 24.0 copy-start.74
  35.3 24.0 copy-start.69
  35.3 24.0 copy-start.70
  40.3 19.6 copy-start.54
  40.3 319.7 %all-gather.15.cloned.1.call-start = ((), (), s32[]{:S(2)}) async-start(), calls=%async_computation.3 | async-start | bytes 13271040 | tf_op jit(solution)/shard_map/all_gather | solution.py:145
  45.7 2836.8 %all-reduce.14.cloned.1.call-start = ((), (), s32[]{:S(2)}) async-start(), calls=%async_computation.4 | async-start | bytes 1441792
  58.5 316.2 %copy-start.55 = (bf16[4600]{0:T(1024)(128)(2,1)}, bf16[4600]{0:T(1024)(128)(2,1)S(1)}, u32[]{:S(2)}) copy-start(bf16[4600]{0:T(1024)(128)(2,1)S(1)} %get-tuple-element.3178) | copy-start | bytes 27604
  59.3 315.4 %copy-start.56 = (pred[44,2]{0,1:T(4,128)(4,1)}, pred[44,2]{0,1:T(4,128)(4,1)S(1)}, u32[]{:S(2)}) copy-start(pred[44,2]{0,1:T(4,128)(4,1)S(1)} %get-tuple-element.3454) | copy-start | bytes 268
  59.3 208.7 %copy-start.67 = (f32[2,400]{1,0:T(2,128)}, f32[2,400]{1,0:T(2,128)S(1)}, u32[]{:S(2)}) copy-start(f32[2,400]{1,0:T(2,128)S(1)} %fusion.741) | copy-start | bytes 9604
  60.6 314.1 %copy-start.37 = (bf16[2,44,400]{2,1,0:T(8,128)(2,1)}, bf16[2,44,400]{2,1,0:T(8,128)(2,1)S(1)}, u32[]{:S(2)}) copy-start(bf16[2,44,400]{2,1,0:T(8,128)(2,1)S(1)} %get-tuple-element.3441) | copy-start | bytes 211204
  374.7 211.3 %copy-start.34 = (bf16[2,44,400]{2,1,0:T(8,128)(2,1)S(1)}, bf16[2,44,400]{2,1,0:T(8,128)(2,1)}, u32[]{:S(2)}) copy-start(bf16[2,44,400]{2,1,0:T(8,128)(2,1)} %get-tuple-element.3440) | copy-start | bytes 211204
  374.7 211.3 %copy-start.64 = (pred[44,2]{0,1:T(4,128)(4,1)S(1)}, pred[44,2]{0,1:T(4,128)(4,1)}, u32[]{:S(2)}) copy-start(pred[44,2]{0,1:T(4,128)(4,1)} %get-tuple-element.3453) | copy-start | bytes 268
  386.8 199.2 %collective-permute-start = (bf16[2,44,1150]{2,1,0:T(8,128)(2,1)S(1)}, bf16[2,44,1150]{2,1,0:T(8,128)(2,1)S(1)}, u32[]{:S(2)}, u32[]{:S(2)}) collective-permute-start(bf16[2,44,1150]{2,1,0:T(8,128)(2,1)S(1)} %get-tuple-element.3439), channel_id=1, source_target_pairs={{0,64},{32,96},{1,65},{33,97},{2,66},{34,98},{3,67},{35,99},{4,68}... | collective-permute-start | bytes 607208 | tf_op jit(solution)/shard_map/ppermute | solution.py:16
  586.0 204.2 %copy-start.46 = (f32[2,1150]{1,0:T(2,128)S(1)}, f32[2,1150]{1,0:T(2,128)}, u32[]{:S(2)}) copy-start(f32[2,1150]{1,0:T(2,128)} %multiply_bitcast_fusion.3) | copy-start | bytes 27604
  586.0 206.2 %copy-start.31 = (bf16[1,2,88,1150]{3,1,2,0:T(2,128)(2,1)S(1)}, bf16[1,2,88,1150]{3,1,2,0:T(2,128)(2,1)}, u32[]{:S(2)}) copy-start(bf16[1,2,88,1150]{3,1,2,0:T(2,128)(2,1)} %copy.414) | copy-start | bytes 1214404
  586.0 215.1 %copy-start.66 = (pred[44,2]{0,1:T(4,128)(4,1)S(1)}, pred[44,2]{0,1:T(4,128)(4,1)}, u32[]{:S(2)}) copy-start(pred[44,2]{0,1:T(4,128)(4,1)} %get-tuple-element.3452) | copy-start | bytes 268
  790.9 10.2 collective-permute-start.1
  982.6 427.7 %copy-start.32 = (bf16[1,2,88,1150]{3,1,2,0:T(2,128)(2,1)S(1)}, bf16[1,2,88,1150]{3,1,2,0:T(2,128)(2,1)}, u32[]{:S(2)}) copy-start(bf16[1,2,88,1150]{3,1,2,0:T(2,128)(2,1)} %copy.414) | copy-start | bytes 1214404
  982.6 427.7 %copy-start.47 = (f32[2,1150]{1,0:T(2,128)S(1)}, f32[2,1150]{1,0:T(2,128)}, u32[]{:S(2)}) copy-start(f32[2,1150]{1,0:T(2,128)} %multiply_bitcast_fusion.3) | copy-start | bytes 27604
  982.6 427.9 %copy-start.51 = (bf16[2,44,1150]{2,1,0:T(8,128)(2,1)S(1)}, bf16[2,44,1150]{2,1,0:T(8,128)(2,1)}, u32[]{:S(2)}) copy-start(bf16[2,44,1150]{2,1,0:T(8,128)(2,1)} %copy-done.50) | copy-start | bytes 607204
  982.6 427.9 %copy-start.65 = (pred[44,2]{0,1:T(4,128)(4,1)S(1)}, pred[44,2]{0,1:T(4,128)(4,1)}, u32[]{:S(2)}) copy-start(pred[44,2]{0,1:T(4,128)(4,1)} %get-tuple-element.3453) | copy-start | bytes 268
  1357.6 11.7 copy-start.16
  1404.1 6.1 collective-permute-start.2
  1410.5 427.3 %copy-start.33 = (bf16[1,2,88,1150]{3,1,2,0:T(2,128)(2,1)S(1)}, bf16[1,2,88,1150]{3,1,2,0:T(2,128)(2,1)}, u32[]{:S(2)}) copy-start(bf16[1,2,88,1150]{3,1,2,0:T(2,128)(2,1)} %copy.414) | copy-start | bytes 1214404
  1410.5 427.2 %copy-start.48 = (f32[2,1150]{1,0:T(2,128)S(1)}, f32[2,1150]{1,0:T(2,128)}, u32[]{:S(2)}) copy-start(f32[2,1150]{1,0:T(2,128)} %multiply_bitcast_fusion.3) | copy-start | bytes 27604
  1410.5 427.5 %copy-start.38 = (bf16[2,44,400]{2,1,0:T(8,128)(2,1)S(1)}, bf16[2,44,400]{2,1,0:T(8,128)(2,1)}, u32[]{:S(2)}) copy-start(bf16[2,44,400]{2,1,0:T(8,128)(2,1)} %copy-done.37) | copy-start | bytes 211204
  1410.5 427.5 %copy-start.57 = (pred[44,2]{0,1:T(4,128)(4,1)S(1)}, pred[44,2]{0,1:T(4,128)(4,1)}, u32[]{:S(2)}) copy-start(pred[44,2]{0,1:T(4,128)(4,1)} %copy-done.56) | copy-start | bytes 268
  1424.7 15.7 copy-start.18
  1424.7 15.7 copy-start.26
  1831.6 6.1 collective-permute-start.3
  1865.8 30.8 copy-start.14
  1865.8 30.7 copy-start.43
  1865.8 30.7 copy-start.62
  1949.5 95.5 %collective-permute-start.6 = (f32[2,1150,1150]{2,0,1:T(2,128)}, f32[2,1150,1150]{2,0,1:T(2,128)}, u32[]{:S(2)}, u32[]{:S(2)}) collective-permute-start(f32[2,1150,1150]{2,0,1:T(2,128)} %pad_maximum_fusion.5), channel_id=1, source_target_pairs={{0,32},{32,0},{64,96},{96,64},{1,33},{33,1},{65,97},{97,65},{2,34}... | collective-permute-start | bytes 31740008 | tf_op jit(solution)/shard_map/ppermute | solution.py:22
  2030.5 410.5 %collective-permute-start.4 = (f32[2,1150,1150]{2,0,1:T(2,128)}, f32[2,1150,1150]{2,0,1:T(2,128)}, u32[]{:S(2)}, u32[]{:S(2)}) collective-permute-start(f32[2,1150,1150]{2,0,1:T(2,128)} %pad_maximum_fusion.4), channel_id=1, source_target_pairs={{0,32},{32,0},{64,96},{96,64},{1,33},{33,1},{65,97},{97,65},{2,34}... | collective-permute-start | bytes 31740008 | tf_op jit(solution)/shard_map/ppermute | solution.py:22
  2078.4 489.8 %collective-permute-start.7 = (f32[1150,1150]{0,1:T(8,128)}, f32[1150,1150]{0,1:T(8,128)}, u32[]{:S(2)}, u32[]{:S(2)}) collective-permute-start(f32[1150,1150]{0,1:T(8,128)} %slice_bitcast_fusion.49), channel_id=1, source_target_pairs={{0,64},{32,96},{64,0},{96,32},{1,65},{33,97},{65,1},{97,33},{2,66}... | collective-permute-start | bytes 15870008 | tf_op jit(solution)/shard_map/ppermute | solution.py:28
  2474.4 207.0 %collective-permute-start.5 = (f32[1150,1150]{0,1:T(8,128)}, f32[1150,1150]{0,1:T(8,128)}, u32[]{:S(2)}, u32[]{:S(2)}) collective-permute-start(f32[1150,1150]{0,1:T(8,128)} %slice_bitcast_fusion.51), channel_id=1, source_target_pairs={{0,64},{32,96},{64,0},{96,32},{1,65},{33,97},{65,1},{97,33},{2,66}... | collective-permute-start | bytes 15870008 | tf_op jit(solution)/shard_map/ppermute | solution.py:28
  2475.5 666.7 %all-reduce.16.cloned.1.call-start = ((), (), s32[]{:S(2)}) async-start(), calls=%async_computation.5 | async-start | bytes 36569088 | tf_op jit(solution)/shard_map/psum | solution.py:386
  2692.1 1.3 collective-permute-start.8
  2693.5 5.0 collective-permute-start.9
  3164.0 13.8 copy-start.1
  (48 other events, 283.4 us)
Sparse Core Ops, SparseCore 0:
  9.7 42.7 all-gather.8
  54.2 100.8 all-gather.10
  156.7 100.8 all-gather.12
  259.1 100.8 all-gather.14
  2475.6 48.4 all-reduce.13
  2691.3 450.8 all-reduce.15
where the time goes:
time: 3200 us; the launch traced here: 3190 us
  waiting for transfers between devices  933 us (29%)
  matrix products  889 us (28%)
  local copies, waits for them, and re-layouts  443 us (14%)
  starting transfers between devices  372 us (12%)
  other arithmetic  289 us (9%)
  blocking collectives  195 us (6%)
  loops' own time  48.3 us (2%)
    dot_general x88, matrix products, retreat(): lax.dot_general(gate_grad, w_recur, (((1,), (1,)), ((), ())), preferred_e...  605 us
    ppermute x3, starting transfers between devices, passed_along(): return lax.ppermute(value, axis, pairs)  366 us
    psum x1, waiting for transfers between devices, local(): summed = lax.psum((part_a, part_b, part_c, part_d, part_e, part_f), 'dp')  258 us
    dot_general x88, matrix products, advance(): jnp.dot(hidden_prev, w_recur, preferred_element_type=jnp.float32)  225 us
    ppermute x4, waiting for transfers between devices, shifted(): return lax.ppermute(block, axis, route)  214 us
    ppermute x3, waiting for transfers between devices, passed_along(): return lax.ppermute(value, axis, pairs)  198 us
    psum x1, blocking collectives, local(): summed = lax.psum((part_a, part_b, part_c, part_d, part_e, part_f), 'dp')  184 us
    all_gather x1, waiting for transfers between devices, local(): lax.all_gather(rec_second_own, 'pipe', axis=1, tiled=True)  103 us
  transfers between devices with their start and end apart: 16, of which 12 were waited for; matrix products, arithmetic and copies ran while one was open for 8% of the time, Pallas kernels for 0%

commit v1 on v0

v1 whole, which is shorter than its diff:
```python
import functools

import jax
import jax.numpy as jnp
from jax import lax
from jax.experimental import pallas as pl
from jax.experimental.pallas import tpu as pltpu
from jax.sharding import PartitionSpec as P

MESH = pl.DeviceIdType.MESH
HID = 1150
WIDE = 1152
D_IN = 400
D_WIDE = 416
STEPS = 88
ROWS = 4
CHUNKS = 44
GROUP = 4
HALF = WIDE // 2

keep_scale = 4.0 / 3.0
weight_scale = 2.0

LAYER_ONE, SOURCE_GRAD, LAYER_TWO, BETWEEN = 0, 1, 2, 3
W_ONE, R_ONE, R_TWO, W_TWO, R_ONE_T, R_TWO_T, W_TWO_T, W_ONE_T = range(8)
USER = {
    W_ONE: LAYER_ONE,
    R_ONE: LAYER_ONE,
    R_TWO: LAYER_TWO,
    W_TWO: BETWEEN,
    R_ONE_T: LAYER_ONE,
    R_TWO_T: LAYER_TWO,
    W_TWO_T: BETWEEN,
    W_ONE_T: SOURCE_GRAD,
}
FORWARD = (W_ONE, W_TWO, R_ONE, R_TWO)
BACKWARD = (R_TWO_T, W_TWO_T, R_ONE_T, W_ONE_T)


def sigmoid(value):
    return 0.5 * jnp.tanh(0.5 * value) + 0.5


def dot(left, right):
    return jnp.dot(left, right, preferred_element_type=jnp.float32)


def relay_kernel(
    w_one, r_one, r_two, w_two, r_one_t, r_two_t, w_two_t, w_one_t,
    source, keep, layer_keep, cotangent,
    o_u, o_hp_one, o_hp_two, o_out, o_dz_one, o_dz_two, o_dx,
    w_front, w_back, w_in, zx, extra, dz, du, dx, hidden, cell, stage_a, stage_b, stage_z,
    block_send, block_recv, block_local,
    u_send, u_recv, z_send, z_recv, dz_send, dz_recv, du_send, du_recv,
    bulk_send, bulk_recv, part_send, part_recv, dx_send, dx_recv, local_sem,
):
    pipe = lax.axis_index("pipe")
    dp = lax.axis_index("dp")
    dp_count = lax.axis_size("dp")
    dp_far = lax.rem(dp + dp_count // 2, dp_count)

    barrier = pltpu.get_barrier_semaphore()
    for step in range(1, 4):
        pl.semaphore_signal(
            barrier, inc=1, device_id={"pipe": lax.rem(pipe + step, 4), "dp": dp}, device_id_type=MESH
        )
    for step in range(4):
        pl.semaphore_signal(
            barrier, inc=1, device_id={"pipe": lax.rem(pipe + step, 4), "dp": dp_far}, device_id_type=MESH
        )
    pl.semaphore_wait(barrier, 7)

    blocks = {
        W_ONE: w_one, R_ONE: r_one, R_TWO: r_two, W_TWO: w_two,
        R_ONE_T: r_one_t, R_TWO_T: r_two_t, W_TWO_T: w_two_t, W_ONE_T: w_one_t,
    }

    def landing(kind, p):
        if kind == W_ONE:
            return w_in.at[p]
        if kind in (R_ONE, R_TWO, W_TWO):
            return w_front.at[p]
        if kind == W_ONE_T:
            return w_front.at[p, :, pl.ds(0, 512)]
        return w_back.at[p]

    def block_copies(kind, p):
        user = USER[kind]
        source_ref, target = blocks[kind], landing(kind, p)
        if p == user:
            return [pltpu.make_async_copy(source_ref, target, block_local.at[kind])]
        if p // 2 == user // 2:
            return [
                pltpu.make_async_remote_copy(
                    source_ref, target, block_send.at[kind, 0], block_recv.at[kind, p, 0],
                    device_id={"pipe": user, "dp": dp}, device_id_type=MESH,
                )
            ]
        rows = source_ref.shape[0] // 2
        return [
            pltpu.make_async_remote_copy(
                source_ref.at[pl.ds(part * rows, rows)], target.at[pl.ds(part * rows, rows)],
                block_send.at[kind, part], block_recv.at[kind, p, part],
                device_id={"pipe": user, "dp": (dp, dp_far)[part]}, device_id_type=MESH,
            )
            for part in range(2)
        ]

    def start_blocks(kinds, p):
        for kind in kinds:
            for copy in block_copies(kind, p):
                copy.start()

    def finish_blocks(kinds, p):
        for kind in kinds:
            if p != USER[kind]:
                for copy in block_copies(kind, p):
                    copy.wait_send()

    def await_blocks(kind):
        for p in range(4):
            for copy in block_copies(kind, p):
                if p == USER[kind]:
                    copy.wait()
                else:
                    copy.wait_recv()

    def to(pipe_to, source_ref, target, send, recv):
        return pltpu.make_async_remote_copy(
            source_ref, target, send, recv,
            device_id={"pipe": pipe_to, "dp": dp}, device_id_type=MESH,
        )

    def copy_u(c):
        return to(BETWEEN, o_u.at[c], o_u.at[c], u_send, u_recv.at[c])

    def copy_z(c):
        return to(LAYER_TWO, zx.at[c], zx.at[c], z_send, z_recv.at[c])

    def copy_dz(pipe_to, c):
        return to(pipe_to, dz.at[:, c], dz.at[:, c], dz_send, dz_recv.at[c])

    def copy_du(c):
        return to(LAYER_ONE, du.at[c], du.at[c], du_send, du_recv.at[c])

    def copy_part(pipe_to, output, group, slot, gate):
        span = pl.ds(group * GROUP, GROUP)
        return to(pipe_to, dz.at[gate, span], output.at[span], part_send.at[slot], part_recv.at[group])

    def copy_dx(pipe_to, group, slot):
        span = pl.ds(group * GROUP, GROUP)
        return to(
            pipe_to, dx.at[span, :, pl.ds(pipe_to * 128, 128)], o_dx.at[span], dx_send.at[slot], dx_recv.at[group]
        )

    def copy_bulk(pipe_to, ref, slot, which):
        return to(pipe_to, ref, ref, bulk_send.at[slot], bulk_recv.at[which])

    def keep_rows(c, j):
        return jnp.broadcast_to(keep[c, ROWS * j : ROWS * j + ROWS, 0:1], (ROWS, WIDE))

    def clear():
        hidden[...] = jnp.zeros_like(hidden)
        cell[...] = jnp.zeros_like(cell)

    def forward_pair(c, mask, with_one, o_hp, o_layer):
        column = lax.broadcasted_iota(jnp.int32, (ROWS, WIDE), 1)
        for j in range(2):
            rows = pl.ds(ROWS * j, ROWS)
            kept = keep_rows(c, j)
            hidden_prev = hidden[...] * kept
            cell_prev = cell[...] * kept
            left = hidden_prev.astype(jnp.bfloat16)
            gates = [
                dot(left, w_front[g]) + zx[c, rows, pl.ds(g * WIDE, WIDE)] for g in range(4)
            ]
            gate_in, gate_forget = sigmoid(gates[0]), sigmoid(gates[1])
            gate_cand, gate_out = jnp.tanh(gates[2]), sigmoid(gates[3])
            cell_now = gate_forget * cell_prev + gate_in * gate_cand
            cell_tanh = jnp.tanh(cell_now)
            hidden_now = (gate_out * cell_tanh).astype(jnp.bfloat16).astype(jnp.float32)
            cell[...] = cell_now
            hidden[...] = hidden_now
            stage_a[rows, :] = hidden_prev
            layer = hidden_now * mask
            if with_one:
                layer = jnp.where(column == HID, 1.0, layer)
            stage_b[rows, :] = layer
            zx[c, rows, pl.ds(0, WIDE)] = gate_cand * gate_in * (1.0 - gate_in)
            zx[c, rows, pl.ds(WIDE, WIDE)] = cell_prev * gate_forget * (1.0 - gate_forget)
            zx[c, rows, pl.ds(2 * WIDE, WIDE)] = gate_in * (1.0 - gate_cand * gate_cand)
            zx[c, rows, pl.ds(3 * WIDE, WIDE)] = cell_tanh * gate_out * (1.0 - gate_out)
            extra[c, rows, pl.ds(0, WIDE)] = gate_out * (1.0 - cell_tanh * cell_tanh)
            extra[c, rows, pl.ds(WIDE, WIDE)] = gate_forget * kept
        o_hp[c] = stage_a[...].astype(jnp.bfloat16)
        o_layer[c] = stage_b[...].astype(jnp.bfloat16)

    def backward_pair(c, mask, upstream):
        above = upstream[c].astype(jnp.float32)
        for j in (1, 0):
            rows = pl.ds(ROWS * j, ROWS)
            total = hidden[...] + above[ROWS * j : ROWS * j + ROWS] * mask
            out_grad = total * zx[c, rows, pl.ds(3 * WIDE, WIDE)]
            cell_total = cell[...] + total * extra[c, rows, pl.ds(0, WIDE)]
            cell[...] = cell_total * extra[c, rows, pl.ds(WIDE, WIDE)]
            grads = [cell_total * zx[c, rows, pl.ds(g * WIDE, WIDE)] for g in range(3)] + [out_grad]
            back = None
            for g in range(4):
                stage_z[rows, pl.ds(g * WIDE, WIDE)] = grads[g]
                part = dot(grads[g].astype(jnp.bfloat16), w_back[g])
                back = part if back is None else back + part
            hidden[...] = back * keep_rows(c, j)
        for g in range(4):
            dz[g, c] = stage_z[:, pl.ds(g * WIDE, WIDE)].astype(jnp.bfloat16)

    last = CHUNKS - 1
    groups = CHUNKS // GROUP

    @pl.when(pipe == LAYER_ONE)
    def _():
        me = LAYER_ONE
        start_blocks(FORWARD, me)
        await_blocks(W_ONE)
        for g in range(4):
            zx[:, :, pl.ds(g * WIDE, WIDE)] = dot(source[...], w_in[g]).reshape(CHUNKS, 2 * ROWS, WIDE)
        await_blocks(R_ONE)
        start_blocks(BACKWARD, me)
        clear()

        def ahead(c, carry):
            forward_pair(c, layer_keep[0], True, o_hp_one, o_u)
            copy_u(c).start()
            return carry

        lax.fori_loop(0, CHUNKS, ahead, 0)
        bulk = [
            copy_bulk(SOURCE_GRAD, o_u, 0, 0), copy_bulk(LAYER_TWO, o_u, 1, 0),
            copy_bulk(SOURCE_GRAD, o_hp_one, 2, 1), copy_bulk(LAYER_TWO, o_hp_one, 3, 1),
            copy_bulk(BETWEEN, o_hp_one, 4, 1),
        ]
        for copy in bulk:
            copy.start()
        await_blocks(R_ONE_T)
        clear()

        def behind(i, carry):
            c = last - i
            copy_du(c).wait_recv()
            backward_pair(c, layer_keep[0], du)
            copy_dz(SOURCE_GRAD, c).start()

            @pl.when(lax.rem(c, GROUP) == 0)
            def _():
                group = c // GROUP
                copy_part(LAYER_TWO, o_dz_one, group, 0, LAYER_TWO).start()
                copy_part(BETWEEN, o_dz_one, group, 1, BETWEEN).start()

            return carry

        lax.fori_loop(0, CHUNKS, behind, 0)
        own = pltpu.make_async_copy(dz.at[me], o_dz_one, local_sem.at[0])
        own.start()
        finish_blocks(FORWARD + BACKWARD, me)
        to(BETWEEN, o_u, o_u, u_send, u_recv.at[0]).wait_send()
        for copy in bulk:
            copy.wait_send()
        to(SOURCE_GRAD, dz, dz, dz_send, dz_recv.at[0]).wait_send()
        to(LAYER_TWO, dz.at[me], o_dz_one, part_send.at[0], part_recv.at[0]).wait_send()
        to(BETWEEN, dz.at[me], o_dz_one, part_send.at[1], part_recv.at[0]).wait_send()
        own.wait()

        copy_bulk(me, o_hp_two, 0, 2).wait_recv()
        for group in range(groups):
            copy_part(me, o_dz_two, group, 0, me).wait_recv()
            copy_dx(me, group, 0).wait_recv()

    @pl.when(pipe == LAYER_TWO)
    def _():
        me = LAYER_TWO
        start_blocks(FORWARD, me)
        await_blocks(R_TWO)
        start_blocks(BACKWARD, me)
        clear()

        def ahead(c, carry):
            copy_z(c).wait_recv()
            forward_pair(c, layer_keep[1], False, o_hp_two, o_out)
            return carry

        lax.fori_loop(0, CHUNKS, ahead, 0)
        bulk = [
            copy_bulk(LAYER_ONE, o_hp_two, 0, 2), copy_bulk(SOURCE_GRAD, o_hp_two, 1, 2),
            copy_bulk(BETWEEN, o_hp_two, 2, 2), copy_bulk(BETWEEN, o_out, 3, 3),
        ]
        for copy in bulk:
            copy.start()
        await_blocks(R_TWO_T)
        clear()

        def behind(i, carry):
            c = last - i
            backward_pair(c, layer_keep[1], cotangent)
            copy_dz(BETWEEN, c).start()

            @pl.when(lax.rem(c, GROUP) == 0)
            def _():
                group = c // GROUP
                copy_part(LAYER_ONE, o_dz_two, group, 0, LAYER_ONE).start()
                copy_part(SOURCE_GRAD, o_dz_two, group, 1, SOURCE_GRAD).start()

            return carry

        lax.fori_loop(0, CHUNKS, behind, 0)
        own = pltpu.make_async_copy(dz.at[me], o_dz_two, local_sem.at[0])
        own.start()
        finish_blocks(FORWARD + BACKWARD, me)
        for copy in bulk:
            copy.wait_send()
        to(BETWEEN, dz, dz, dz_send, dz_recv.at[0]).wait_send()
        to(LAYER_ONE, dz.at[me], o_dz_two, part_send.at[0], part_recv.at[0]).wait_send()
        to(SOURCE_GRAD, dz.at[me], o_dz_two, part_send.at[1], part_recv.at[0]).wait_send()
        own.wait()

        copy_bulk(me, o_u, 0, 0).wait_recv()
        copy_bulk(me, o_hp_one, 0, 1).wait_recv()
        for group in range(groups):
            copy_part(me, o_dz_one, group, 0, me).wait_recv()
            copy_dx(me, group, 0).wait_recv()

    @pl.when(pipe == BETWEEN)
    def _():
        me = BETWEEN
        start_blocks(FORWARD, me)
        await_blocks(W_TWO)
        start_blocks(BACKWARD, me)

        def ahead(c, carry):
            copy_u(c).wait_recv()
            for g in range(4):
                zx[c, :, pl.ds(g * WIDE, WIDE)] = dot(o_u[c], w_front[g])
            copy_z(c).start()
            return carry

        lax.fori_loop(0, CHUNKS, ahead, 0)
        await_blocks(W_TWO_T)

        def behind(i, carry):
            c = last - i
            copy_dz(me, c).wait_recv()
            back = None
            for g in range(4):
                part = dot(dz[g, c], w_back[g])
                back = part if back is None else back + part
            du[c] = back.astype(jnp.bfloat16)
            copy_du(c).start()
            return carry

        lax.fori_loop(0, CHUNKS, behind, 0)
        own = pltpu.make_async_copy(dz.at[me], o_dz_two, local_sem.at[0])
        own.start()
        finish_blocks(FORWARD + BACKWARD, me)
        to(LAYER_TWO, zx, zx, z_send, z_recv.at[0]).wait_send()
        to(LAYER_ONE, du, du, du_send, du_recv.at[0]).wait_send()
        own.wait()

        copy_bulk(me, o_hp_one, 0, 1).wait_recv()
        copy_bulk(me, o_hp_two, 0, 2).wait_recv()
        copy_bulk(me, o_out, 0, 3).wait_recv()
        for group in range(groups):
            copy_part(me, o_dz_one, group, 0, me).wait_recv()
            copy_dx(me, group, 0).wait_recv()

    @pl.when(pipe == SOURCE_GRAD)
    def _():
        me = SOURCE_GRAD
        start_blocks(FORWARD, me)
        finish_blocks(FORWARD, me)
        start_blocks(BACKWARD, me)
        await_blocks(W_ONE_T)

        def behind(i, carry):
            c = last - i
            copy_dz(me, c).wait_recv()
            back = None
            for g in range(4):
                part = dot(dz[g, c], w_front[g, :, :512])
                back = part if back is None else back + part
            dx[c] = back

            @pl.when(lax.rem(c, GROUP) == 0)
            def _():
                group = c // GROUP
                copy_dx(LAYER_ONE, group, 0).start()
                copy_dx(LAYER_TWO, group, 1).start()
                copy_dx(BETWEEN, group, 2).start()

            return carry

        lax.fori_loop(0, CHUNKS, behind, 0)
        own = pltpu.make_async_copy(dz.at[me], o_dz_one, local_sem.at[0])
        own.start()
        own_dx = pltpu.make_async_copy(dx.at[:, :, pl.ds(me * 128, 128)], o_dx, local_sem.at[1])
        own_dx.start()
        finish_blocks(BACKWARD, me)
        for slot, pipe_to in enumerate((LAYER_ONE, LAYER_TWO, BETWEEN)):
            to(pipe_to, o_dx, o_dx, dx_send.at[slot], dx_recv.at[0]).wait_send()
        own.wait()
        own_dx.wait()

        copy_bulk(me, o_u, 0, 0).wait_recv()
        copy_bulk(me, o_hp_one, 0, 1).wait_recv()
        copy_bulk(me, o_hp_two, 0, 2).wait_recv()
        for group in range(groups):
            copy_part(me, o_dz_two, group, 0, me).wait_recv()


def relay(blocks, source, keep, layer_keep, cotangent):
    whole = pl.BlockSpec(memory_space=pltpu.VMEM)
    rows = (CHUNKS, 2 * ROWS, WIDE)
    half, full = jnp.bfloat16, jnp.float32
    shapes = [jax.ShapeDtypeStruct(rows, half)] * 6 + [
        jax.ShapeDtypeStruct((CHUNKS, 2 * ROWS, 128), full)
    ]
    dma = pltpu.SemaphoreType.DMA
    return pl.pallas_call(
        relay_kernel,
        out_shape=shapes,
        in_specs=[pl.BlockSpec(memory_space=pl.ANY)] * 8 + [whole] * 4,
        out_specs=[whole] * 7,
        scratch_shapes=[
            pltpu.VMEM((4, WIDE, WIDE), half),
            pltpu.VMEM((4, WIDE, WIDE), half),
            pltpu.VMEM((4, D_WIDE, WIDE), half),
            pltpu.VMEM((CHUNKS, 2 * ROWS, 4 * WIDE), full),
            pltpu.VMEM((CHUNKS, 2 * ROWS, 2 * WIDE), full),
            pltpu.VMEM((4,) + rows, half),
            pltpu.VMEM(rows, half),
            pltpu.VMEM((CHUNKS, 2 * ROWS, 512), full),
            pltpu.VMEM((ROWS, WIDE), full),
            pltpu.VMEM((ROWS, WIDE), full),
            pltpu.VMEM((2 * ROWS, WIDE), full),
            pltpu.VMEM((2 * ROWS, WIDE), full),
            pltpu.VMEM((2 * ROWS, 4 * WIDE), full),
            dma((8, 2)), dma((8, 4, 2)), dma((8,)),
            dma, dma((CHUNKS,)), dma, dma((CHUNKS,)), dma, dma((CHUNKS,)), dma, dma((CHUNKS,)),
            dma((5,)), dma((4,)), dma((2,)), dma((CHUNKS // GROUP,)), dma((3,)), dma((CHUNKS // GROUP,)), dma((2,)),
        ],
        compiler_params=pltpu.CompilerParams(
            vmem_limit_bytes=60 << 20, collective_id=0, has_side_effects=True
        ),
        name="relay",
    )(*blocks, source, keep, layer_keep, cotangent)


def padded(array, rows, columns):
    return jnp.pad(array, ((0, rows - array.shape[0]), (0, columns - array.shape[1])))


def by_time(array):
    ordered = jnp.transpose(array, (2, 0, 1, 3))
    return ordered.reshape(CHUNKS, 2 * ROWS, array.shape[3])


def local(
    inputs, resets, in_mask, mid_mask, out_mask,
    w_ih_one, w_hh_one, bias_one, drop_one, w_ih_two, w_hh_two, bias_two, drop_two, cotangent,
):
    pipe = lax.axis_index("pipe")
    rec_one, rec_two = (
        (weights.astype(jnp.float32) * drop.astype(jnp.float32) * weight_scale).astype(jnp.bfloat16)
        for weights, drop in ((w_hh_one, drop_one), (w_hh_two, drop_two))
    )
    blocks = (
        padded(jnp.concatenate([w_ih_one, bias_one[None]], 0), D_WIDE, WIDE),
        padded(rec_one, WIDE, WIDE),
        padded(rec_two, WIDE, WIDE),
        padded(jnp.concatenate([w_ih_two, bias_two[None]], 0), WIDE, WIDE),
        padded(rec_one.T, WIDE, WIDE),
        padded(rec_two.T, WIDE, WIDE),
        padded(w_ih_two.T, WIDE, WIDE),
        jnp.pad(w_ih_one.T.reshape(HID, 4, 100), ((0, 2), (0, 0), (0, 28))).reshape(WIDE, 512),
    )
    keep_in = in_mask.astype(jnp.float32) * keep_scale
    source = by_time((inputs * keep_in[:, :, None, :]).astype(jnp.bfloat16)).reshape(STEPS * ROWS, D_IN)
    ones = jnp.ones((STEPS * ROWS, 1), jnp.bfloat16)
    source = padded(jnp.concatenate([source, ones], 1), STEPS * ROWS, D_WIDE)
    positions = jnp.arange(STEPS, dtype=jnp.int32)
    keep = (resets.reshape(1, ROWS) != positions[:, None]).astype(jnp.float32)
    keep = jnp.broadcast_to(keep.reshape(CHUNKS, 2 * ROWS, 1), (CHUNKS, 2 * ROWS, 128))
    layer_keep = jnp.stack([mid_mask.reshape(ROWS, HID), out_mask.reshape(ROWS, HID)]).astype(jnp.float32)
    layer_keep = jnp.pad(layer_keep * keep_scale, ((0, 0), (0, 0), (0, WIDE - HID)))
    cot = jnp.pad(by_time(cotangent), ((0, 0), (0, 0), (0, WIDE - HID)))

    u_two, hp_one, hp_two, out_two, dz_one, dz_two, dx = relay(blocks, source, keep, layer_keep, cot)

    layer = jnp.where(pipe < 2, u_two, out_two).reshape(STEPS, 2, 2, WIDE)[..., :HID]
    layer = lax.dynamic_index_in_dim(layer, pipe % 2, 1, keepdims=False)
    layer_outputs = jnp.swapaxes(layer, 0, 1)[None]
    grad_input = jnp.transpose(dx.reshape(STEPS, 2, 2, 128)[..., :100], (1, 2, 0, 3))
    keep_part = lax.dynamic_slice_in_dim(keep_in, pipe * 100, 100, 2)
    grad_input = grad_input * keep_part[:, :, None, :]

    def grads(left, right):
        return lax.dot_general(
            left.reshape(STEPS * ROWS, -1), right.reshape(STEPS * ROWS, WIDE),
            (((0,), (0,)), ((), ())), preferred_element_type=jnp.float32,
        ).astype(jnp.bfloat16)

    parts = (grads(source, dz_one), grads(hp_one, dz_one), grads(u_two, dz_two), grads(hp_two, dz_two))
    total = lax.psum(jnp.concatenate(parts, 0), "dp").astype(jnp.float32)
    in_one, total = total[:D_WIDE], total[D_WIDE:]
    rec_one_grad, in_two, rec_two_grad = total[:WIDE], total[WIDE : 2 * WIDE], total[2 * WIDE :]
    return (
        layer_outputs,
        grad_input,
        in_one[:D_IN, :HID],
        rec_one_grad[:HID, :HID] * drop_one.astype(jnp.float32) * weight_scale,
        in_one[D_IN, :HID],
        in_two[:HID, :HID],
        rec_two_grad[:HID, :HID] * drop_two.astype(jnp.float32) * weight_scale,
        in_two[HID, :HID],
    )


def solution(mesh):
    placed = (
        P(None, "dp", None, None),
        P(None, "dp"),
        P(None, "dp", None),
        P(None, "dp", None),
        P(None, "dp", None),
        P(None, "pipe"),
        P(None, "pipe"),
        P("pipe"),
        P(None, "pipe"),
        P(None, "pipe"),
        P(None, "pipe"),
        P("pipe"),
        P(None, "pipe"),
        P(None, "dp", None, None),
    )
    return jax.shard_map(
        local,
        mesh=mesh,
        in_specs=placed,
        out_specs=(
            P("pipe", "dp", None, None),
            P(None, "dp", None, "pipe"),
            P(None, "pipe"),
            P(None, "pipe"),
            P("pipe"),
            P(None, "pipe"),
            P(None, "pipe"),
            P("pipe"),
        ),
        check_vma=False,
    )
```

time: 3200 us -> 972 us (0.30)
  matrix products: 889 us -> 11.8 us
  waiting for transfers between devices: 933 us -> 388 us
  Pallas kernels: 0 us -> 394 us
  starting transfers between devices: 372 us -> 0.04 us
  local copies, waits for them, and re-layouts: 443 us -> 111 us
  other arithmetic: 289 us -> 41.2 us
  blocking collectives: 195 us -> 0 us
  loops' own time: 48.3 us -> 0 us
    dot_general x184 -> x4, matrix products: 889 us -> 11.8 us  [grads(): lax.dot_general(left.reshape(STEPS * ROWS, -1), right.reshape(STEPS * ROW...]
    ppermute x10 -> x0, waiting for transfers between devices: 413 us -> none  [the longest x4 214 us: shifted(): return lax.ppermute(block, axis, route)]
    pallas_call x0 -> x1, Pallas kernels: none -> 394 us  [relay(): pl.pallas_call(relay_kernel, out_shape=shapes, in_specs=[pl.BlockSpec(mem...]
    ppermute x10 -> x0, starting transfers between devices: 372 us -> none  [the longest x3 366 us: passed_along(): return lax.ppermute(value, axis, pairs)]
    all_gather x4 -> x0, waiting for transfers between devices: 261 us -> none  [the longest x1 103 us: local(): lax.all_gather(rec_second_own, 'pipe', axis=1, tiled=True)]
    psum x1 -> x0, blocking collectives: 184 us -> none  [local(): summed = lax.psum((part_a, part_b, part_c, part_d, part_e, part_f), 'dp')]
    another operation x24 -> x3, local copies, waits for them, and re-layouts: 145 us -> 0.33 us  [the longest x1 0.28 us: local(): by_time((inputs * keep_in[:, :, None, :]).astype(jnp.bfloat16))]
    psum x1, waiting for transfers between devices: 258 us -> 388 us  [local(): total = lax.psum(jnp.concatenate(parts, 0), 'dp').astype(jnp.float32)]
  transfers between devices with their start and end apart: 16 -> 1, of which waited for: 12 -> 1; matrix products, arithmetic and copies ran while one was open for 8% -> 0% of each run, Pallas kernels for 0% -> 0%
where the time goes in v1:
time: 972 us; the launch traced here: 961 us
  Pallas kernels  394 us (41%)
  waiting for transfers between devices  388 us (40%)
  local copies, waits for them, and re-layouts  111 us (11%)
  other arithmetic  41.2 us (4%)
  between operations  14.6 us (2%)
  matrix products  11.8 us (1%)
    pallas_call x1, Pallas kernels, relay(): pl.pallas_call(relay_kernel, out_shape=shapes, in_specs=[pl.BlockSpec(mem...  394 us
    psum x1, waiting for transfers between devices, local(): total = lax.psum(jnp.concatenate(parts, 0), 'dp').astype(jnp.float32)  388 us
    unnamed x51, local copies, waits for them, and re-layouts  59.3 us
  transfers between devices with their start and end apart: 1, of which 1 were waited for; matrix products, arithmetic and copies ran while one was open for 0% of the time, Pallas kernels for 0%

profile of v1, /device:TPU:32, one launch (start us, length us, event | category | flops | bytes accessed | tf_op | source)
XLA Modules:
  0.0 960.5 jit_solution(18370708669560214360)
XLA Ops:
  7.2 7.0 copy.76
  14.3 3.2 copy.75
  17.5 4.1 multiply_convert_fusion.1
  21.6 3.3 copy.104
  24.9 6.9 copy.78
  31.7 5.2 copy.77
  36.9 5.6 multiply_convert_fusion
  42.6 5.2 copy.105
  47.8 3.6 pad.42.clone.r_one
  51.4 1.7 pad.43.clone.r_two
  53.1 1.8 pad.45.r_one_t
  54.9 1.0 copy-done
  55.8 1.7 pad.46.r_two_t
  58.2 0.8 fusion.18.source
  59.0 0.4 copy-done.1
  59.4 3.3 copy.79
  62.7 3.6 pad.47.w_two_t
  66.3 2.4 reshape.68
  68.6 2.3 pad.48
  70.9 2.4 copy.99.w_one_t
  73.4 4.5 fusion.10.w_two
  77.9 0.6 copy.83
  78.6 0.6 reshape.70
  79.2 1.0 pad.51.cotangent
  80.2 1.0 fusion.16.w_one
  81.7 0.6 pad.50.layer_keep
  82.3 0.8 broadcast_in_dim.20.keep
  83.1 394.3 %relay.1 = (bf16[44,8,1152]{2,1,0:T(8,128)(2,1)}, bf16[44,8,1152]{2,1,0:T(8,128)(2,1)}, bf16[44,8,1152]{2,1,0:T(8,128)(2,1)}, bf16[44,8,1152]{2,1,0:T(8,128)(2,1...) custom-call(bf16[416,1152]{1,0:T(8,128)(2,1)} %fusion.16.w_one, ...), custom_call_target="tpu_custom_call" | custom-call | tf_op jit(solution)/shard_map/relay/pallas_call | solution.py:425
  477.4 4.7 fusion.1
  482.0 3.2 fusion.2
  485.3 0.7 convolution_convert_fusion
  486.0 3.2 fusion
  489.2 1.0 copy.91
  490.2 15.8 %concatenate.15 = bf16[3872,1152]{0,1:T(8,128)(2,1)} concatenate(bf16[416,1152]{0,1:T(8,128)(2,1)S(1)} %copy.91, bf16[1152,1152]{0,1:T(8,128)(2,1)} %fusion, bf16[1152,1152]{0,1:T(8,128)(2,1)} %fusion.1, bf16[1152,1152]{0,1:T(8,128)(2,1)} %fusion.2), dimensions={0} | concatenate | bytes 17842176 | tf_op jit(solution)/shard_map/concatenate | solution.py:510
  506.0 1.1 copy-done.6
  507.5 0.3 reshape.71
  508.1 0.8 copy.110
  509.0 0.7 fusion.20
  509.6 387.8 %all-reduce.14.cloned.1.call-done = bf16[3872,1152]{0,1:T(8,128)(2,1)} async-done(((bf16[3872,1152]{0,1:T(8,128)(2,1)}), bf16[3872,1152]{0,1:T(8,128)(2,1)}) %all-reduce.14.cloned.1.call-update) | async-done | bytes 8921104 | tf_op jit(solution)/shard_map/psum | solution.py:510
  897.4 11.0 %convert_element_type.83 = f32[3872,1152]{0,1:T(8,128)} convert(bf16[3872,1152]{0,1:T(8,128)(2,1)} %all-reduce.14.cloned.1.call-done) | non-fusion elementwise | flops 4460544 | bytes 26763264 | tf_op jit(solution)/shard_map/convert_element_type | solution.py:510
  908.5 13.1 %fusion.3 = (f32[1150,1150]{0,1:T(8,128)}, f32[1150,1150]{0,1:T(8,128)}) fusion(f32[3872,1152]{0,1:T(8,128)} %convert_element_type.83, s32[1150,1150]{0,1:T(8,128)} %copy.78, s32[1150,1150]{0,1:T(8,128)} %copy.76), kind=kLoop, calls=%fused_computation.7 | loop fusion | flops 7935000 | bytes 31740000 | tf_op jit(solution)/shard_map/mul | solution.py:520
  921.6 2.6 slice_reduce_fusion
  924.1 6.9 copy.93
  931.0 6.9 copy.95
  937.9 5.3 slice.51
  943.1 6.9 copy.94
  950.0 1.6 slice.48
  951.6 1.9 copy.92
  (58 shorter events, 1.9 us)
Async XLA Ops:
  7.2 890.3 %all-reduce.14.cloned.1.call-start = ((), (), s32[]{:S(2)}) async-start(), calls=%async_computation | async-start | bytes 18284544 | tf_op jit(solution)/shard_map/psum | solution.py:510
  7.2 7.0 copy-start.4
  47.8 3.6 copy-start.2
  53.1 2.7 copy-start
  55.8 1.7 copy-start.12
  55.8 1.7 copy-start.8
  57.5 1.9 copy-start.1
  68.6 4.7 copy-start.13
  73.4 4.6 copy-start.5
  77.9 2.3 copy-start.14
  77.9 2.3 copy-start.3
  78.6 2.7 copy-start.19
  78.6 3.0 copy-start.10
  78.6 3.0 copy-start.11
  477.3 4.7 copy-start.17
  477.4 4.7 copy-start.18
  482.0 3.2 copy-start.16
  482.0 4.0 copy-start.15
  506.0 1.1 copy-start.6
  506.0 1.4 copy-start.7
  507.4 1.6 copy-start.9
Sparse Core Ops, SparseCore 0:
  506.1 391.2 all-reduce.13

commit v2 on v1

--- a/solution.py
+++ b/solution.py
@@ -16,7 +16,12 @@
 ROWS = 4
 CHUNKS = 44
 GROUP = 4
-HALF = WIDE // 2
+UNIT = 128
+HALF_UNIT = 64
+UNITS = 32
+HP_ONE, SOURCE, U_TWO, HP_TWO = 0, 1152, 1792, 2944
+SOURCE_WIDE = 640
+SWITCH = 14
 
 keep_scale = 4.0 / 3.0
 weight_scale = 2.0
@@ -48,12 +53,14 @@
 def relay_kernel(
     w_one, r_one, r_two, w_two, r_one_t, r_two_t, w_two_t, w_one_t,
     source, keep, layer_keep, cotangent,
-    o_u, o_hp_one, o_hp_two, o_out, o_dz_one, o_dz_two, o_dx,
+    o_left, o_out, o_dz, o_dx,
     w_front, w_back, w_in, zx, extra, dz, du, dx, hidden, cell, stage_a, stage_b, stage_z,
     block_send, block_recv, block_local,
     u_send, u_recv, z_send, z_recv, dz_send, dz_recv, du_send, du_recv,
     bulk_send, bulk_recv, part_send, part_recv, dx_send, dx_recv, local_sem,
 ):
+    o_hp_one, o_u, o_hp_two = (o_left.at[:, :, pl.ds(start, WIDE)] for start in (HP_ONE, U_TWO, HP_TWO))
+    o_dz_one, o_dz_two = o_dz.at[0], o_dz.at[1]
     pipe = lax.axis_index("pipe")
     dp = lax.axis_index("dp")
     dp_count = lax.axis_size("dp")
@@ -69,6 +76,8 @@
             barrier, inc=1, device_id={"pipe": lax.rem(pipe + step, 4), "dp": dp_far}, device_id_type=MESH
         )
     pl.semaphore_wait(barrier, 7)
+
+    o_left[:, :, pl.ds(SOURCE, SOURCE_WIDE)] = source[...].reshape(CHUNKS, 2 * ROWS, SOURCE_WIDE)
 
     blocks = {
         W_ONE: w_one, R_ONE: r_one, R_TWO: r_two, W_TWO: w_two,
@@ -222,7 +231,7 @@
         start_blocks(FORWARD, me)
         await_blocks(W_ONE)
         for g in range(4):
-            zx[:, :, pl.ds(g * WIDE, WIDE)] = dot(source[...], w_in[g]).reshape(CHUNKS, 2 * ROWS, WIDE)
+            zx[:, :, pl.ds(g * WIDE, WIDE)] = dot(source[:, :D_WIDE], w_in[g]).reshape(CHUNKS, 2 * ROWS, WIDE)
         await_blocks(R_ONE)
         start_blocks(BACKWARD, me)
         clear()
@@ -418,15 +427,18 @@
     whole = pl.BlockSpec(memory_space=pltpu.VMEM)
     rows = (CHUNKS, 2 * ROWS, WIDE)
     half, full = jnp.bfloat16, jnp.float32
-    shapes = [jax.ShapeDtypeStruct(rows, half)] * 6 + [
-        jax.ShapeDtypeStruct((CHUNKS, 2 * ROWS, 128), full)
+    shapes = [
+        jax.ShapeDtypeStruct((CHUNKS, 2 * ROWS, UNITS * UNIT), half),
+        jax.ShapeDtypeStruct(rows, half),
+        jax.ShapeDtypeStruct((2,) + rows, half),
+        jax.ShapeDtypeStruct((CHUNKS, 2 * ROWS, 128), full),
     ]
     dma = pltpu.SemaphoreType.DMA
     return pl.pallas_call(
         relay_kernel,
         out_shape=shapes,
         in_specs=[pl.BlockSpec(memory_space=pl.ANY)] * 8 + [whole] * 4,
-        out_specs=[whole] * 7,
+        out_specs=[whole] * 4,
         scratch_shapes=[
             pltpu.VMEM((4, WIDE, WIDE), half),
             pltpu.VMEM((4, WIDE, WIDE), half),
@@ -452,6 +464,314 @@
     )(*blocks, source, keep, layer_keep, cotangent)
 
 
+def reduce_kernel(
+    left, dz, total, own, near, far, part, cross,
+    near_send, near_recv, far_send, far_recv, part_send, part_recv, last_send, last_recv,
+    cross_send, cross_recv, back_send, back_recv, wide_send, wide_recv,
+):
+    pipe = lax.axis_index("pipe")
+    dp = lax.axis_index("dp")
+    z, x, y = dp // 16, lax.rem(dp // 4, 4), lax.rem(dp, 4)
+
+    def device(z_, x_, y_):
+        return {"pipe": pipe, "dp": z_ * 16 + lax.rem(x_ + 4, 4) * 4 + lax.rem(y_ + 4, 4)}
+
+    first = (lambda d: device(z, x + d, y), lambda d: device(z, x, y + d))
+    second = (lambda d: device(z, x, y + d), lambda d: device(z, x + d, y))
+    across = device(1 - z, x, y)
+    place = ((x, y), (y, x))
+
+    barrier = pltpu.get_barrier_semaphore()
+    for target in (first[0](1), first[0](-1), first[1](1), first[1](-1), across):
+        pl.semaphore_signal(barrier, inc=1, device_id=target, device_id_type=MESH)
+    pl.semaphore_wait(barrier, 5)
+
+    def unit(p, block, rel):
+        a, b = place[p]
+        return p * 16 + lax.rem(a + block + 4, 4) * 4 + lax.rem(b + rel, 4)
+
+    def send(source, target, s, r, to):
+        return pltpu.make_async_remote_copy(source, target, s, r, device_id=to, device_id_type=MESH)
+
+    rows_of = (pl.ds(0, UNIT), pl.ds(0, HALF_UNIT), pl.ds(HALF_UNIT, HALF_UNIT))
+
+    def add(index, others, start=0, count=UNIT):
+        def body(i, carry):
+            rows = pl.ds(pl.multiple_of(start + i * 16, 16), 16)
+            value = own[index, rows].astype(jnp.float32)
+            for ref in others:
+                value = value + ref[rows].astype(jnp.float32)
+            own[index, rows] = value.astype(jnp.bfloat16)
+            return carry
+
+        lax.fori_loop(0, count // 16, body, 0)
+
+    def product(p, block, rel):
+        u = unit(p, block, rel)
+        columns = pl.ds(pl.multiple_of(u * UNIT, UNIT), UNIT)
+        which = jnp.where(u < SWITCH, 0, 1)
+        own[u] = lax.dot_general(
+            left[:, columns], dz[which], (((0,), (0,)), ((), ())), preferred_element_type=jnp.float32
+        ).astype(jnp.bfloat16)
+
+    RIGHT, LEFT = (2, 1), (3, 0)
+    side = {1: RIGHT, -1: LEFT}
+    pairs = [(p, d) for d in (1, -1) for p in (0, 1)]
+    slot = {1: 0, -1: 1}
+
+    def near_copy(p, d, k):
+        rel = side[d][k]
+        return send(own.at[unit(p, 2, rel)], near.at[p, slot[d], k], near_send.at[p, slot[d], k],
+                    near_recv.at[p, slot[d], k], first[p](d))
+
+    def far_copy(p, d, k):
+        rel = (side[-d] + side[d])[k]
+        return send(own.at[unit(p, d, rel)], far.at[p, slot[d], rel], far_send.at[p, slot[d], k],
+                    far_recv.at[p, slot[d], rel], first[p](d))
+
+    def far_arrival(p, d, rel):
+        return send(own.at[unit(p, 0, rel)], far.at[p, slot[d], rel], far_send.at[p, slot[d], 0],
+                    far_recv.at[p, slot[d], rel], first[p](d))
+
+    started = []
+
+    def go(copy):
+        copy.start()
+        started.append(copy)
+
+    for k in range(2):
+        for p, d in pairs:
+            product(p, 2, side[d][k])
+            go(near_copy(p, d, k))
+    for k in range(2):
+        for p, d in pairs:
+            product(p, d, side[-d][k])
+            go(far_copy(p, d, k))
+    for k in range(2):
+        for p, d in pairs:
+            product(p, d, side[d][k])
+    for p in (0, 1):
+        for rel in range(4):
+            product(p, 0, rel)
+    for k in range(2):
+        for p, d in pairs:
+            near_copy(p, d, k).wait_recv()
+            add(unit(p, d, side[d][k]), [near.at[p, slot[d], k]])
+            go(far_copy(p, d, 2 + k))
+
+    def collect(p, rel):
+        for d in (1, -1):
+            far_arrival(p, d, rel).wait_recv()
+        add(unit(p, 0, rel), [far.at[p, 0, rel], far.at[p, 1, rel]])
+
+    def part_copy(p, d):
+        rows = rows_of[1 if d == 1 else 2]
+        return send(own.at[unit(p, 0, 2), rows], part.at[p, slot[d], rows], part_send.at[p, slot[d]],
+                    part_recv.at[p, slot[d]], second[p](d))
+
+    def last_copy(p, d, k):
+        rel = 1 if d == 1 else 3
+        half = (2 - k) if d == 1 else (1 + k)
+        rows = rows_of[half]
+        return send(own.at[unit(p, 0, rel), rows], part.at[p, 2 + slot[d], rows], last_send.at[p, slot[d], k],
+                    last_recv.at[p, slot[d], k], second[p](d))
+
+    for p in (0, 1):
+        collect(p, 2)
+        for d in (1, -1):
+            go(part_copy(p, d))
+    for rel, d in ((3, -1), (1, 1)):
+        for p in (0, 1):
+            collect(p, rel)
+            go(last_copy(p, d, 0))
+    for p in (0, 1):
+        collect(p, 0)
+    for d in (1, -1):
+        for p in (0, 1):
+            part_copy(p, d).wait_recv()
+            rel = 1 if d == 1 else 3
+            add(unit(p, 0, rel), [part.at[p, slot[d]]], 0 if d == 1 else HALF_UNIT, HALF_UNIT)
+            go(last_copy(p, d, 1))
+
+    def cross_copy(p):
+        return send(own.at[unit(p, 0, 0)], cross.at[p], cross_send.at[p], cross_recv.at[p], across)
+
+    for p in (0, 1):
+        for d in (1, -1):
+            for k in range(2):
+                last_copy(p, d, k).wait_recv()
+        add(unit(p, 0, 0), [part.at[p, 2], part.at[p, 3]])
+        go(cross_copy(p))
+
+    def back_copy(p, d):
+        u = unit(p, 0, 0)
+        return send(total.at[u], total.at[u], back_send.at[p, slot[d], 0], back_recv.at[p, slot[d], 0], second[p](d))
+
+    def back_arrival(p, d):
+        u = unit(p, 0, -d % 4)
+        return send(total.at[u], total.at[u], back_send.at[p, slot[d], 0], back_recv.at[p, slot[d], 0], second[p](d))
+
+    def back_on(p, d):
+        u = unit(p, 0, -d % 4)
+        rows = rows_of[1 if d == 1 else 2]
+        return send(total.at[u, rows], total.at[u, rows], back_send.at[p, slot[d], 1], back_recv.at[p, slot[d], 1],
+                    second[p](d))
+
+    def back_on_arrival(p, d):
+        u = unit(p, 0, 2)
+        rows = rows_of[1 if d == 1 else 2]
+        return send(total.at[u, rows], total.at[u, rows], back_send.at[p, slot[d], 1], back_recv.at[p, slot[d], 1],
+                    second[p](d))
+
+    def wide_copy(p, d, rel):
+        u = unit(p, 0, rel)
+        return send(total.at[u], total.at[u], wide_send.at[p, slot[d], rel], wide_recv.at[p, slot[d], rel], first[p](d))
+
+    def wide_arrival(p, d, rel):
+        u = unit(p, -d % 4, rel)
+        return send(total.at[u], total.at[u], wide_send.at[p, slot[d], rel], wide_recv.at[p, slot[d], rel], first[p](d))
+
+    ON = {1: (0, 1), -1: (3, 2)}
+
+    def wide_on(p, d, k):
+        u = unit(p, -d % 4, ON[d][k])
+        return send(total.at[u], total.at[u], wide_send.at[p, slot[d], 4 + k], wide_recv.at[p, slot[d], 4 + k], first[p](d))
+
+    def wide_on_arrival(p, d, k):
+        u = unit(p, 2, ON[d][k])
+        return send(total.at[u], total.at[u], wide_send.at[p, slot[d], 4 + k], wide_recv.at[p, slot[d], 4 + k], first[p](d))
+
+    for p in (0, 1):
+        cross_copy(p).wait_recv()
+        u = unit(p, 0, 0)
+
+        def body(i, carry):
+            rows = pl.ds(pl.multiple_of(i * 16, 16), 16)
+            value = own[u, rows].astype(jnp.float32) + cross[p, rows].astype(jnp.float32)
+            total[u, rows] = value.astype(jnp.bfloat16)
+            return carry
+
+        lax.fori_loop(0, UNIT // 16, body, 0)
+        for d in (1, -1):
+            go(back_copy(p, d))
+        for d in (1, -1):
+            go(wide_copy(p, d, 0))
+    for d in (1, -1):
+        for p in (0, 1):
+            back_arrival(p, d).wait_recv()
+            go(back_on(p, d))
+            for e in (1, -1):
+                go(wide_copy(p, e, -d % 4))
+    for p in (0, 1):
+        for d in (1, -1):
+            back_on_arrival(p, d).wait_recv()
+        for d in (1, -1):
+            go(wide_copy(p, d, 2))
+    for k in range(2):
+        for d in (1, -1):
+            for p in (0, 1):
+                wide_arrival(p, d, ON[d][k]).wait_recv()
+                go(wide_on(p, d, k))
+    for p in (0, 1):
+        for d in (1, -1):
+            for rel in range(4):
+                if rel not in ON[d]:
+                    wide_arrival(p, d, rel).wait_recv()
+            for k in range(2):
+                wide_on_arrival(p, d, k).wait_recv()
+    for copy in started:
+        copy.wait_send()
+
+
+def reduce_over_dp(left, dz):
+    whole = pl.BlockSpec(memory_space=pltpu.VMEM)
+    half = jnp.bfloat16
+    dma = pltpu.SemaphoreType.DMA
+    return pl.pallas_call(
+        reduce_kernel,
+        out_shape=jax.ShapeDtypeStruct((UNITS, UNIT, WIDE), half),
+        in_specs=[whole] * 2,
+        out_specs=whole,
+        scratch_shapes=[
+            pltpu.VMEM((UNITS, UNIT, WIDE), half),
+            pltpu.VMEM((2, 2, 2, UNIT, WIDE), half),
+            pltpu.VMEM((2, 2, 4, UNIT, WIDE), half),
+            pltpu.VMEM((2, 4, UNIT, WIDE), half),
+            pltpu.VMEM((2, UNIT, WIDE), half),
+            dma((2, 2, 2)), dma((2, 2, 2)), dma((2, 2, 4)), dma((2, 2, 4)), dma((2, 2)), dma((2, 2)),
+            dma((2, 2, 2)), dma((2, 2, 2)), dma((2,)), dma((2,)), dma((2, 2, 2)), dma((2, 2, 2)),
+            dma((2, 2, 6)), dma((2, 2, 6)),
+        ],
+        compiler_params=pltpu.CompilerParams(
+            vmem_limit_bytes=60 << 20, collective_id=1, has_side_effects=True
+        ),
+        name="reduce",
+    )(left, dz)
+
+
+def prepare_kernel(
+    w_one, bias_one, r_one, drop_one, w_two, bias_two, r_two, drop_two,
+    o_w_one, o_r_one, o_r_two, o_w_two, o_r_one_t, o_r_two_t, o_w_two_t, o_w_one_t,
+    square, small, apart,
+):
+    column = pl.program_id(0) * UNIT + lax.broadcasted_iota(jnp.int32, (WIDE, UNIT), 1)
+    inside = column < HID
+
+    def finish(o_plain, o_turned, turned_rows):
+        value = jnp.where(inside, square[...], 0.0)
+        o_plain[...] = value.astype(jnp.bfloat16)
+        row = lax.broadcasted_iota(jnp.int32, (WIDE, UNIT), 0)
+        if turned_rows < WIDE:
+            value = jnp.where(row < turned_rows, value, 0.0)
+        o_turned[...] = value.T.astype(jnp.bfloat16)
+
+    square[...] = jnp.zeros_like(square)
+    for weights, drop, o_plain, o_turned in (
+        (r_one, drop_one, o_r_one, o_r_one_t), (r_two, drop_two, o_r_two, o_r_two_t),
+    ):
+        square[:HID, :] = weights[...].astype(jnp.float32) * drop[...].astype(jnp.float32) * weight_scale
+        finish(o_plain, o_turned, WIDE)
+    square[:HID, :] = w_two[...].astype(jnp.float32)
+    square[HID : HID + 1, :] = bias_two[...].astype(jnp.float32)
+    finish(o_w_two, o_w_two_t, HID)
+
+    w_one_f = w_one[...].astype(jnp.float32)
+    small[...] = jnp.zeros_like(small)
+    small[:D_IN, :] = w_one_f
+    small[D_IN : D_IN + 1, :] = bias_one[...].astype(jnp.float32)
+    o_w_one[...] = jnp.where(inside[:D_WIDE], small[...], 0.0).astype(jnp.bfloat16)
+    apart[...] = jnp.zeros_like(apart)
+    for q in range(4):
+        apart[q * UNIT : q * UNIT + 100, :] = small[q * 100 : q * 100 + 100, :]
+    o_w_one_t[...] = jnp.where(inside[:512], apart[...], 0.0).T.astype(jnp.bfloat16)
+
+
+def prepare(w_one, bias_one, r_one, drop_one, w_two, bias_two, r_two, drop_two):
+    half = jnp.bfloat16
+
+    def slab(rows):
+        return pl.BlockSpec((rows, UNIT), lambda j: (0, j))
+
+    def turned(columns):
+        return pl.BlockSpec((UNIT, columns), lambda j: (j, 0))
+
+    square = jax.ShapeDtypeStruct((WIDE, WIDE), half)
+    return pl.pallas_call(
+        prepare_kernel,
+        grid=(WIDE // UNIT,),
+        in_specs=[slab(D_IN), slab(1), slab(HID), slab(HID), slab(HID), slab(1), slab(HID), slab(HID)],
+        out_specs=[slab(D_WIDE)] + [slab(WIDE)] * 3 + [turned(WIDE)] * 3 + [turned(512)],
+        out_shape=[jax.ShapeDtypeStruct((D_WIDE, WIDE), half)] + [square] * 6
+        + [jax.ShapeDtypeStruct((WIDE, 512), half)],
+        scratch_shapes=[
+            pltpu.VMEM((WIDE, UNIT), jnp.float32), pltpu.VMEM((D_WIDE, UNIT), jnp.float32),
+            pltpu.VMEM((512, UNIT), jnp.float32),
+        ],
+        compiler_params=pltpu.CompilerParams(vmem_limit_bytes=32 << 20),
+        name="prepare",
+    )(w_one, bias_one[None], r_one, drop_one, w_two, bias_two[None], r_two, drop_two)
+
+
 def padded(array, rows, columns):
     return jnp.pad(array, ((0, rows - array.shape[0]), (0, columns - array.shape[1])))
 
@@ -466,24 +786,11 @@
     w_ih_one, w_hh_one, bias_one, drop_one, w_ih_two, w_hh_two, bias_two, drop_two, cotangent,
 ):
     pipe = lax.axis_index("pipe")
-    rec_one, rec_two = (
-        (weights.astype(jnp.float32) * drop.astype(jnp.float32) * weight_scale).astype(jnp.bfloat16)
-        for weights, drop in ((w_hh_one, drop_one), (w_hh_two, drop_two))
-    )
-    blocks = (
-        padded(jnp.concatenate([w_ih_one, bias_one[None]], 0), D_WIDE, WIDE),
-        padded(rec_one, WIDE, WIDE),
-        padded(rec_two, WIDE, WIDE),
-        padded(jnp.concatenate([w_ih_two, bias_two[None]], 0), WIDE, WIDE),
-        padded(rec_one.T, WIDE, WIDE),
-        padded(rec_two.T, WIDE, WIDE),
-        padded(w_ih_two.T, WIDE, WIDE),
-        jnp.pad(w_ih_one.T.reshape(HID, 4, 100), ((0, 2), (0, 0), (0, 28))).reshape(WIDE, 512),
-    )
+    blocks = prepare(w_ih_one, bias_one, w_hh_one, drop_one, w_ih_two, bias_two, w_hh_two, drop_two)
     keep_in = in_mask.astype(jnp.float32) * keep_scale
     source = by_time((inputs * keep_in[:, :, None, :]).astype(jnp.bfloat16)).reshape(STEPS * ROWS, D_IN)
     ones = jnp.ones((STEPS * ROWS, 1), jnp.bfloat16)
-    source = padded(jnp.concatenate([source, ones], 1), STEPS * ROWS, D_WIDE)
+    source = padded(jnp.concatenate([source, ones], 1), STEPS * ROWS, SOURCE_WIDE)
     positions = jnp.arange(STEPS, dtype=jnp.int32)
     keep = (resets.reshape(1, ROWS) != positions[:, None]).astype(jnp.float32)
     keep = jnp.broadcast_to(keep.reshape(CHUNKS, 2 * ROWS, 1), (CHUNKS, 2 * ROWS, 128))
@@ -491,8 +798,11 @@
     layer_keep = jnp.pad(layer_keep * keep_scale, ((0, 0), (0, 0), (0, WIDE - HID)))
     cot = jnp.pad(by_time(cotangent), ((0, 0), (0, 0), (0, WIDE - HID)))
 
-    u_two, hp_one, hp_two, out_two, dz_one, dz_two, dx = relay(blocks, source, keep, layer_keep, cot)
-
+    left, out_two, dz, dx = relay(blocks, source, keep, layer_keep, cot)
+    left = left.reshape(STEPS * ROWS, UNITS * UNIT)
+    total = reduce_over_dp(left, dz.reshape(2, STEPS * ROWS, WIDE)).reshape(UNITS * UNIT, WIDE)
+
+    u_two = left[:, U_TWO : U_TWO + WIDE].reshape(out_two.shape)
     layer = jnp.where(pipe < 2, u_two, out_two).reshape(STEPS, 2, 2, WIDE)[..., :HID]
     layer = lax.dynamic_index_in_dim(layer, pipe % 2, 1, keepdims=False)
     layer_outputs = jnp.swapaxes(layer, 0, 1)[None]
@@ -500,25 +810,18 @@
     keep_part = lax.dynamic_slice_in_dim(keep_in, pipe * 100, 100, 2)
     grad_input = grad_input * keep_part[:, :, None, :]
 
-    def grads(left, right):
-        return lax.dot_general(
-            left.reshape(STEPS * ROWS, -1), right.reshape(STEPS * ROWS, WIDE),
-            (((0,), (0,)), ((), ())), preferred_element_type=jnp.float32,
-        ).astype(jnp.bfloat16)
-
-    parts = (grads(source, dz_one), grads(hp_one, dz_one), grads(u_two, dz_two), grads(hp_two, dz_two))
-    total = lax.psum(jnp.concatenate(parts, 0), "dp").astype(jnp.float32)
-    in_one, total = total[:D_WIDE], total[D_WIDE:]
-    rec_one_grad, in_two, rec_two_grad = total[:WIDE], total[WIDE : 2 * WIDE], total[2 * WIDE :]
+    def grads(start, rows):
+        return total[start : start + rows, :HID].astype(jnp.float32)
+
     return (
         layer_outputs,
         grad_input,
-        in_one[:D_IN, :HID],
-        rec_one_grad[:HID, :HID] * drop_one.astype(jnp.float32) * weight_scale,
-        in_one[D_IN, :HID],
-        in_two[:HID, :HID],
-        rec_two_grad[:HID, :HID] * drop_two.astype(jnp.float32) * weight_scale,
-        in_two[HID, :HID],
+        grads(SOURCE, D_IN),
+        grads(HP_ONE, HID) * drop_one.astype(jnp.float32) * weight_scale,
+        grads(SOURCE + D_IN, 1)[0],
+        grads(U_TWO, HID),
+        grads(HP_TWO, HID) * drop_two.astype(jnp.float32) * weight_scale,
+        grads(U_TWO + HID, 1)[0],
     )
 
 

time: 972 us -> 582 us (0.60); the launches traced: 961 us -> 582 us
  waiting for transfers between devices: 388 us -> 0 us
  Pallas kernels: 394 us -> 531 us
  local copies, waits for them, and re-layouts: 111 us -> 25.6 us
  other arithmetic: 41.2 us -> 24.5 us
  between operations: 14.6 us -> 0.78 us
  matrix products: 11.8 us -> 0 us
    psum x1 -> x0, waiting for transfers between devices: 388 us -> none  [local(): total = lax.psum(jnp.concatenate(parts, 0), 'dp').astype(jnp.float32)]
    pallas_call x0 -> x2, Pallas kernels: none -> 131 us  [the longest x1 119 us: reduce_over_dp(): pl.pallas_call(reduce_kernel, out_shape=jax.ShapeDtypeStruct((UNITS, UNIT...]
    unnamed x51 -> x22, local copies, waits for them, and re-layouts: 59.3 us -> 12.3 us
    concatenate x1 -> x0, local copies, waits for them, and re-layouts: 15.8 us -> none  [local(): total = lax.psum(jnp.concatenate(parts, 0), 'dp').astype(jnp.float32)]
    pad x6 -> x0, local copies, waits for them, and re-layouts: 14.7 us -> none  [the longest x5 12.4 us: padded(): jnp.pad(array, ((0, rows - array.shape[0]), (0, columns - array.shape[1])))]
    convert_element_type x3 -> x2, other arithmetic: 20.8 us -> 7 us  [grads(): return total[start:start + rows, :HID].astype(jnp.float32)]
    dot_general x4 -> x0, matrix products: 11.8 us -> none  [grads(): lax.dot_general(left.reshape(STEPS * ROWS, -1), right.reshape(STEPS * ROW...]
  transfers between devices with their start and end apart: 1 -> 0, of which waited for: 1 -> 0; matrix products, arithmetic and copies ran while one was open for 0% -> 0% of each run, Pallas kernels for 0% -> 0%
where the time goes in v2:
time: 582 us
  Pallas kernels  531 us (91%)
  local copies, waits for them, and re-layouts  25.6 us (4%)
  other arithmetic  24.5 us (4%)
    pallas_call x1, Pallas kernels, relay(): pl.pallas_call(relay_kernel, out_shape=shapes, in_specs=[pl.BlockSpec(mem...  400 us
    pallas_call x1, Pallas kernels, reduce_over_dp(): pl.pallas_call(reduce_kernel, out_shape=jax.ShapeDtypeStruct((UNITS, UNIT...  119 us
    unnamed x22, local copies, waits for them, and re-layouts  12.3 us

profile of v2, /device:TPU:32, one launch (start us, length us, event | category | flops | bytes accessed | tf_op | source)
XLA Modules:
  0.0 581.5 jit_solution(16170635472922035078)
XLA Ops:
  0.6 0.0 copy-start
  0.7 0.9 ne.37
  1.6 0.1 ne.39
  1.7 0.1 compare_convert_fusion
  1.7 0.7 broadcast_in_dim.8.bias_one
  2.4 0.7 broadcast_in_dim.9.bias_two
  3.1 0.7 convert_multiply_fusion
  3.8 0.1 constant_dynamic-slice_fusion
  3.9 0.7 stack_reshape.6
  4.7 0.7 stack_reshape.7
  5.4 0.6 pad.14.layer_keep
  6.0 0.1 copy.27
  6.1 0.8 broadcast_in_dim.20.keep
  6.9 1.2 fusion.2
  8.1 0.3 copy.26
  8.4 0.3 reshape_reshape.3
  8.7 0.8 fusion.source
  9.5 2.7 copy.28
  12.2 2.3 reshape.65
  14.5 1.0 pad.15.cotangent
  15.4 0.0 copy-done
  15.5 1.2 copy-done.9
  16.6 11.2 %prepare.1 = (bf16[416,1152]{1,0:T(8,128)(2,1)S(1)}, bf16[1152,1152]{1,0:T(8,128)(2,1)S(1)}, bf16[1152,1152]{1,0:T(8,128)(2,1)S(1)}, bf16[1152,1152]{1,0:T(8,128...) custom-call(bf16[400,1150]{1,0:T(8,128)(2,1)S(1)} %copy-done.9, ...), custom_call_target="tpu_custom_call" | custom-call | tf_op jit(solution)/shard_map/prepare/pallas_call | solution.py:759
  27.8 0.0 copy-start.1
  27.8 1.5 copy-done.1
  29.3 0.0 copy-start.2
  29.3 1.5 copy-done.2
  30.8 1.5 copy-done.3
  32.3 0.0 copy-start.4
  32.3 1.5 copy-done.4
  33.8 0.0 copy-start.5
  33.9 1.6 copy-done.5
  35.4 1.5 copy-done.6
  36.9 1.0 copy-done.7
  37.9 1.0 copy-done.8
  38.9 400.1 %relay.1 = (bf16[44,8,4096]{2,1,0:T(8,128)(2,1)}, bf16[44,8,1152]{2,1,0:T(8,128)(2,1)}, bf16[2,44,8,1152]{3,2,1,0:T(8,128)(2,1)}, f32[44,8,128]{2,1,0:T(8,128)}) custom-call(bf16[416,1152]{1,0:T(8,128)(2,1)} %copy-done.8, bf16[1152,1152]{1,0:T(8,128)(2,1)} %copy-done.1, bf16[1152,1152]{1,0:T(8,128)(2,1)} %copy-done.2, bf16[1152,1152]{1,0:T(8,128)(2,1)} %copy-done.3, ...), custom_call_target="tpu_custom_call" | custom-call | tf_op jit(solution)/shard_map/relay/pallas_call | solution.py:437
  439.0 0.0 copy-start.10
  439.0 1.5 fusion.1
  440.5 0.3 reshape.68
  440.8 0.3 constant_dynamic-slice_fusion.1
  441.1 0.8 copy.36
  441.9 0.0 copy-done.10
  441.9 0.7 fusion.3
  442.6 119.5 %reduce.5 = bf16[32,128,1152]{2,1,0:T(8,128)(2,1)} custom-call(bf16[352,4096]{1,0:T(8,128)(2,1)} %bitcast.28, bf16[2,352,1152]{2,1,0:T(8,128)(2,1)} %bitcast.30), custom_call_target="tpu_custom_call" | custom-call | tf_op jit(solution)/shard_map/reduce/pallas_call | solution.py:690
  562.1 1.4 fusion.5
  563.5 2.5 slice_convert_fusion.1
  566.0 4.5 slice_convert_fusion
  570.5 11.1 %multiply_multiply_fusion = (f32[1150,1150]{1,0:T(8,128)}, f32[1150,1150]{1,0:T(8,128)}) fusion(s32[1150,1150]{1,0:T(8,128)} %drop_two.1, bf16[4096,1152]{1,0:T(8,128)(2,1)} %bitcast.26, s32[1150,1150]{1,0:T(8,128)} %drop_one.1), kind=kLoop, calls=%fused_computation | loop fusion | flops 10580000 | bytes 26450000 | tf_op jit(solution)/shard_map/mul | solution.py:823
  (9 shorter events, 0.0 us)
Async XLA Ops:
  0.6 14.8 %copy-start = (bf16[1150,1150]{1,0:T(8,128)(2,1)S(1)}, bf16[1150,1150]{1,0:T(8,128)(2,1)}, u32[]{:S(2)}) copy-start(bf16[1150,1150]{1,0:T(8,128)(2,1)} %r_one.1) | copy-start | bytes 7935004
  15.5 1.2 copy-start.9
  27.8 1.5 copy-start.1
  29.3 1.5 copy-start.2
  30.8 1.5 copy-start.3
  32.3 1.5 copy-start.4
  33.8 1.6 copy-start.5
  35.4 1.5 copy-start.6
  36.9 1.0 copy-start.7
  37.9 1.0 copy-start.8
  439.0 2.9 copy-start.10

commit v3 on v2

--- a/solution.py
+++ b/solution.py
@@ -16,6 +16,8 @@
 ROWS = 4
 CHUNKS = 44
 GROUP = 4
+LATER = 3
+TURNS = 36
 UNIT = 128
 HALF_UNIT = 64
 UNITS = 32
@@ -38,7 +40,7 @@
     W_TWO_T: BETWEEN,
     W_ONE_T: SOURCE_GRAD,
 }
-FORWARD = (W_ONE, W_TWO, R_ONE, R_TWO)
+FORWARD = (W_ONE,)
 BACKWARD = (R_TWO_T, W_TWO_T, R_ONE_T, W_ONE_T)
 
 
@@ -55,7 +57,7 @@
     source, keep, layer_keep, cotangent,
     o_left, o_out, o_dz, o_dx,
     w_front, w_back, w_in, zx, extra, dz, du, dx, hidden, cell, stage_a, stage_b, stage_z,
-    block_send, block_recv, block_local,
+    block_send, block_recv, block_local, cross_send, cross_recv, ring_send, ring_recv, go_on,
     u_send, u_recv, z_send, z_recv, dz_send, dz_recv, du_send, du_recv,
     bulk_send, bulk_recv, part_send, part_recv, dx_send, dx_recv, local_sem,
 ):
@@ -75,7 +77,15 @@
         pl.semaphore_signal(
             barrier, inc=1, device_id={"pipe": lax.rem(pipe + step, 4), "dp": dp_far}, device_id_type=MESH
         )
-    pl.semaphore_wait(barrier, 7)
+    z, x, y = dp // 16, lax.rem(dp // 4, 4), lax.rem(dp, 4)
+    rings = (
+        lambda d: {"pipe": pipe, "dp": z * 16 + lax.rem(x + d + 4, 4) * 4 + y},
+        lambda d: {"pipe": pipe, "dp": z * 16 + x * 4 + lax.rem(y + d + 4, 4)},
+    )
+    for ring in rings:
+        for d in (1, -1):
+            pl.semaphore_signal(barrier, inc=1, device_id=ring(d), device_id_type=MESH)
+    pl.semaphore_wait(barrier, 11)
 
     o_left[:, :, pl.ds(SOURCE, SOURCE_WIDE)] = source[...].reshape(CHUNKS, 2 * ROWS, SOURCE_WIDE)
 
@@ -93,7 +103,7 @@
             return w_front.at[p, :, pl.ds(0, 512)]
         return w_back.at[p]
 
-    def block_copies(kind, p):
+    def block_copies(kind, p, turn=None):
         user = USER[kind]
         source_ref, target = blocks[kind], landing(kind, p)
         if p == user:
@@ -106,19 +116,129 @@
                 )
             ]
         rows = source_ref.shape[0] // 2
+        if turn is None:
+            spans = [pl.ds(part * rows, rows) for part in range(2)]
+        else:
+            piece = rows // TURNS
+            spans = [pl.ds(pl.multiple_of(part * rows + turn * piece, piece), piece) for part in range(2)]
         return [
             pltpu.make_async_remote_copy(
-                source_ref.at[pl.ds(part * rows, rows)], target.at[pl.ds(part * rows, rows)],
+                source_ref.at[spans[part]], target.at[spans[part]],
                 block_send.at[kind, part], block_recv.at[kind, p, part],
                 device_id={"pipe": user, "dp": (dp, dp_far)[part]}, device_id_type=MESH,
             )
             for part in range(2)
         ]
 
+    def rows_at(first, count=UNIT):
+        return pl.ds(pl.multiple_of(first, 64), count)
+
+    def part_rows(ring, step):
+        place = (x, y)[ring]
+        return UNIT * (1 + 4 * ring + lax.rem(place + step + 4, 4))
+
+    def from_other_plane(kind):
+        return [p for p in range(4) if p // 2 != USER[kind] // 2]
+
+    def cross_copy(kind, p, k, slot):
+        rows = rows_at((part_rows(0, 0), part_rows(1, 0), 0)[k])
+        return pltpu.make_async_remote_copy(
+            blocks[kind].at[rows], w_front.at[p, rows], cross_send.at[slot, k], cross_recv.at[p % 2, k],
+            device_id={"pipe": USER[kind], "dp": (dp, dp_far)[p % 2]}, device_id_type=MESH,
+        )
+
+    def ring_copy(p, ring, d, on):
+        k = 2 * on + (0 if d == 1 else 1)
+        if on:
+            rows = rows_at(part_rows(ring, -d) + (0 if d == 1 else HALF_UNIT), HALF_UNIT)
+        else:
+            rows = rows_at(part_rows(ring, 0))
+        ref = w_front.at[p, rows]
+        return pltpu.make_async_remote_copy(
+            ref, ref, ring_send.at[p % 2, ring, k], ring_recv.at[p % 2, ring, k],
+            device_id=rings[ring](d), device_id_type=MESH,
+        )
+
+    def ring_arrival(p, ring, d, on):
+        k = 2 * on + (0 if d == 1 else 1)
+        if on:
+            rows = rows_at(part_rows(ring, 2) + (0 if d == 1 else HALF_UNIT), HALF_UNIT)
+        else:
+            rows = rows_at(part_rows(ring, -d))
+        ref = w_front.at[p, rows]
+        return pltpu.make_async_remote_copy(
+            ref, ref, ring_send.at[p % 2, ring, k], ring_recv.at[p % 2, ring, k],
+            device_id=rings[ring](d), device_id_type=MESH,
+        )
+
+    SPREAD = (W_TWO, R_TWO, R_ONE)
+
+    def start_spread(me):
+        kinds = [kind for kind in SPREAD if me // 2 != USER[kind] // 2]
+        for k in range(3):
+            for slot, kind in enumerate(kinds):
+                cross_copy(kind, me, k, slot).start()
+        for kind in SPREAD:
+            if me // 2 == USER[kind] // 2:
+                block_copies(kind, me)[0].start()
+
+    def finish_spread(me):
+        kinds = [kind for kind in SPREAD if me // 2 != USER[kind] // 2]
+        for slot, kind in enumerate(kinds):
+            for k in range(3):
+                cross_copy(kind, me, k, slot).wait_send()
+        for kind in SPREAD:
+            if me // 2 == USER[kind] // 2 and me != USER[kind]:
+                block_copies(kind, me)[0].wait_send()
+
+    def receive_spread(kind):
+        me = USER[kind]
+        others = from_other_plane(kind)
+        for ring in range(2):
+            for p in others:
+                cross_copy(kind, p, ring, 0).wait_recv()
+                for d in (1, -1):
+                    ring_copy(p, ring, d, 0).start()
+        for d in (1, -1):
+            for p in others:
+                for ring in range(2):
+                    ring_arrival(p, ring, d, 0).wait_recv()
+                    ring_copy(p, ring, d, 1).start()
+        for p in others:
+            cross_copy(kind, p, 2, 0).wait_recv()
+            for ring in range(2):
+                for d in (1, -1):
+                    ring_arrival(p, ring, d, 1).wait_recv()
+        for p in (me, me ^ 1):
+            copy = block_copies(kind, p)[0]
+            if p == me:
+                copy.wait()
+            else:
+                copy.wait_recv()
+
+    def finish_rings(kind):
+        for p in from_other_plane(kind):
+            for ring in range(2):
+                for d in (1, -1):
+                    for on in range(2):
+                        ring_copy(p, ring, d, on).wait_send()
+
     def start_blocks(kinds, p):
         for kind in kinds:
             for copy in block_copies(kind, p):
                 copy.start()
+
+    def start_near(p):
+        for kind in BACKWARD:
+            if p // 2 == USER[kind] // 2:
+                for copy in block_copies(kind, p):
+                    copy.start()
+
+    def start_turn(p, turn):
+        for kind in BACKWARD:
+            if p // 2 != USER[kind] // 2:
+                for copy in block_copies(kind, p, turn):
+                    copy.start()
 
     def finish_blocks(kinds, p):
         for kind in kinds:
@@ -228,17 +348,29 @@
     @pl.when(pipe == LAYER_ONE)
     def _():
         me = LAYER_ONE
+        start_spread(me)
         start_blocks(FORWARD, me)
         await_blocks(W_ONE)
         for g in range(4):
             zx[:, :, pl.ds(g * WIDE, WIDE)] = dot(source[:, :D_WIDE], w_in[g]).reshape(CHUNKS, 2 * ROWS, WIDE)
-        await_blocks(R_ONE)
-        start_blocks(BACKWARD, me)
+        receive_spread(R_ONE)
         clear()
 
         def ahead(c, carry):
             forward_pair(c, layer_keep[0], True, o_hp_one, o_u)
             copy_u(c).start()
+
+            @pl.when((c >= LATER) & (c < LATER + TURNS))
+            def _():
+                pl.semaphore_signal(
+                    go_on, inc=1, device_id={"pipe": SOURCE_GRAD, "dp": dp}, device_id_type=MESH
+                )
+                start_turn(me, c - LATER)
+
+            @pl.when(c == LATER)
+            def _():
+                start_near(me)
+
             return carry
 
         lax.fori_loop(0, CHUNKS, ahead, 0)
@@ -269,6 +401,8 @@
         lax.fori_loop(0, CHUNKS, behind, 0)
         own = pltpu.make_async_copy(dz.at[me], o_dz_one, local_sem.at[0])
         own.start()
+        finish_rings(R_ONE)
+        finish_spread(me)
         finish_blocks(FORWARD + BACKWARD, me)
         to(BETWEEN, o_u, o_u, u_send, u_recv.at[0]).wait_send()
         for copy in bulk:
@@ -286,13 +420,22 @@
     @pl.when(pipe == LAYER_TWO)
     def _():
         me = LAYER_TWO
+        start_spread(me)
         start_blocks(FORWARD, me)
-        await_blocks(R_TWO)
-        start_blocks(BACKWARD, me)
+        receive_spread(R_TWO)
         clear()
 
         def ahead(c, carry):
             copy_z(c).wait_recv()
+
+            @pl.when((c >= LATER) & (c < LATER + TURNS))
+            def _():
+                start_turn(me, c - LATER)
+
+            @pl.when(c == LATER)
+            def _():
+                start_near(me)
+
             forward_pair(c, layer_keep[1], False, o_hp_two, o_out)
             return carry
 
@@ -322,6 +465,8 @@
         lax.fori_loop(0, CHUNKS, behind, 0)
         own = pltpu.make_async_copy(dz.at[me], o_dz_two, local_sem.at[0])
         own.start()
+        finish_rings(R_TWO)
+        finish_spread(me)
         finish_blocks(FORWARD + BACKWARD, me)
         for copy in bulk:
             copy.wait_send()
@@ -339,15 +484,24 @@
     @pl.when(pipe == BETWEEN)
     def _():
         me = BETWEEN
+        start_spread(me)
         start_blocks(FORWARD, me)
-        await_blocks(W_TWO)
-        start_blocks(BACKWARD, me)
+        receive_spread(W_TWO)
 
         def ahead(c, carry):
             copy_u(c).wait_recv()
             for g in range(4):
                 zx[c, :, pl.ds(g * WIDE, WIDE)] = dot(o_u[c], w_front[g])
             copy_z(c).start()
+
+            @pl.when((c >= LATER) & (c < LATER + TURNS))
+            def _():
+                start_turn(me, c - LATER)
+
+            @pl.when(c == LATER)
+            def _():
+                start_near(me)
+
             return carry
 
         lax.fori_loop(0, CHUNKS, ahead, 0)
@@ -367,6 +521,8 @@
         lax.fori_loop(0, CHUNKS, behind, 0)
         own = pltpu.make_async_copy(dz.at[me], o_dz_two, local_sem.at[0])
         own.start()
+        finish_rings(W_TWO)
+        finish_spread(me)
         finish_blocks(FORWARD + BACKWARD, me)
         to(LAYER_TWO, zx, zx, z_send, z_recv.at[0]).wait_send()
         to(LAYER_ONE, du, du, du_send, du_recv.at[0]).wait_send()
@@ -382,9 +538,16 @@
     @pl.when(pipe == SOURCE_GRAD)
     def _():
         me = SOURCE_GRAD
+        start_spread(me)
         start_blocks(FORWARD, me)
-        finish_blocks(FORWARD, me)
-        start_blocks(BACKWARD, me)
+
+        def pass_on(turn, carry):
+            pl.semaphore_wait(go_on, 1)
+            start_turn(me, turn)
+            return carry
+
+        lax.fori_loop(0, TURNS, pass_on, 0)
+        start_near(me)
         await_blocks(W_ONE_T)
 
         def behind(i, carry):
@@ -410,7 +573,8 @@
         own.start()
         own_dx = pltpu.make_async_copy(dx.at[:, :, pl.ds(me * 128, 128)], o_dx, local_sem.at[1])
         own_dx.start()
-        finish_blocks(BACKWARD, me)
+        finish_spread(me)
+        finish_blocks(FORWARD + BACKWARD, me)
         for slot, pipe_to in enumerate((LAYER_ONE, LAYER_TWO, BETWEEN)):
             to(pipe_to, o_dx, o_dx, dx_send.at[slot], dx_recv.at[0]).wait_send()
         own.wait()
@@ -454,6 +618,7 @@
             pltpu.VMEM((2 * ROWS, WIDE), full),
             pltpu.VMEM((2 * ROWS, 4 * WIDE), full),
             dma((8, 2)), dma((8, 4, 2)), dma((8,)),
+            dma((2, 3)), dma((2, 3)), dma((2, 2, 4)), dma((2, 2, 4)), pltpu.SemaphoreType.REGULAR,
             dma, dma((CHUNKS,)), dma, dma((CHUNKS,)), dma, dma((CHUNKS,)), dma, dma((CHUNKS,)),
             dma((5,)), dma((4,)), dma((2,)), dma((CHUNKS // GROUP,)), dma((3,)), dma((CHUNKS // GROUP,)), dma((2,)),
         ],
@@ -767,7 +932,7 @@
             pltpu.VMEM((WIDE, UNIT), jnp.float32), pltpu.VMEM((D_WIDE, UNIT), jnp.float32),
             pltpu.VMEM((512, UNIT), jnp.float32),
         ],
-        compiler_params=pltpu.CompilerParams(vmem_limit_bytes=32 << 20),
+        compiler_params=pltpu.CompilerParams(vmem_limit_bytes=60 << 20),
         name="prepare",
     )(w_one, bias_one[None], r_one, drop_one, w_two, bias_two[None], r_two, drop_two)
 

time: 582 us -> 507 us (0.87)
  Pallas kernels: 531 us -> 469 us
  local copies, waits for them, and re-layouts: 25.6 us -> 11.8 us
    pallas_call x1, Pallas kernels: 400 us -> 334 us  [relay(): pl.pallas_call(relay_kernel, out_shape=shapes, in_specs=[pl.BlockSpec(mem...]
    unnamed x22 -> x2, local copies, waits for them, and re-layouts: 12.3 us -> 0.01 us
where the time goes in v3:
time: 507 us; the launch traced here: 506 us
  Pallas kernels  469 us (93%)
  other arithmetic  24.5 us (5%)
  local copies, waits for them, and re-layouts  11.8 us (2%)
    pallas_call x1, Pallas kernels, relay(): pl.pallas_call(relay_kernel, out_shape=shapes, in_specs=[pl.BlockSpec(mem...  334 us
    pallas_call x1, Pallas kernels, reduce_over_dp(): pl.pallas_call(reduce_kernel, out_shape=jax.ShapeDtypeStruct((UNITS, UNIT...  118 us
    pallas_call x1, Pallas kernels, prepare(): pl.pallas_call(prepare_kernel, grid=(WIDE // UNIT,), in_specs=[slab(D_IN)...  16.9 us
    mul x1, other arithmetic, local(): grads(HP_TWO, HID) * drop_two.astype(jnp.float32) * weight_scale  11.1 us

profile of v3, /device:TPU:32, one launch (start us, length us, event | category | flops | bytes accessed | tf_op | source)
XLA Modules:
  0.0 506.0 jit_solution(14634127456419938769)
XLA Ops:
  0.7 0.8 ne.37
  1.4 0.1 ne.39
  1.5 0.1 compare_convert_fusion
  1.6 1.3 broadcast_in_dim.8.bias_one
  2.9 1.3 broadcast_in_dim.9.bias_two
  4.2 0.7 convert_multiply_fusion
  4.9 0.1 constant_dynamic-slice_fusion
  4.9 0.7 stack_reshape.6
  5.7 0.7 stack_reshape.7
  6.4 0.6 pad.14.layer_keep
  7.1 0.1 copy.27
  7.2 0.8 broadcast_in_dim.20.keep
  7.9 1.2 fusion.2
  9.1 0.3 copy.26
  9.4 0.3 reshape_reshape.3
  9.7 0.8 fusion.source
  10.5 1.8 copy.28
  12.3 0.6 reshape.65
  12.9 0.9 pad.15.cotangent
  13.9 16.9 %prepare.1 = (bf16[416,1152]{1,0:T(8,128)(2,1)}, bf16[1152,1152]{1,0:T(8,128)(2,1)}, bf16[1152,1152]{1,0:T(8,128)(2,1)}, bf16[1152,1152]{1,0:T(8,128)(2,1)}, bf1...) custom-call(bf16[400,1150]{1,0:T(8,128)(2,1)} %w_one.1, ...), custom_call_target="tpu_custom_call" | custom-call | tf_op jit(solution)/shard_map/prepare/pallas_call | solution.py:924
  30.8 333.8 %relay.1 = (bf16[44,8,4096]{2,1,0:T(8,128)(2,1)}, bf16[44,8,1152]{2,1,0:T(8,128)(2,1)}, bf16[2,44,8,1152]{3,2,1,0:T(8,128)(2,1)}, f32[44,8,128]{2,1,0:T(8,128)}) custom-call(bf16[416,1152]{1,0:T(8,128)(2,1)} %get-tuple-element.20.w_one, bf16[1152,1152]{1,0:T(8,128)(2,1)} %get-tuple-element.21.r_one, bf16[1152,1152]{1,0:T(8,128)(2,1)} %get-tuple-element.22.r_two, ...), custom_call_target="tpu_custom_call" | custom-call | tf_op jit(solution)/shard_map/relay/pallas_call | solution.py:601
  364.6 0.0 copy-start
  364.6 1.5 fusion.1
  366.2 0.3 reshape.68
  366.5 0.3 constant_dynamic-slice_fusion.1
  366.8 0.8 copy.36
  367.6 0.0 copy-done
  367.6 0.7 fusion.3
  368.3 118.3 %reduce.5 = bf16[32,128,1152]{2,1,0:T(8,128)(2,1)} custom-call(bf16[352,4096]{1,0:T(8,128)(2,1)} %bitcast.28, bf16[2,352,1152]{2,1,0:T(8,128)(2,1)} %bitcast.30), custom_call_target="tpu_custom_call" | custom-call | tf_op jit(solution)/shard_map/reduce/pallas_call | solution.py:855
  486.6 1.4 fusion.5
  488.0 2.5 slice_convert_fusion.1
  490.5 4.5 slice_convert_fusion
  495.0 11.1 %multiply_multiply_fusion = (f32[1150,1150]{1,0:T(8,128)}, f32[1150,1150]{1,0:T(8,128)}) fusion(s32[1150,1150]{1,0:T(8,128)} %drop_two.1, bf16[4096,1152]{1,0:T(8,128)(2,1)} %bitcast.26, s32[1150,1150]{1,0:T(8,128)} %drop_one.1), kind=kLoop, calls=%fused_computation | loop fusion | flops 10580000 | bytes 26450000 | tf_op jit(solution)/shard_map/mul | solution.py:988
  (4 shorter events, 0.0 us)
Async XLA Ops:
  364.6 2.9 copy-start

commit v4 on v3

--- a/solution.py
+++ b/solution.py
@@ -24,6 +24,9 @@
 HP_ONE, SOURCE, U_TWO, HP_TWO = 0, 1152, 1792, 2944
 SOURCE_WIDE = 640
 SWITCH = 14
+BIG, SMALL = 96, 16
+THIRD = 32 * BIG
+SHARE = 32 * SMALL
 
 keep_scale = 4.0 / 3.0
 weight_scale = 2.0
@@ -54,9 +57,9 @@
 
 def relay_kernel(
     w_one, r_one, r_two, w_two, r_one_t, r_two_t, w_two_t, w_one_t,
-    source, keep, layer_keep, cotangent,
+    inputs, in_mask, mid_mask, out_mask, cotangent, resets,
     o_left, o_out, o_dz, o_dx,
-    w_front, w_back, w_in, zx, extra, dz, du, dx, hidden, cell, stage_a, stage_b, stage_z,
+    w_front, w_back, w_in, zx, extra, dz, du, dx, above, line, spread, keep, layer_keep, hidden, cell, stage_a, stage_b, stage_z,
     block_send, block_recv, block_local, cross_send, cross_recv, ring_send, ring_recv, go_on,
     u_send, u_recv, z_send, z_recv, dz_send, dz_recv, du_send, du_recv,
     bulk_send, bulk_recv, part_send, part_recv, dx_send, dx_recv, local_sem,
@@ -86,8 +89,6 @@
         for d in (1, -1):
             pl.semaphore_signal(barrier, inc=1, device_id=ring(d), device_id_type=MESH)
     pl.semaphore_wait(barrier, 11)
-
-    o_left[:, :, pl.ds(SOURCE, SOURCE_WIDE)] = source[...].reshape(CHUNKS, 2 * ROWS, SOURCE_WIDE)
 
     blocks = {
         W_ONE: w_one, R_ONE: r_one, R_TWO: r_two, W_TWO: w_two,
@@ -178,6 +179,8 @@
         for k in range(3):
             for slot, kind in enumerate(kinds):
                 cross_copy(kind, me, k, slot).start()
+            if k == 1:
+                start_blocks(FORWARD, me)
         for kind in SPREAD:
             if me // 2 == USER[kind] // 2:
                 block_copies(kind, me)[0].start()
@@ -191,8 +194,7 @@
             if me // 2 == USER[kind] // 2 and me != USER[kind]:
                 block_copies(kind, me)[0].wait_send()
 
-    def receive_spread(kind):
-        me = USER[kind]
+    def share_blocks(kind):
         others = from_other_plane(kind)
         for ring in range(2):
             for p in others:
@@ -204,6 +206,10 @@
                 for ring in range(2):
                     ring_arrival(p, ring, d, 0).wait_recv()
                     ring_copy(p, ring, d, 1).start()
+
+    def receive_rest(kind):
+        me = USER[kind]
+        others = from_other_plane(kind)
         for p in others:
             cross_copy(kind, p, 2, 0).wait_recv()
             for ring in range(2):
@@ -277,9 +283,10 @@
         return to(pipe_to, dz.at[gate, span], output.at[span], part_send.at[slot], part_recv.at[group])
 
     def copy_dx(pipe_to, group, slot):
-        span = pl.ds(group * GROUP, GROUP)
+        count = GROUP * 2 * ROWS
+        span = pl.ds(pl.multiple_of(group * count, count), count)
         return to(
-            pipe_to, dx.at[span, :, pl.ds(pipe_to * 128, 128)], o_dx.at[span], dx_send.at[slot], dx_recv.at[group]
+            pipe_to, dx.at[span, pl.ds(pipe_to * 128, 128)], o_dx.at[span], dx_send.at[slot], dx_recv.at[group]
         )
 
     def copy_bulk(pipe_to, ref, slot, which):
@@ -287,6 +294,52 @@
 
     def keep_rows(c, j):
         return jnp.broadcast_to(keep[c, ROWS * j : ROWS * j + ROWS, 0:1], (ROWS, WIDE))
+
+    def by_time(target, width, whole, value_of):
+        for start in range(0, whole, 128):
+            count = min(128, width - start)
+            if count < 128:
+                line[...] = jnp.zeros_like(line)
+            for i in range(ROWS):
+                value = value_of(i, slice(start, start + count))
+                if count < 128:
+                    line[:, :count] = value
+                    value = line[...]
+                spread[pl.ds(i, STEPS, stride=ROWS), :] = value
+            target[:, start : start + 128] = spread[...]
+
+    def set_up():
+        shape = (CHUNKS, 2 * ROWS, 128)
+        row = lax.broadcasted_iota(jnp.int32, shape, 1)
+        time = 2 * lax.broadcasted_iota(jnp.int32, shape, 0) + row // ROWS
+        stream = lax.rem(row, ROWS)
+        reset = jnp.zeros(shape, jnp.int32)
+        for i in range(ROWS):
+            reset = jnp.where(stream == i, resets[i // 2, i % 2], reset)
+        keep[...] = jnp.where(time == reset, 0.0, 1.0)
+        layer_keep[...] = jnp.zeros_like(layer_keep)
+        for i in range(ROWS):
+            h, s = i // 2, i % 2
+            for m, mask in enumerate((mid_mask, out_mask)):
+                layer_keep[m, i : i + 1, :HID] = mask[h, s : s + 1, :].astype(jnp.float32) * keep_scale
+
+        def masked(i, lanes):
+            h, s = i // 2, i % 2
+            kept = in_mask[h, s : s + 1, lanes].astype(jnp.float32) * keep_scale
+            return (inputs[h, s, :, lanes] * kept).astype(jnp.bfloat16).astype(jnp.float32)
+
+        by_time(dx, D_IN, 512, masked)
+        column = lax.broadcasted_iota(jnp.int32, (STEPS * ROWS, 512), 1)
+        value = jnp.where(column == D_IN, 1.0, dx[...])
+        dx[...] = value
+        o_left[:, :, pl.ds(SOURCE, 512)] = value.astype(jnp.bfloat16).reshape(CHUNKS, 2 * ROWS, 512)
+        o_left[:, :, pl.ds(SOURCE + 512, 128)] = jnp.zeros((CHUNKS, 2 * ROWS, 128), jnp.bfloat16)
+
+    def set_up_above():
+        def masked(i, lanes):
+            return cotangent[i // 2, i % 2, :, lanes].astype(jnp.float32) * layer_keep[1, i : i + 1, lanes]
+
+        by_time(above, HID, WIDE, masked)
 
     def clear():
         hidden[...] = jnp.zeros_like(hidden)
@@ -324,11 +377,10 @@
         o_hp[c] = stage_a[...].astype(jnp.bfloat16)
         o_layer[c] = stage_b[...].astype(jnp.bfloat16)
 
-    def backward_pair(c, mask, upstream):
-        above = upstream[c].astype(jnp.float32)
+    def backward_pair(c, upstream):
         for j in (1, 0):
             rows = pl.ds(ROWS * j, ROWS)
-            total = hidden[...] + above[ROWS * j : ROWS * j + ROWS] * mask
+            total = hidden[...] + upstream[ROWS * j : ROWS * j + ROWS]
             out_grad = total * zx[c, rows, pl.ds(3 * WIDE, WIDE)]
             cell_total = cell[...] + total * extra[c, rows, pl.ds(0, WIDE)]
             cell[...] = cell_total * extra[c, rows, pl.ds(WIDE, WIDE)]
@@ -349,11 +401,13 @@
     def _():
         me = LAYER_ONE
         start_spread(me)
-        start_blocks(FORWARD, me)
+        set_up()
+        share_blocks(R_ONE)
         await_blocks(W_ONE)
+        source = dx[:, :D_WIDE].astype(jnp.bfloat16)
         for g in range(4):
-            zx[:, :, pl.ds(g * WIDE, WIDE)] = dot(source[:, :D_WIDE], w_in[g]).reshape(CHUNKS, 2 * ROWS, WIDE)
-        receive_spread(R_ONE)
+            zx[:, :, pl.ds(g * WIDE, WIDE)] = dot(source, w_in[g]).reshape(CHUNKS, 2 * ROWS, WIDE)
+        receive_rest(R_ONE)
         clear()
 
         def ahead(c, carry):
@@ -387,7 +441,8 @@
         def behind(i, carry):
             c = last - i
             copy_du(c).wait_recv()
-            backward_pair(c, layer_keep[0], du)
+            mask = jnp.concatenate([layer_keep[0]] * 2, 0)
+            backward_pair(c, du[c].astype(jnp.float32) * mask)
             copy_dz(SOURCE_GRAD, c).start()
 
             @pl.when(lax.rem(c, GROUP) == 0)
@@ -421,8 +476,10 @@
     def _():
         me = LAYER_TWO
         start_spread(me)
-        start_blocks(FORWARD, me)
-        receive_spread(R_TWO)
+        set_up()
+        set_up_above()
+        share_blocks(R_TWO)
+        receive_rest(R_TWO)
         clear()
 
         def ahead(c, carry):
@@ -451,7 +508,7 @@
 
         def behind(i, carry):
             c = last - i
-            backward_pair(c, layer_keep[1], cotangent)
+            backward_pair(c, above[pl.ds(pl.multiple_of(c * 2 * ROWS, 2 * ROWS), 2 * ROWS), :])
             copy_dz(BETWEEN, c).start()
 
             @pl.when(lax.rem(c, GROUP) == 0)
@@ -485,8 +542,9 @@
     def _():
         me = BETWEEN
         start_spread(me)
-        start_blocks(FORWARD, me)
-        receive_spread(W_TWO)
+        set_up()
+        share_blocks(W_TWO)
+        receive_rest(W_TWO)
 
         def ahead(c, carry):
             copy_u(c).wait_recv()
@@ -539,7 +597,7 @@
     def _():
         me = SOURCE_GRAD
         start_spread(me)
-        start_blocks(FORWARD, me)
+        set_up()
 
         def pass_on(turn, carry):
             pl.semaphore_wait(go_on, 1)
@@ -557,7 +615,7 @@
             for g in range(4):
                 part = dot(dz[g, c], w_front[g, :, :512])
                 back = part if back is None else back + part
-            dx[c] = back
+            dx[pl.ds(pl.multiple_of(c * 2 * ROWS, 2 * ROWS), 2 * ROWS), :] = back
 
             @pl.when(lax.rem(c, GROUP) == 0)
             def _():
@@ -571,7 +629,7 @@
         lax.fori_loop(0, CHUNKS, behind, 0)
         own = pltpu.make_async_copy(dz.at[me], o_dz_one, local_sem.at[0])
         own.start()
-        own_dx = pltpu.make_async_copy(dx.at[:, :, pl.ds(me * 128, 128)], o_dx, local_sem.at[1])
+        own_dx = pltpu.make_async_copy(dx.at[:, pl.ds(me * 128, 128)], o_dx, local_sem.at[1])
         own_dx.start()
         finish_spread(me)
         finish_blocks(FORWARD + BACKWARD, me)
@@ -587,7 +645,7 @@
             copy_part(me, o_dz_two, group, 0, me).wait_recv()
 
 
-def relay(blocks, source, keep, layer_keep, cotangent):
+def relay(blocks, inputs, in_mask, mid_mask, out_mask, cotangent, resets):
     whole = pl.BlockSpec(memory_space=pltpu.VMEM)
     rows = (CHUNKS, 2 * ROWS, WIDE)
     half, full = jnp.bfloat16, jnp.float32
@@ -595,13 +653,14 @@
         jax.ShapeDtypeStruct((CHUNKS, 2 * ROWS, UNITS * UNIT), half),
         jax.ShapeDtypeStruct(rows, half),
         jax.ShapeDtypeStruct((2,) + rows, half),
-        jax.ShapeDtypeStruct((CHUNKS, 2 * ROWS, 128), full),
+        jax.ShapeDtypeStruct((STEPS * ROWS, 128), full),
     ]
     dma = pltpu.SemaphoreType.DMA
     return pl.pallas_call(
         relay_kernel,
         out_shape=shapes,
-        in_specs=[pl.BlockSpec(memory_space=pl.ANY)] * 8 + [whole] * 4,
+        in_specs=[pl.BlockSpec(memory_space=pl.ANY)] * 8 + [whole] * 5
+        + [pl.BlockSpec(memory_space=pltpu.SMEM)],
         out_specs=[whole] * 4,
         scratch_shapes=[
             pltpu.VMEM((4, WIDE, WIDE), half),
@@ -611,7 +670,12 @@
             pltpu.VMEM((CHUNKS, 2 * ROWS, 2 * WIDE), full),
             pltpu.VMEM((4,) + rows, half),
             pltpu.VMEM(rows, half),
-            pltpu.VMEM((CHUNKS, 2 * ROWS, 512), full),
+            pltpu.VMEM((STEPS * ROWS, 512), full),
+            pltpu.VMEM((STEPS * ROWS, WIDE), full),
+            pltpu.VMEM((STEPS, 128), full),
+            pltpu.VMEM((STEPS * ROWS, 128), full),
+            pltpu.VMEM((CHUNKS, 2 * ROWS, 128), full),
+            pltpu.VMEM((2, ROWS, WIDE), full),
             pltpu.VMEM((ROWS, WIDE), full),
             pltpu.VMEM((ROWS, WIDE), full),
             pltpu.VMEM((2 * ROWS, WIDE), full),
@@ -626,13 +690,13 @@
             vmem_limit_bytes=60 << 20, collective_id=0, has_side_effects=True
         ),
         name="relay",
-    )(*blocks, source, keep, layer_keep, cotangent)
+    )(*blocks, inputs, in_mask, mid_mask, out_mask, cotangent, resets)
 
 
 def reduce_kernel(
-    left, dz, total, own, near, far, part, cross,
+    left, dz, total, own, near, far, part, cross, share,
     near_send, near_recv, far_send, far_recv, part_send, part_recv, last_send, last_recv,
-    cross_send, cross_recv, back_send, back_recv, wide_send, wide_recv,
+    cross_send, cross_recv, back_send, back_recv, wide_send, wide_recv, share_send, share_recv,
 ):
     pipe = lax.axis_index("pipe")
     dp = lax.axis_index("dp")
@@ -641,209 +705,246 @@
     def device(z_, x_, y_):
         return {"pipe": pipe, "dp": z_ * 16 + lax.rem(x_ + 4, 4) * 4 + lax.rem(y_ + 4, 4)}
 
-    first = (lambda d: device(z, x + d, y), lambda d: device(z, x, y + d))
-    second = (lambda d: device(z, x, y + d), lambda d: device(z, x + d, y))
+    along_x, along_y = (lambda d: device(z, x + d, y)), (lambda d: device(z, x, y + d))
+    first, second = (along_x, along_y) * 2, (along_y, along_x) * 2
+    place = ((x, y), (y, x)) * 2
     across = device(1 - z, x, y)
-    place = ((x, y), (y, x))
+    size = (BIG, BIG, SMALL, SMALL)
+    base = (0, 16 * BIG, THIRD + z * SHARE, THIRD + z * SHARE + 16 * SMALL)
 
     barrier = pltpu.get_barrier_semaphore()
-    for target in (first[0](1), first[0](-1), first[1](1), first[1](-1), across):
+    for target in (along_x(1), along_x(-1), along_y(1), along_y(-1), across):
         pl.semaphore_signal(barrier, inc=1, device_id=target, device_id_type=MESH)
     pl.semaphore_wait(barrier, 5)
 
+    lanes_of = (pl.ds(0, WIDE), pl.ds(0, 640), pl.ds(640, 512))
+
     def unit(p, block, rel):
         a, b = place[p]
-        return p * 16 + lax.rem(a + block + 4, 4) * 4 + lax.rem(b + rel, 4)
+        index = lax.rem(a + block + 4, 4) * 4 + lax.rem(b + rel + 4, 4)
+        return pl.ds(pl.multiple_of(base[p] + index * size[p], 16), size[p])
 
     def send(source, target, s, r, to):
         return pltpu.make_async_remote_copy(source, target, s, r, device_id=to, device_id_type=MESH)
 
-    rows_of = (pl.ds(0, UNIT), pl.ds(0, HALF_UNIT), pl.ds(HALF_UNIT, HALF_UNIT))
-
-    def add(index, others, start=0, count=UNIT):
+    def add(target, rows, others, lanes=lanes_of[0]):
         def body(i, carry):
-            rows = pl.ds(pl.multiple_of(start + i * 16, 16), 16)
-            value = own[index, rows].astype(jnp.float32)
+            span = pl.ds(pl.multiple_of(rows.start + i * 16, 16), 16)
+            value = own[span, lanes].astype(jnp.float32)
             for ref in others:
-                value = value + ref[rows].astype(jnp.float32)
-            own[index, rows] = value.astype(jnp.bfloat16)
+                value = value + ref[pl.ds(pl.multiple_of(i * 16, 16), 16), lanes].astype(jnp.float32)
+            target[span, lanes] = value.astype(jnp.bfloat16)
             return carry
 
-        lax.fori_loop(0, count // 16, body, 0)
-
-    def product(p, block, rel):
-        u = unit(p, block, rel)
+        lax.fori_loop(0, rows.size // 16, body, 0)
+
+    def product(u):
         columns = pl.ds(pl.multiple_of(u * UNIT, UNIT), UNIT)
-        which = jnp.where(u < SWITCH, 0, 1)
-        own[u] = lax.dot_general(
-            left[:, columns], dz[which], (((0,), (0,)), ((), ())), preferred_element_type=jnp.float32
+        own[columns, :] = lax.dot_general(
+            left[:, columns], dz[jnp.where(u < SWITCH, 0, 1)], (((0,), (0,)), ((), ())),
+            preferred_element_type=jnp.float32,
         ).astype(jnp.bfloat16)
 
-    RIGHT, LEFT = (2, 1), (3, 0)
-    side = {1: RIGHT, -1: LEFT}
-    pairs = [(p, d) for d in (1, -1) for p in (0, 1)]
+    def products(start, count):
+        def body(i, carry):
+            product(start + i)
+            return carry
+
+        lax.fori_loop(0, count, body, 0)
+
+    block_units = 4 * BIG // UNIT
+
+    def block_products(p, block):
+        products(p * 4 * block_units + lax.rem(place[p][0] + block + 4, 4) * block_units, block_units)
+
+    side = {1: (2, 1), -1: (3, 0)}
+    on_side = {1: (0, 1), -1: (3, 2)}
     slot = {1: 0, -1: 1}
-
-    def near_copy(p, d, k):
-        rel = side[d][k]
-        return send(own.at[unit(p, 2, rel)], near.at[p, slot[d], k], near_send.at[p, slot[d], k],
-                    near_recv.at[p, slot[d], k], first[p](d))
-
-    def far_copy(p, d, k):
-        rel = (side[-d] + side[d])[k]
-        return send(own.at[unit(p, d, rel)], far.at[p, slot[d], rel], far_send.at[p, slot[d], k],
-                    far_recv.at[p, slot[d], rel], first[p](d))
-
-    def far_arrival(p, d, rel):
-        return send(own.at[unit(p, 0, rel)], far.at[p, slot[d], rel], far_send.at[p, slot[d], 0],
-                    far_recv.at[p, slot[d], rel], first[p](d))
-
     started = []
 
     def go(copy):
         copy.start()
         started.append(copy)
 
-    for k in range(2):
-        for p, d in pairs:
-            product(p, 2, side[d][k])
-            go(near_copy(p, d, k))
-    for k in range(2):
-        for p, d in pairs:
-            product(p, d, side[-d][k])
-            go(far_copy(p, d, k))
-    for k in range(2):
-        for p, d in pairs:
-            product(p, d, side[d][k])
-    for p in (0, 1):
-        for rel in range(4):
-            product(p, 0, rel)
-    for k in range(2):
-        for p, d in pairs:
-            near_copy(p, d, k).wait_recv()
-            add(unit(p, d, side[d][k]), [near.at[p, slot[d], k]])
-            go(far_copy(p, d, 2 + k))
+    def near_copy(p, d, k):
+        at = (p, slot[d], k)
+        return send(own.at[unit(p, 2, side[d][k])], near.at[at].at[pl.ds(0, size[p])], near_send.at[at],
+                    near_recv.at[at], first[p](d))
+
+    def far_copy(p, d, k, block=None):
+        rel = (side[-d] + side[d])[k]
+        at = (p, slot[d], rel)
+        return send(own.at[unit(p, d if block is None else block, rel)], far.at[at].at[pl.ds(0, size[p])],
+                    far_send.at[at], far_recv.at[at], first[p](d))
+
+    def part_copy(p, d):
+        lanes = lanes_of[1 if d == 1 else 2]
+        at = (p, slot[d])
+        return send(own.at[unit(p, 0, 2), lanes], part.at[at].at[pl.ds(0, size[p]), lanes], part_send.at[at],
+                    part_recv.at[at], second[p](d))
+
+    def last_copy(p, d, k):
+        lanes = lanes_of[(2 - k) if d == 1 else (1 + k)]
+        at = (p, slot[d], k)
+        return send(own.at[unit(p, 0, d), lanes], part.at[p, 2 + slot[d]].at[pl.ds(0, size[p]), lanes],
+                    last_send.at[at], last_recv.at[at], second[p](d))
+
+    def cross_copy(p):
+        return send(own.at[unit(p, 0, 0)], cross.at[p], cross_send.at[p], cross_recv.at[p], across)
+
+    def share_copy(i):
+        rows = pl.ds(pl.multiple_of(THIRD + (1 - z) * SHARE + i * UNIT, UNIT), UNIT)
+        return send(own.at[rows], share.at[pl.ds(i * UNIT, UNIT)], share_send.at[i], share_recv.at[i], across)
+
+    def share_back(half):
+        rows = pl.ds(pl.multiple_of(THIRD + half * SHARE, UNIT), SHARE)
+        return send(total.at[rows], total.at[rows], share_send.at[4], share_recv.at[4], across)
+
+    def back_copy(p, d, rel=0, on=0):
+        at = (p, slot[d], on)
+        ref = total.at[unit(p, 0, rel), lanes_of[0 if not on else 1 if d == 1 else 2]]
+        return send(ref, ref, back_send.at[at], back_recv.at[at], second[p](d))
+
+    def wide_copy(p, d, rel, block=0, on=0):
+        at = (p, slot[d], rel + 4 * on)
+        ref = total.at[unit(p, block, rel)]
+        return send(ref, ref, wide_send.at[at], wide_recv.at[at], first[p](d))
+
+    def start_near(parts):
+        for k in range(2):
+            for p in parts:
+                for d in (1, -1):
+                    go(near_copy(p, d, k))
+
+    def start_far(parts):
+        for k in range(2):
+            for p in parts:
+                for d in (1, -1):
+                    go(far_copy(p, d, k))
+
+    def finish_near(parts):
+        for k in range(2):
+            for p in parts:
+                for d in (1, -1):
+                    near_copy(p, d, k).wait_recv()
+                    add(own, unit(p, d, side[d][k]), [near.at[p, slot[d], k]])
+                    go(far_copy(p, d, 2 + k))
 
     def collect(p, rel):
         for d in (1, -1):
-            far_arrival(p, d, rel).wait_recv()
-        add(unit(p, 0, rel), [far.at[p, 0, rel], far.at[p, 1, rel]])
-
-    def part_copy(p, d):
-        rows = rows_of[1 if d == 1 else 2]
-        return send(own.at[unit(p, 0, 2), rows], part.at[p, slot[d], rows], part_send.at[p, slot[d]],
-                    part_recv.at[p, slot[d]], second[p](d))
-
-    def last_copy(p, d, k):
-        rel = 1 if d == 1 else 3
-        half = (2 - k) if d == 1 else (1 + k)
-        rows = rows_of[half]
-        return send(own.at[unit(p, 0, rel), rows], part.at[p, 2 + slot[d], rows], last_send.at[p, slot[d], k],
-                    last_recv.at[p, slot[d], k], second[p](d))
-
-    for p in (0, 1):
-        collect(p, 2)
+            far_copy(p, d, (side[-d] + side[d]).index(rel), 0).wait_recv()
+        add(own, unit(p, 0, rel), [far.at[p, 0, rel], far.at[p, 1, rel]])
+
+    def start_second(parts):
+        for p in parts:
+            collect(p, 2)
+            for d in (1, -1):
+                go(part_copy(p, d))
+        for rel, d in ((3, -1), (1, 1)):
+            for p in parts:
+                collect(p, rel)
+                go(last_copy(p, d, 0))
+        for p in parts:
+            collect(p, 0)
+
+    def finish_part(parts):
         for d in (1, -1):
-            go(part_copy(p, d))
-    for rel, d in ((3, -1), (1, 1)):
-        for p in (0, 1):
-            collect(p, rel)
-            go(last_copy(p, d, 0))
-    for p in (0, 1):
-        collect(p, 0)
+            for p in parts:
+                part_copy(p, d).wait_recv()
+                add(own, unit(p, 0, d), [part.at[p, slot[d]]], lanes_of[1 if d == 1 else 2])
+                go(last_copy(p, d, 1))
+
+    def finish_second(parts, target):
+        for p in parts:
+            for d in (1, -1):
+                for k in range(2):
+                    last_copy(p, d, k).wait_recv()
+            add(target, unit(p, 0, 0), [part.at[p, 2], part.at[p, 3]])
+
+    def start_back(parts):
+        for p in parts:
+            for d in (1, -1):
+                go(back_copy(p, d))
+            for d in (1, -1):
+                go(wide_copy(p, d, 0))
+
+    def pass_back(parts):
+        for d in (1, -1):
+            for p in parts:
+                back_copy(p, d, -d).wait_recv()
+                go(back_copy(p, d, -d, 1))
+                for e in (1, -1):
+                    go(wide_copy(p, e, -d % 4))
+
+    def finish_back(parts):
+        for p in parts:
+            for d in (1, -1):
+                back_copy(p, d, 2, 1).wait_recv()
+            for d in (1, -1):
+                go(wide_copy(p, d, 2))
+
+    def pass_wide(parts):
+        for k in range(2):
+            for d in (1, -1):
+                for p in parts:
+                    rel = on_side[d][k]
+                    wide_copy(p, d, rel, -d).wait_recv()
+                    go(wide_copy(p, d, rel, -d, 1))
+
+    def finish_wide(parts):
+        for p in parts:
+            for d in (1, -1):
+                for rel in range(4):
+                    if rel not in on_side[d]:
+                        wide_copy(p, d, rel, -d).wait_recv()
+                for rel in on_side[d]:
+                    wide_copy(p, d, rel, 2, 1).wait_recv()
+
+    big, small = (0, 1), (2, 3)
+    for p in big:
+        block_products(p, 2)
+    start_near(big)
+    for i in range(4):
+        product(THIRD // UNIT + (1 - z) * 4 + i)
+        go(share_copy(i))
     for d in (1, -1):
-        for p in (0, 1):
-            part_copy(p, d).wait_recv()
-            rel = 1 if d == 1 else 3
-            add(unit(p, 0, rel), [part.at[p, slot[d]]], 0 if d == 1 else HALF_UNIT, HALF_UNIT)
-            go(last_copy(p, d, 1))
-
-    def cross_copy(p):
-        return send(own.at[unit(p, 0, 0)], cross.at[p], cross_send.at[p], cross_recv.at[p], across)
-
-    for p in (0, 1):
-        for d in (1, -1):
-            for k in range(2):
-                last_copy(p, d, k).wait_recv()
-        add(unit(p, 0, 0), [part.at[p, 2], part.at[p, 3]])
+        for p in big:
+            block_products(p, d)
+    start_far(big)
+    for p in big:
+        block_products(p, 0)
+    products(THIRD // UNIT + z * 4, 4)
+    finish_near(big)
+    for i in range(4):
+        share_copy(i).wait_recv()
+        rows = pl.ds(pl.multiple_of(THIRD + z * SHARE + i * UNIT, UNIT), UNIT)
+        add(own, rows, [share.at[pl.ds(i * UNIT, UNIT)]])
+    start_near(small)
+    start_far(small)
+    start_second(big)
+    finish_near(small)
+    finish_part(big)
+    start_second(small)
+    finish_second(big, own)
+    for p in big:
         go(cross_copy(p))
-
-    def back_copy(p, d):
-        u = unit(p, 0, 0)
-        return send(total.at[u], total.at[u], back_send.at[p, slot[d], 0], back_recv.at[p, slot[d], 0], second[p](d))
-
-    def back_arrival(p, d):
-        u = unit(p, 0, -d % 4)
-        return send(total.at[u], total.at[u], back_send.at[p, slot[d], 0], back_recv.at[p, slot[d], 0], second[p](d))
-
-    def back_on(p, d):
-        u = unit(p, 0, -d % 4)
-        rows = rows_of[1 if d == 1 else 2]
-        return send(total.at[u, rows], total.at[u, rows], back_send.at[p, slot[d], 1], back_recv.at[p, slot[d], 1],
-                    second[p](d))
-
-    def back_on_arrival(p, d):
-        u = unit(p, 0, 2)
-        rows = rows_of[1 if d == 1 else 2]
-        return send(total.at[u, rows], total.at[u, rows], back_send.at[p, slot[d], 1], back_recv.at[p, slot[d], 1],
-                    second[p](d))
-
-    def wide_copy(p, d, rel):
-        u = unit(p, 0, rel)
-        return send(total.at[u], total.at[u], wide_send.at[p, slot[d], rel], wide_recv.at[p, slot[d], rel], first[p](d))
-
-    def wide_arrival(p, d, rel):
-        u = unit(p, -d % 4, rel)
-        return send(total.at[u], total.at[u], wide_send.at[p, slot[d], rel], wide_recv.at[p, slot[d], rel], first[p](d))
-
-    ON = {1: (0, 1), -1: (3, 2)}
-
-    def wide_on(p, d, k):
-        u = unit(p, -d % 4, ON[d][k])
-        return send(total.at[u], total.at[u], wide_send.at[p, slot[d], 4 + k], wide_recv.at[p, slot[d], 4 + k], first[p](d))
-
-    def wide_on_arrival(p, d, k):
-        u = unit(p, 2, ON[d][k])
-        return send(total.at[u], total.at[u], wide_send.at[p, slot[d], 4 + k], wide_recv.at[p, slot[d], 4 + k], first[p](d))
-
-    for p in (0, 1):
+    finish_part(small)
+    finish_second(small, total)
+    start_back(small)
+    pass_back(small)
+    for p in big:
         cross_copy(p).wait_recv()
-        u = unit(p, 0, 0)
-
-        def body(i, carry):
-            rows = pl.ds(pl.multiple_of(i * 16, 16), 16)
-            value = own[u, rows].astype(jnp.float32) + cross[p, rows].astype(jnp.float32)
-            total[u, rows] = value.astype(jnp.bfloat16)
-            return carry
-
-        lax.fori_loop(0, UNIT // 16, body, 0)
-        for d in (1, -1):
-            go(back_copy(p, d))
-        for d in (1, -1):
-            go(wide_copy(p, d, 0))
-    for d in (1, -1):
-        for p in (0, 1):
-            back_arrival(p, d).wait_recv()
-            go(back_on(p, d))
-            for e in (1, -1):
-                go(wide_copy(p, e, -d % 4))
-    for p in (0, 1):
-        for d in (1, -1):
-            back_on_arrival(p, d).wait_recv()
-        for d in (1, -1):
-            go(wide_copy(p, d, 2))
-    for k in range(2):
-        for d in (1, -1):
-            for p in (0, 1):
-                wide_arrival(p, d, ON[d][k]).wait_recv()
-                go(wide_on(p, d, k))
-    for p in (0, 1):
-        for d in (1, -1):
-            for rel in range(4):
-                if rel not in ON[d]:
-                    wide_arrival(p, d, rel).wait_recv()
-            for k in range(2):
-                wide_on_arrival(p, d, k).wait_recv()
+        add(total, unit(p, 0, 0), [cross.at[p]])
+    start_back(big)
+    finish_back(small)
+    pass_wide(small)
+    pass_back(big)
+    finish_wide(small)
+    go(share_back(z))
+    finish_back(big)
+    pass_wide(big)
+    finish_wide(big)
+    share_back(1 - z).wait_recv()
     for copy in started:
         copy.wait_send()
 
@@ -854,18 +955,19 @@
     dma = pltpu.SemaphoreType.DMA
     return pl.pallas_call(
         reduce_kernel,
-        out_shape=jax.ShapeDtypeStruct((UNITS, UNIT, WIDE), half),
+        out_shape=jax.ShapeDtypeStruct((UNITS * UNIT, WIDE), half),
         in_specs=[whole] * 2,
         out_specs=whole,
         scratch_shapes=[
-            pltpu.VMEM((UNITS, UNIT, WIDE), half),
-            pltpu.VMEM((2, 2, 2, UNIT, WIDE), half),
-            pltpu.VMEM((2, 2, 4, UNIT, WIDE), half),
-            pltpu.VMEM((2, 4, UNIT, WIDE), half),
-            pltpu.VMEM((2, UNIT, WIDE), half),
-            dma((2, 2, 2)), dma((2, 2, 2)), dma((2, 2, 4)), dma((2, 2, 4)), dma((2, 2)), dma((2, 2)),
-            dma((2, 2, 2)), dma((2, 2, 2)), dma((2,)), dma((2,)), dma((2, 2, 2)), dma((2, 2, 2)),
-            dma((2, 2, 6)), dma((2, 2, 6)),
+            pltpu.VMEM((UNITS * UNIT, WIDE), half),
+            pltpu.VMEM((4, 2, 2, BIG, WIDE), half),
+            pltpu.VMEM((4, 2, 4, BIG, WIDE), half),
+            pltpu.VMEM((4, 4, BIG, WIDE), half),
+            pltpu.VMEM((2, BIG, WIDE), half),
+            pltpu.VMEM((SHARE, WIDE), half),
+            dma((4, 2, 2)), dma((4, 2, 2)), dma((4, 2, 4)), dma((4, 2, 4)), dma((4, 2)), dma((4, 2)),
+            dma((4, 2, 2)), dma((4, 2, 2)), dma((2,)), dma((2,)), dma((4, 2, 2)), dma((4, 2, 2)),
+            dma((4, 2, 8)), dma((4, 2, 8)), dma((5,)), dma((5,)),
         ],
         compiler_params=pltpu.CompilerParams(
             vmem_limit_bytes=60 << 20, collective_id=1, has_side_effects=True
@@ -875,7 +977,7 @@
 
 
 def prepare_kernel(
-    w_one, bias_one, r_one, drop_one, w_two, bias_two, r_two, drop_two,
+    w_one, bias, r_one, drop_one, w_two, r_two, drop_two,
     o_w_one, o_r_one, o_r_two, o_w_two, o_r_one_t, o_r_two_t, o_w_two_t, o_w_one_t,
     square, small, apart,
 ):
@@ -897,13 +999,13 @@
         square[:HID, :] = weights[...].astype(jnp.float32) * drop[...].astype(jnp.float32) * weight_scale
         finish(o_plain, o_turned, WIDE)
     square[:HID, :] = w_two[...].astype(jnp.float32)
-    square[HID : HID + 1, :] = bias_two[...].astype(jnp.float32)
+    square[HID : HID + 1, :] = bias[1:2].astype(jnp.float32)
     finish(o_w_two, o_w_two_t, HID)
 
     w_one_f = w_one[...].astype(jnp.float32)
     small[...] = jnp.zeros_like(small)
     small[:D_IN, :] = w_one_f
-    small[D_IN : D_IN + 1, :] = bias_one[...].astype(jnp.float32)
+    small[D_IN : D_IN + 1, :] = bias[0:1].astype(jnp.float32)
     o_w_one[...] = jnp.where(inside[:D_WIDE], small[...], 0.0).astype(jnp.bfloat16)
     apart[...] = jnp.zeros_like(apart)
     for q in range(4):
@@ -911,7 +1013,7 @@
     o_w_one_t[...] = jnp.where(inside[:512], apart[...], 0.0).T.astype(jnp.bfloat16)
 
 
-def prepare(w_one, bias_one, r_one, drop_one, w_two, bias_two, r_two, drop_two):
+def prepare(w_one, bias, r_one, drop_one, w_two, r_two, drop_two):
     half = jnp.bfloat16
 
     def slab(rows):
@@ -924,7 +1026,7 @@
     return pl.pallas_call(
         prepare_kernel,
         grid=(WIDE // UNIT,),
-        in_specs=[slab(D_IN), slab(1), slab(HID), slab(HID), slab(HID), slab(1), slab(HID), slab(HID)],
+        in_specs=[slab(D_IN), slab(2), slab(HID), slab(HID), slab(HID), slab(HID), slab(HID)],
         out_specs=[slab(D_WIDE)] + [slab(WIDE)] * 3 + [turned(WIDE)] * 3 + [turned(512)],
         out_shape=[jax.ShapeDtypeStruct((D_WIDE, WIDE), half)] + [square] * 6
         + [jax.ShapeDtypeStruct((WIDE, 512), half)],
@@ -934,16 +1036,53 @@
         ],
         compiler_params=pltpu.CompilerParams(vmem_limit_bytes=60 << 20),
         name="prepare",
-    )(w_one, bias_one[None], r_one, drop_one, w_two, bias_two[None], r_two, drop_two)
-
-
-def padded(array, rows, columns):
-    return jnp.pad(array, ((0, rows - array.shape[0]), (0, columns - array.shape[1])))
-
-
-def by_time(array):
-    ordered = jnp.transpose(array, (2, 0, 1, 3))
-    return ordered.reshape(CHUNKS, 2 * ROWS, array.shape[3])
+    )(w_one, bias, r_one, drop_one, w_two, r_two, drop_two)
+
+
+def finish_kernel(
+    hp_one, source, u_two, hp_two, drop_one, drop_two, o_in_one, o_rec_one, o_bias_one, o_in_two, o_rec_two, o_bias_two
+):
+    step = pl.program_id(0)
+
+    def wide(ref):
+        return ref[:, :HID].astype(jnp.float32)
+
+    o_rec_one[...] = wide(hp_one) * drop_one[...].astype(jnp.float32) * weight_scale
+    o_rec_two[...] = wide(hp_two) * drop_two[...].astype(jnp.float32) * weight_scale
+    o_in_one[...] = wide(source)
+    o_in_two[...] = wide(u_two)
+
+    @pl.when(step == D_IN // UNIT)
+    def _():
+        o_bias_one[...] = wide(source)[D_IN % UNIT : D_IN % UNIT + 1]
+
+    @pl.when(step == HID // UNIT)
+    def _():
+        o_bias_two[...] = wide(u_two)[HID % UNIT : HID % UNIT + 1]
+
+
+def finish(total, drop_one, drop_two):
+    def units(first, last):
+        return pl.BlockSpec((UNIT, WIDE), lambda i: (first + jnp.minimum(i, last), 0))
+
+    def rows(last):
+        return pl.BlockSpec((UNIT, HID), lambda i: (jnp.minimum(i, last), 0))
+
+    one = pl.BlockSpec((1, HID), lambda i: (0, 0))
+    count, short = WIDE // UNIT, D_IN // UNIT
+    square, line = jax.ShapeDtypeStruct((HID, HID), jnp.float32), jax.ShapeDtypeStruct((1, HID), jnp.float32)
+    return pl.pallas_call(
+        finish_kernel,
+        grid=(count,),
+        in_specs=[
+            units(HP_ONE // UNIT, count), units(SOURCE // UNIT, short), units(U_TWO // UNIT, count),
+            units(HP_TWO // UNIT, count), rows(count), rows(count),
+        ],
+        out_specs=[rows(short), rows(count), one, rows(count), rows(count), one],
+        out_shape=[jax.ShapeDtypeStruct((D_IN, HID), jnp.float32), square, line, square, square, line],
+        compiler_params=pltpu.CompilerParams(vmem_limit_bytes=60 << 20),
+        name="finish",
+    )(total, total, total, total, drop_one, drop_two)
 
 
 def local(
@@ -951,43 +1090,23 @@
     w_ih_one, w_hh_one, bias_one, drop_one, w_ih_two, w_hh_two, bias_two, drop_two, cotangent,
 ):
     pipe = lax.axis_index("pipe")
-    blocks = prepare(w_ih_one, bias_one, w_hh_one, drop_one, w_ih_two, bias_two, w_hh_two, drop_two)
-    keep_in = in_mask.astype(jnp.float32) * keep_scale
-    source = by_time((inputs * keep_in[:, :, None, :]).astype(jnp.bfloat16)).reshape(STEPS * ROWS, D_IN)
-    ones = jnp.ones((STEPS * ROWS, 1), jnp.bfloat16)
-    source = padded(jnp.concatenate([source, ones], 1), STEPS * ROWS, SOURCE_WIDE)
-    positions = jnp.arange(STEPS, dtype=jnp.int32)
-    keep = (resets.reshape(1, ROWS) != positions[:, None]).astype(jnp.float32)
-    keep = jnp.broadcast_to(keep.reshape(CHUNKS, 2 * ROWS, 1), (CHUNKS, 2 * ROWS, 128))
-    layer_keep = jnp.stack([mid_mask.reshape(ROWS, HID), out_mask.reshape(ROWS, HID)]).astype(jnp.float32)
-    layer_keep = jnp.pad(layer_keep * keep_scale, ((0, 0), (0, 0), (0, WIDE - HID)))
-    cot = jnp.pad(by_time(cotangent), ((0, 0), (0, 0), (0, WIDE - HID)))
-
-    left, out_two, dz, dx = relay(blocks, source, keep, layer_keep, cot)
+    bias = jnp.stack([bias_one, bias_two])
+    blocks = prepare(w_ih_one, bias, w_hh_one, drop_one, w_ih_two, w_hh_two, drop_two)
+    left, out_two, dz, dx = relay(blocks, inputs, in_mask, mid_mask, out_mask, cotangent, resets)
     left = left.reshape(STEPS * ROWS, UNITS * UNIT)
-    total = reduce_over_dp(left, dz.reshape(2, STEPS * ROWS, WIDE)).reshape(UNITS * UNIT, WIDE)
+    total = reduce_over_dp(left, dz.reshape(2, STEPS * ROWS, WIDE))
 
     u_two = left[:, U_TWO : U_TWO + WIDE].reshape(out_two.shape)
     layer = jnp.where(pipe < 2, u_two, out_two).reshape(STEPS, 2, 2, WIDE)[..., :HID]
     layer = lax.dynamic_index_in_dim(layer, pipe % 2, 1, keepdims=False)
     layer_outputs = jnp.swapaxes(layer, 0, 1)[None]
     grad_input = jnp.transpose(dx.reshape(STEPS, 2, 2, 128)[..., :100], (1, 2, 0, 3))
+    keep_in = in_mask.astype(jnp.float32) * keep_scale
     keep_part = lax.dynamic_slice_in_dim(keep_in, pipe * 100, 100, 2)
     grad_input = grad_input * keep_part[:, :, None, :]
 
-    def grads(start, rows):
-        return total[start : start + rows, :HID].astype(jnp.float32)
-
-    return (
-        layer_outputs,
-        grad_input,
-        grads(SOURCE, D_IN),
-        grads(HP_ONE, HID) * drop_one.astype(jnp.float32) * weight_scale,
-        grads(SOURCE + D_IN, 1)[0],
-        grads(U_TWO, HID),
-        grads(HP_TWO, HID) * drop_two.astype(jnp.float32) * weight_scale,
-        grads(U_TWO + HID, 1)[0],
-    )
+    in_one, rec_one, bias_one, in_two, rec_two, bias_two = finish(total, drop_one, drop_two)
+    return (layer_outputs, grad_input, in_one, rec_one, bias_one[0], in_two, rec_two, bias_two[0])
 
 
 def solution(mesh):

time: 507 us -> 475 us (0.937)
  other arithmetic: 24.5 us -> 6.2 us
  local copies, waits for them, and re-layouts: 11.8 us -> 2.78 us
    mul x2 -> x0, other arithmetic: 11.1 us -> none  [the longest x1 11.1 us: local(): grads(HP_TWO, HID) * drop_two.astype(jnp.float32) * weight_scale]
    pallas_call x1, Pallas kernels: 334 us -> 323 us  [relay(): pl.pallas_call(relay_kernel, out_shape=shapes, in_specs=[pl.BlockSpec(mem...]
    convert_element_type x3 -> x0, other arithmetic: 7.07 us -> none  [the longest x2 7 us: grads(): return total[start:start + rows, :HID].astype(jnp.float32)]
    pallas_call x1 -> x2, Pallas kernels: 118 us -> 124 us  [the longest x1 108 us: reduce_over_dp(): pl.pallas_call(reduce_kernel, out_shape=jax.ShapeDtypeStruct((UNITS * UNI...]
where the time goes in v4:
time: 475 us; the launch traced here: 474 us
  Pallas kernels  465 us (98%)
  other arithmetic  6.2 us (1%)
    pallas_call x1, Pallas kernels, relay(): pl.pallas_call(relay_kernel, out_shape=shapes, in_specs=[pl.BlockSpec(mem...  323 us
    pallas_call x1, Pallas kernels, reduce_over_dp(): pl.pallas_call(reduce_kernel, out_shape=jax.ShapeDtypeStruct((UNITS * UNI...  108 us
    pallas_call x1, Pallas kernels, prepare(): pl.pallas_call(prepare_kernel, grid=(WIDE // UNIT,), in_specs=[slab(D_IN)...  17.2 us
    pallas_call x1, Pallas kernels, finish(): pl.pallas_call(finish_kernel, grid=(count,), in_specs=[units(HP_ONE // UN...  16.4 us

profile of v4, /device:TPU:32, one launch (start us, length us, event | category | flops | bytes accessed | tf_op | source)
XLA Modules:
  0.0 474.3 jit_solution(2960138879445011240)
XLA Ops:
  0.7 0.8 fusion.2
  1.4 0.7 stack.9
  2.1 0.7 stack.10
  2.8 0.6 pad_maximum_fusion.bias
  3.4 17.2 %prepare.1 = (bf16[416,1152]{1,0:T(8,128)(2,1)}, bf16[1152,1152]{1,0:T(8,128)(2,1)}, bf16[1152,1152]{1,0:T(8,128)(2,1)}, bf16[1152,1152]{1,0:T(8,128)(2,1)}, bf1...) custom-call(bf16[400,1150]{1,0:T(8,128)(2,1)} %w_one.1, ...), custom_call_target="tpu_custom_call" | custom-call | tf_op jit(solution)/shard_map/prepare/pallas_call | solution.py:1026
  20.6 323.2 %relay.1 = (bf16[44,8,4096]{2,1,0:T(8,128)(2,1)}, bf16[44,8,1152]{2,1,0:T(8,128)(2,1)}, bf16[2,44,8,1152]{3,2,1,0:T(8,128)(2,1)}, f32[352,128]{1,0:T(8,128)}) custom-call(bf16[416,1152]{1,0:T(8,128)(2,1)} %get-tuple-element.26.w_one, bf16[1152,1152]{1,0:T(8,128)(2,1)} %get-tuple-element.27.r_one, bf16[1152,1152]{1,0:T(8,128)(2,1)} %get-tuple-element.28.r_two, ...), custom_call_target="tpu_custom_call" | custom-call | tf_op jit(solution)/shard_map/relay/pallas_call | solution.py:659
  343.8 0.0 copy-start
  343.8 1.5 fusion
  345.4 0.3 reshape.34
  345.7 0.3 constant_dynamic-slice_fusion
  346.0 0.8 copy.29
  346.8 0.0 copy-done
  346.8 0.7 fusion.1
  347.5 107.8 %reduce.3.hp_one.source.u_two.hp_two = bf16[4096,1152]{1,0:T(8,128)(2,1)} custom-call(bf16[352,4096]{1,0:T(8,128)(2,1)} %bitcast.19, bf16[2,352,1152]{2,1,0:T(8,128)(2,1)} %bitcast.21), custom_call_target="tpu_custom_call" | custom-call | tf_op jit(solution)/shard_map/reduce/pallas_call | solution.py:956
  455.3 16.4 %finish.1 = (f32[400,1150]{1,0:T(8,128)}, f32[1150,1150]{1,0:T(8,128)}, f32[1,1150]{1,0:T(1,128)}, f32[1150,1150]{1,0:T(8,128)}, f32[1150,1150]{1,0:T(8,128)}, /*index=5*/f32[1,1150]{1,0:T(1,128)}) custom-call(bf16[4096,1152]{1,0:T(8,128)(2,1)} %reduce.3.hp_one.source.u_two.hp_two, bf16[4096,1152]{1,0:T(8,128)(2,1)} %reduce.3.hp_one.source.u_two.hp_two, ...), custom_call_target="tpu_custom_call" | custom-call | tf_op jit(solution)/shard_map/finish/pallas_call | solution.py:1074
  471.6 1.3 reduce.1
  473.0 1.3 reduce.2
Async XLA Ops:
  343.8 2.9 copy-start

commit v5 on v4

--- a/solution.py
+++ b/solution.py
@@ -21,9 +21,10 @@
 UNIT = 128
 HALF_UNIT = 64
 UNITS = 32
-HP_ONE, SOURCE, U_TWO, HP_TWO = 0, 1152, 1792, 2944
+HP_ONE, U_TWO, HP_TWO, SOURCE = 0, 1152, 2304, 3456
 SOURCE_WIDE = 640
-SWITCH = 14
+SLAB = 384
+DEEP = 4
 BIG, SMALL = 96, 16
 THIRD = 32 * BIG
 SHARE = 32 * SMALL
@@ -56,10 +57,11 @@
 
 
 def relay_kernel(
-    w_one, r_one, r_two, w_two, r_one_t, r_two_t, w_two_t, w_one_t,
+    w_one, bias, tails, r_one, drop_one, r_two, drop_two, w_two,
     inputs, in_mask, mid_mask, out_mask, cotangent, resets,
-    o_left, o_out, o_dz, o_dx,
-    w_front, w_back, w_in, zx, extra, dz, du, dx, above, line, spread, keep, layer_keep, hidden, cell, stage_a, stage_b, stage_z,
+    o_left, o_out, o_dz, o_dx, turned, turned_in,
+    raw_weights, raw_drop, raw_sem, plain, plain_in, turn, small, apart, turn_sem,
+    w_front, w_back, zx, extra, dz, du, dx, above, line, spread, keep, layer_keep, hidden, cell, stage_a, stage_b, stage_z,
     block_send, block_recv, block_local, cross_send, cross_recv, ring_send, ring_recv, go_on,
     u_send, u_recv, z_send, z_recv, dz_send, dz_recv, du_send, du_recv,
     bulk_send, bulk_recv, part_send, part_recv, dx_send, dx_recv, local_sem,
@@ -88,16 +90,114 @@
     for ring in rings:
         for d in (1, -1):
             pl.semaphore_signal(barrier, inc=1, device_id=ring(d), device_id_type=MESH)
+
+    def make_plain(m, also=None):
+        weights, drop = ((r_one, drop_one), (r_two, drop_two), (w_two, None))[m]
+        plain[m, :, pl.ds(HID // UNIT * UNIT, UNIT)] = jnp.zeros((WIDE, UNIT), jnp.bfloat16)
+
+        def copies(i):
+            slot = lax.rem(i, DEEP)
+            span = pl.ds(pl.multiple_of(i * UNIT, UNIT), UNIT)
+            return [
+                pltpu.make_async_copy(array.at[span], raw.at[slot], raw_sem.at[k, slot])
+                for k, (array, raw) in enumerate(((weights, raw_weights), (drop, raw_drop)))
+                if array is not None
+            ]
+
+        def start(i):
+            for copy in copies(i):
+                copy.start()
+
+        whole = HID // UNIT
+
+        def body(i, carry):
+            for copy in copies(i):
+                copy.wait()
+            slot = lax.rem(i, DEEP)
+            value = raw_weights[slot]
+            if drop is not None:
+                value = value.astype(jnp.float32) * raw_drop[slot].astype(jnp.float32) * weight_scale
+            plain[m, pl.ds(pl.multiple_of(i * UNIT, UNIT), UNIT), pl.ds(0, HID)] = value.astype(jnp.bfloat16)
+            pl.when(i + DEEP < whole)(lambda: start(i + DEEP))
+            if also is not None:
+                also(i)
+            return carry
+
+        for i in range(DEEP):
+            start(i)
+        plain[m, pl.ds(whole * UNIT, UNIT)] = tails[m]
+        lax.fori_loop(0, whole, body, 0)
+        if also is not None:
+            also(whole)
+
+    def turn_copy(m, i, slot):
+        rows = pl.ds(pl.multiple_of(i * UNIT, UNIT), UNIT)
+        return pltpu.make_async_copy(turn.at[slot], turned.at[m, rows], turn_sem.at[slot])
+
+    def make_turned(m, order, i):
+        slot = lax.rem(order * (WIDE // UNIT) + i, 2)
+        if order:
+            turn_copy(m, i, slot).wait()
+        else:
+            pl.when(i >= 2)(lambda: turn_copy(m, i, slot).wait())
+        value = plain[m, :, pl.ds(pl.multiple_of(i * UNIT, UNIT), UNIT)].astype(jnp.float32).T
+        column = lax.broadcasted_iota(jnp.int32, (UNIT, WIDE), 1)
+        turn[slot] = jnp.where(column < HID, value, 0.0).astype(jnp.bfloat16)
+        turn_copy(m, i, slot).start()
+
+    def turn_in_copy(i):
+        slot = lax.rem(i, 2)
+        rows = pl.ds(pl.multiple_of(i * UNIT, UNIT), UNIT)
+        return pltpu.make_async_copy(turn.at[slot, :, pl.ds(0, 512)], turned_in.at[rows], turn_sem.at[slot])
+
+    def make_plain_in():
+        plain_in[...] = jnp.zeros_like(plain_in)
+        plain_in[:D_IN, :HID] = w_one[...]
+        row = lax.broadcasted_iota(jnp.int32, (D_WIDE - D_IN, HID), 0)
+        below = jnp.where(row == 0, bias[0:1].astype(jnp.float32), 0.0)
+        plain_in[D_IN:, :HID] = below.astype(jnp.bfloat16)
+
+    def make_turned_in(i, carry):
+        small[...] = plain_in[:D_IN, pl.ds(pl.multiple_of(i * UNIT, UNIT), UNIT)].astype(jnp.float32)
+        for q in range(4):
+            apart[q * UNIT : q * UNIT + 100, :] = small[q * 100 : q * 100 + 100, :]
+        pl.when(i >= 2)(lambda: turn_in_copy(i).wait())
+        turn[lax.rem(i, 2), :, pl.ds(0, 512)] = apart[...].T.astype(jnp.bfloat16)
+        turn_in_copy(i).start()
+        return carry
+
+    def finish_turned(m, order):
+        def body(i, carry):
+            make_turned(m, order, i)
+            return carry
+
+        lax.fori_loop(0, WIDE // UNIT, body, 0)
+        for slot in range(2):
+            turn_copy(m, 0, slot).wait()
+        apart[...] = jnp.zeros_like(apart)
+        lax.fori_loop(0, WIDE // UNIT, make_turned_in, 0)
+        for i in range(2):
+            turn_in_copy(i).wait()
+
+    @pl.when(pipe >= 2)
+    def _():
+        make_plain(0)
+
+    @pl.when(pipe < 2)
+    def _():
+        make_plain(2)
+
+    make_plain_in()
     pl.semaphore_wait(barrier, 11)
 
     blocks = {
-        W_ONE: w_one, R_ONE: r_one, R_TWO: r_two, W_TWO: w_two,
-        R_ONE_T: r_one_t, R_TWO_T: r_two_t, W_TWO_T: w_two_t, W_ONE_T: w_one_t,
+        W_ONE: plain_in, R_ONE: plain.at[0], R_TWO: plain.at[1], W_TWO: plain.at[2],
+        R_ONE_T: turned.at[0], R_TWO_T: turned.at[1], W_TWO_T: turned.at[2], W_ONE_T: turned_in,
     }
 
     def landing(kind, p):
         if kind == W_ONE:
-            return w_in.at[p]
+            return w_back.at[p, pl.ds(0, D_WIDE)]
         if kind in (R_ONE, R_TWO, W_TWO):
             return w_front.at[p]
         if kind == W_ONE_T:
@@ -174,20 +274,36 @@
 
     SPREAD = (W_TWO, R_TWO, R_ONE)
 
+    def start_cross(me, kind, ks):
+        slot = (R_TWO, W_TWO, R_ONE).index(kind) % 2
+        for k in ks:
+            cross_copy(kind, me, k, slot).start()
+
     def start_spread(me):
-        kinds = [kind for kind in SPREAD if me // 2 != USER[kind] // 2]
-        for k in range(3):
-            for slot, kind in enumerate(kinds):
-                cross_copy(kind, me, k, slot).start()
-            if k == 1:
-                start_blocks(FORWARD, me)
-        for kind in SPREAD:
-            if me // 2 == USER[kind] // 2:
-                block_copies(kind, me)[0].start()
+        if me // 2 == 1:
+            start_cross(me, R_ONE, (0, 1))
+            start_blocks(FORWARD, me)
+            start_cross(me, R_ONE, (2,))
+            make_plain(2, functools.partial(make_turned, 0, 0))
+            block_copies(W_TWO, me)[0].start()
+            make_plain(1, functools.partial(make_turned, 2, 1))
+            block_copies(R_TWO, me)[0].start()
+            finish_turned(1, 2)
+        else:
+            start_cross(me, W_TWO, (0, 1))
+            start_blocks(FORWARD, me)
+            make_plain(1, functools.partial(make_turned, 2, 0))
+            start_cross(me, R_TWO, (0, 1))
+            start_cross(me, W_TWO, (2,))
+            start_cross(me, R_TWO, (2,))
+            make_plain(0, functools.partial(make_turned, 1, 1))
+            block_copies(R_ONE, me)[0].start()
+            finish_turned(0, 2)
 
     def finish_spread(me):
         kinds = [kind for kind in SPREAD if me // 2 != USER[kind] // 2]
-        for slot, kind in enumerate(kinds):
+        for kind in kinds:
+            slot = (R_TWO, W_TWO, R_ONE).index(kind) % 2
             for k in range(3):
                 cross_copy(kind, me, k, slot).wait_send()
         for kind in SPREAD:
@@ -406,7 +522,7 @@
         await_blocks(W_ONE)
         source = dx[:, :D_WIDE].astype(jnp.bfloat16)
         for g in range(4):
-            zx[:, :, pl.ds(g * WIDE, WIDE)] = dot(source, w_in[g]).reshape(CHUNKS, 2 * ROWS, WIDE)
+            zx[:, :, pl.ds(g * WIDE, WIDE)] = dot(source, w_back[g, :D_WIDE]).reshape(CHUNKS, 2 * ROWS, WIDE)
         receive_rest(R_ONE)
         clear()
 
@@ -645,8 +761,8 @@
             copy_part(me, o_dz_two, group, 0, me).wait_recv()
 
 
-def relay(blocks, inputs, in_mask, mid_mask, out_mask, cotangent, resets):
-    whole = pl.BlockSpec(memory_space=pltpu.VMEM)
+def relay(w_one, bias, tails, r_one, drop_one, r_two, drop_two, w_two, inputs, in_mask, mid_mask, out_mask, cotangent, resets):
+    whole, away = pl.BlockSpec(memory_space=pltpu.VMEM), pl.BlockSpec(memory_space=pl.ANY)
     rows = (CHUNKS, 2 * ROWS, WIDE)
     half, full = jnp.bfloat16, jnp.float32
     shapes = [
@@ -654,18 +770,28 @@
         jax.ShapeDtypeStruct(rows, half),
         jax.ShapeDtypeStruct((2,) + rows, half),
         jax.ShapeDtypeStruct((STEPS * ROWS, 128), full),
+        jax.ShapeDtypeStruct((3, WIDE, WIDE), half),
+        jax.ShapeDtypeStruct((WIDE, 512), half),
     ]
     dma = pltpu.SemaphoreType.DMA
     return pl.pallas_call(
         relay_kernel,
         out_shape=shapes,
-        in_specs=[pl.BlockSpec(memory_space=pl.ANY)] * 8 + [whole] * 5
+        in_specs=[whole] * 3 + [away] * 5 + [whole] * 5
         + [pl.BlockSpec(memory_space=pltpu.SMEM)],
-        out_specs=[whole] * 4,
+        out_specs=[whole] * 4 + [away] * 2,
         scratch_shapes=[
+            pltpu.VMEM((DEEP, UNIT, HID), half),
+            pltpu.VMEM((DEEP, UNIT, HID), jnp.int32),
+            dma((2, DEEP)),
+            pltpu.VMEM((3, WIDE, WIDE), half),
+            pltpu.VMEM((D_WIDE, WIDE), half),
+            pltpu.VMEM((2, UNIT, WIDE), half),
+            pltpu.VMEM((D_IN, UNIT), full),
+            pltpu.VMEM((512, UNIT), full),
+            dma((2,)),
             pltpu.VMEM((4, WIDE, WIDE), half),
             pltpu.VMEM((4, WIDE, WIDE), half),
-            pltpu.VMEM((4, D_WIDE, WIDE), half),
             pltpu.VMEM((CHUNKS, 2 * ROWS, 4 * WIDE), full),
             pltpu.VMEM((CHUNKS, 2 * ROWS, 2 * WIDE), full),
             pltpu.VMEM((4,) + rows, half),
@@ -690,7 +816,7 @@
             vmem_limit_bytes=60 << 20, collective_id=0, has_side_effects=True
         ),
         name="relay",
-    )(*blocks, inputs, in_mask, mid_mask, out_mask, cotangent, resets)
+    )(w_one, bias, tails, r_one, drop_one, r_two, drop_two, w_two, inputs, in_mask, mid_mask, out_mask, cotangent, resets)
 
 
 def reduce_kernel(
@@ -741,7 +867,7 @@
     def product(u):
         columns = pl.ds(pl.multiple_of(u * UNIT, UNIT), UNIT)
         own[columns, :] = lax.dot_general(
-            left[:, columns], dz[jnp.where(u < SWITCH, 0, 1)], (((0,), (0,)), ((), ())),
+            left[:, columns], dz[jnp.where((u >= U_TWO // UNIT) & (u < SOURCE // UNIT), 1, 0)], (((0,), (0,)), ((), ())),
             preferred_element_type=jnp.float32,
         ).astype(jnp.bfloat16)
 
@@ -976,69 +1102,6 @@
     )(left, dz)
 
 
-def prepare_kernel(
-    w_one, bias, r_one, drop_one, w_two, r_two, drop_two,
-    o_w_one, o_r_one, o_r_two, o_w_two, o_r_one_t, o_r_two_t, o_w_two_t, o_w_one_t,
-    square, small, apart,
-):
-    column = pl.program_id(0) * UNIT + lax.broadcasted_iota(jnp.int32, (WIDE, UNIT), 1)
-    inside = column < HID
-
-    def finish(o_plain, o_turned, turned_rows):
-        value = jnp.where(inside, square[...], 0.0)
-        o_plain[...] = value.astype(jnp.bfloat16)
-        row = lax.broadcasted_iota(jnp.int32, (WIDE, UNIT), 0)
-        if turned_rows < WIDE:
-            value = jnp.where(row < turned_rows, value, 0.0)
-        o_turned[...] = value.T.astype(jnp.bfloat16)
-
-    square[...] = jnp.zeros_like(square)
-    for weights, drop, o_plain, o_turned in (
-        (r_one, drop_one, o_r_one, o_r_one_t), (r_two, drop_two, o_r_two, o_r_two_t),
-    ):
-        square[:HID, :] = weights[...].astype(jnp.float32) * drop[...].astype(jnp.float32) * weight_scale
-        finish(o_plain, o_turned, WIDE)
-    square[:HID, :] = w_two[...].astype(jnp.float32)
-    square[HID : HID + 1, :] = bias[1:2].astype(jnp.float32)
-    finish(o_w_two, o_w_two_t, HID)
-
-    w_one_f = w_one[...].astype(jnp.float32)
-    small[...] = jnp.zeros_like(small)
-    small[:D_IN, :] = w_one_f
-    small[D_IN : D_IN + 1, :] = bias[0:1].astype(jnp.float32)
-    o_w_one[...] = jnp.where(inside[:D_WIDE], small[...], 0.0).astype(jnp.bfloat16)
-    apart[...] = jnp.zeros_like(apart)
-    for q in range(4):
-        apart[q * UNIT : q * UNIT + 100, :] = small[q * 100 : q * 100 + 100, :]
-    o_w_one_t[...] = jnp.where(inside[:512], apart[...], 0.0).T.astype(jnp.bfloat16)
-
-
-def prepare(w_one, bias, r_one, drop_one, w_two, r_two, drop_two):
-    half = jnp.bfloat16
-
-    def slab(rows):
-        return pl.BlockSpec((rows, UNIT), lambda j: (0, j))
-
-    def turned(columns):
-        return pl.BlockSpec((UNIT, columns), lambda j: (j, 0))
-
-    square = jax.ShapeDtypeStruct((WIDE, WIDE), half)
-    return pl.pallas_call(
-        prepare_kernel,
-        grid=(WIDE // UNIT,),
-        in_specs=[slab(D_IN), slab(2), slab(HID), slab(HID), slab(HID), slab(HID), slab(HID)],
-        out_specs=[slab(D_WIDE)] + [slab(WIDE)] * 3 + [turned(WIDE)] * 3 + [turned(512)],
-        out_shape=[jax.ShapeDtypeStruct((D_WIDE, WIDE), half)] + [square] * 6
-        + [jax.ShapeDtypeStruct((WIDE, 512), half)],
-        scratch_shapes=[
-            pltpu.VMEM((WIDE, UNIT), jnp.float32), pltpu.VMEM((D_WIDE, UNIT), jnp.float32),
-            pltpu.VMEM((512, UNIT), jnp.float32),
-        ],
-        compiler_params=pltpu.CompilerParams(vmem_limit_bytes=60 << 20),
-        name="prepare",
-    )(w_one, bias, r_one, drop_one, w_two, r_two, drop_two)
-
-
 def finish_kernel(
     hp_one, source, u_two, hp_two, drop_one, drop_two, o_in_one, o_rec_one, o_bias_one, o_in_two, o_rec_two, o_bias_two
 ):
@@ -1052,31 +1115,31 @@
     o_in_one[...] = wide(source)
     o_in_two[...] = wide(u_two)
 
-    @pl.when(step == D_IN // UNIT)
+    @pl.when(step == D_IN // SLAB)
     def _():
-        o_bias_one[...] = wide(source)[D_IN % UNIT : D_IN % UNIT + 1]
-
-    @pl.when(step == HID // UNIT)
+        o_bias_one[...] = wide(source)[D_IN % SLAB : D_IN % SLAB + 1]
+
+    @pl.when(step == HID // SLAB)
     def _():
-        o_bias_two[...] = wide(u_two)[HID % UNIT : HID % UNIT + 1]
+        o_bias_two[...] = wide(u_two)[HID % SLAB : HID % SLAB + 1]
 
 
 def finish(total, drop_one, drop_two):
     def units(first, last):
-        return pl.BlockSpec((UNIT, WIDE), lambda i: (first + jnp.minimum(i, last), 0))
+        return pl.BlockSpec((SLAB, WIDE), lambda i: (first + jnp.minimum(i, last), 0))
 
     def rows(last):
-        return pl.BlockSpec((UNIT, HID), lambda i: (jnp.minimum(i, last), 0))
+        return pl.BlockSpec((SLAB, HID), lambda i: (jnp.minimum(i, last), 0))
 
     one = pl.BlockSpec((1, HID), lambda i: (0, 0))
-    count, short = WIDE // UNIT, D_IN // UNIT
+    count, short = WIDE // SLAB - 1, D_IN // SLAB
     square, line = jax.ShapeDtypeStruct((HID, HID), jnp.float32), jax.ShapeDtypeStruct((1, HID), jnp.float32)
     return pl.pallas_call(
         finish_kernel,
-        grid=(count,),
+        grid=(count + 1,),
         in_specs=[
-            units(HP_ONE // UNIT, count), units(SOURCE // UNIT, short), units(U_TWO // UNIT, count),
-            units(HP_TWO // UNIT, count), rows(count), rows(count),
+            units(HP_ONE // SLAB, count), units(SOURCE // SLAB, short), units(U_TWO // SLAB, count),
+            units(HP_TWO // SLAB, count), rows(count), rows(count),
         ],
         out_specs=[rows(short), rows(count), one, rows(count), rows(count), one],
         out_shape=[jax.ShapeDtypeStruct((D_IN, HID), jnp.float32), square, line, square, square, line],
@@ -1091,8 +1154,16 @@
 ):
     pipe = lax.axis_index("pipe")
     bias = jnp.stack([bias_one, bias_two])
-    blocks = prepare(w_ih_one, bias, w_hh_one, drop_one, w_ih_two, w_hh_two, drop_two)
-    left, out_two, dz, dx = relay(blocks, inputs, in_mask, mid_mask, out_mask, cotangent, resets)
+    last = WIDE - UNIT
+    tails = jnp.stack([
+        jnp.pad(w_hh_one[last:] * drop_one[last:].astype(jnp.bfloat16) * weight_scale, ((0, 2), (0, 2))),
+        jnp.pad(w_hh_two[last:] * drop_two[last:].astype(jnp.bfloat16) * weight_scale, ((0, 2), (0, 2))),
+        jnp.pad(jnp.concatenate([w_ih_two[last:], bias_two[None]], 0), ((0, 1), (0, 2))),
+    ])
+    left, out_two, dz, dx, _, _ = relay(
+        w_ih_one, bias, tails, w_hh_one, drop_one, w_hh_two, drop_two, w_ih_two,
+        inputs, in_mask, mid_mask, out_mask, cotangent, resets,
+    )
     left = left.reshape(STEPS * ROWS, UNITS * UNIT)
     total = reduce_over_dp(left, dz.reshape(2, STEPS * ROWS, WIDE))
 

time: 475 us -> 466 us (0.981)
  Pallas kernels: 465 us -> 452 us
    pallas_call x3 -> x2, Pallas kernels: 357 us -> 344 us  [the longest x1 330 us: relay(): pl.pallas_call(relay_kernel, out_shape=shapes, in_specs=[whole] * 3 + [aw...]
where the time goes in v5:
time: 466 us; the launch traced here: 465 us
  Pallas kernels  452 us (97%)
  other arithmetic  9.75 us (2%)
    pallas_call x1, Pallas kernels, relay(): pl.pallas_call(relay_kernel, out_shape=shapes, in_specs=[whole] * 3 + [aw...  330 us
    pallas_call x1, Pallas kernels, reduce_over_dp(): pl.pallas_call(reduce_kernel, out_shape=jax.ShapeDtypeStruct((UNITS * UNI...  108 us
    pallas_call x1, Pallas kernels, finish(): pl.pallas_call(finish_kernel, grid=(count + 1,), in_specs=[units(HP_ONE /...  14.3 us

profile of v5, /device:TPU:32, one launch (start us, length us, event | category | flops | bytes accessed | tf_op | source)
XLA Modules:
  0.0 465.3 jit_solution(4134391489430925895)
XLA Ops:
  0.6 0.0 slice-start
  0.7 0.8 fusion.13
  1.5 0.7 stack.22
  2.2 0.7 stack.21
  2.9 0.6 pad_maximum_fusion.1.bias
  3.5 1.2 fusion.9
  4.7 1.2 fusion.11
  5.9 0.0 slice-done
  5.9 0.1 fusion.7
  6.0 1.0 pad_maximum_fusion.tails
  7.0 329.6 %relay.1 = (bf16[44,8,4096]{2,1,0:T(8,128)(2,1)}, bf16[44,8,1152]{2,1,0:T(8,128)(2,1)}, bf16[2,44,8,1152]{3,2,1,0:T(8,128)(2,1)}, f32[352,128]{1,0:T(8,128)}, bf...) custom-call(bf16[400,1150]{1,0:T(8,128)(2,1)} %w_one.1, bf16[2,1150]{1,0:T(2,128)(2,1)} %pad_maximum_fusion.1.bias, ...), custom_call_target="tpu_custom_call" | custom-call | tf_op jit(solution)/shard_map/relay/pallas_call | solution.py:777
  336.6 0.0 copy-start
  336.6 1.5 fusion
  338.2 0.3 reshape.34
  338.5 0.3 constant_dynamic-slice_fusion
  338.8 0.8 copy.29
  339.6 0.0 copy-done
  339.6 0.7 fusion.12
  340.3 108.1 %reduce.3.hp_one.source.u_two.hp_two = bf16[4096,1152]{1,0:T(8,128)(2,1)} custom-call(bf16[352,4096]{1,0:T(8,128)(2,1)} %bitcast.25, bf16[2,352,1152]{2,1,0:T(8,128)(2,1)} %bitcast.27), custom_call_target="tpu_custom_call" | custom-call | tf_op jit(solution)/shard_map/reduce/pallas_call | solution.py:1082
  448.3 14.3 %finish.1 = (f32[400,1150]{1,0:T(8,128)}, f32[1150,1150]{1,0:T(8,128)}, f32[1,1150]{1,0:T(1,128)}, f32[1150,1150]{1,0:T(8,128)}, f32[1150,1150]{1,0:T(8,128)}, /*index=5*/f32[1,1150]{1,0:T(1,128)}) custom-call(bf16[4096,1152]{1,0:T(8,128)(2,1)} %reduce.3.hp_one.source.u_two.hp_two, bf16[4096,1152]{1,0:T(8,128)(2,1)} %reduce.3.hp_one.source.u_two.hp_two, ...), custom_call_target="tpu_custom_call" | custom-call | tf_op jit(solution)/shard_map/finish/pallas_call | solution.py:1137
  462.7 1.3 reduce.1
  464.0 1.3 reduce.2
  (1 shorter events, 0.0 us)
Async XLA Ops:
  0.6 5.3 %slice-start = ((bf16[1150,1150]{1,0:T(8,128)(2,1)}), bf16[126,1150]{1,0:T(8,128)(2,1)S(1)}, s32[]{:S(2)}) async-start(bf16[1150,1150]{1,0:T(8,128)(2,1)} %w_two.1), calls=%async_computation | async-start | bytes 589824 | tf_op jit(solution)/shard_map/slice | solution.py:1161
  336.6 2.9 copy-start

commit v6 on v5

--- a/solution.py
+++ b/solution.py
@@ -57,10 +57,10 @@
 
 
 def relay_kernel(
-    w_one, bias, tails, r_one, drop_one, r_two, drop_two, w_two,
+    plain_in, tails, r_one, drop_one, r_two, drop_two, w_two,
     inputs, in_mask, mid_mask, out_mask, cotangent, resets,
     o_left, o_out, o_dz, o_dx, turned, turned_in,
-    raw_weights, raw_drop, raw_sem, plain, plain_in, turn, small, apart, turn_sem,
+    raw_weights, raw_drop, raw_sem, plain, turn, small, apart, turn_sem,
     w_front, w_back, zx, extra, dz, du, dx, above, line, spread, keep, layer_keep, hidden, cell, stage_a, stage_b, stage_z,
     block_send, block_recv, block_local, cross_send, cross_recv, ring_send, ring_recv, go_on,
     u_send, u_recv, z_send, z_recv, dz_send, dz_recv, du_send, du_recv,
@@ -150,13 +150,6 @@
         rows = pl.ds(pl.multiple_of(i * UNIT, UNIT), UNIT)
         return pltpu.make_async_copy(turn.at[slot, :, pl.ds(0, 512)], turned_in.at[rows], turn_sem.at[slot])
 
-    def make_plain_in():
-        plain_in[...] = jnp.zeros_like(plain_in)
-        plain_in[:D_IN, :HID] = w_one[...]
-        row = lax.broadcasted_iota(jnp.int32, (D_WIDE - D_IN, HID), 0)
-        below = jnp.where(row == 0, bias[0:1].astype(jnp.float32), 0.0)
-        plain_in[D_IN:, :HID] = below.astype(jnp.bfloat16)
-
     def make_turned_in(i, carry):
         small[...] = plain_in[:D_IN, pl.ds(pl.multiple_of(i * UNIT, UNIT), UNIT)].astype(jnp.float32)
         for q in range(4):
@@ -187,7 +180,6 @@
     def _():
         make_plain(2)
 
-    make_plain_in()
     pl.semaphore_wait(barrier, 11)
 
     blocks = {
@@ -761,7 +753,7 @@
             copy_part(me, o_dz_two, group, 0, me).wait_recv()
 
 
-def relay(w_one, bias, tails, r_one, drop_one, r_two, drop_two, w_two, inputs, in_mask, mid_mask, out_mask, cotangent, resets):
+def relay(w_one, tails, r_one, drop_one, r_two, drop_two, w_two, inputs, in_mask, mid_mask, out_mask, cotangent, resets):
     whole, away = pl.BlockSpec(memory_space=pltpu.VMEM), pl.BlockSpec(memory_space=pl.ANY)
     rows = (CHUNKS, 2 * ROWS, WIDE)
     half, full = jnp.bfloat16, jnp.float32
@@ -777,7 +769,7 @@
     return pl.pallas_call(
         relay_kernel,
         out_shape=shapes,
-        in_specs=[whole] * 3 + [away] * 5 + [whole] * 5
+        in_specs=[whole] * 2 + [away] * 5 + [whole] * 5
         + [pl.BlockSpec(memory_space=pltpu.SMEM)],
         out_specs=[whole] * 4 + [away] * 2,
         scratch_shapes=[
@@ -785,7 +777,6 @@
             pltpu.VMEM((DEEP, UNIT, HID), jnp.int32),
             dma((2, DEEP)),
             pltpu.VMEM((3, WIDE, WIDE), half),
-            pltpu.VMEM((D_WIDE, WIDE), half),
             pltpu.VMEM((2, UNIT, WIDE), half),
             pltpu.VMEM((D_IN, UNIT), full),
             pltpu.VMEM((512, UNIT), full),
@@ -816,13 +807,13 @@
             vmem_limit_bytes=60 << 20, collective_id=0, has_side_effects=True
         ),
         name="relay",
-    )(w_one, bias, tails, r_one, drop_one, r_two, drop_two, w_two, inputs, in_mask, mid_mask, out_mask, cotangent, resets)
+    )(w_one, tails, r_one, drop_one, r_two, drop_two, w_two, inputs, in_mask, mid_mask, out_mask, cotangent, resets)
 
 
 def reduce_kernel(
     left, dz, total, own, near, far, part, cross, share,
     near_send, near_recv, far_send, far_recv, part_send, part_recv, last_send, last_recv,
-    cross_send, cross_recv, back_send, back_recv, wide_send, wide_recv, share_send, share_recv,
+    cross_send, cross_recv, back_send, back_recv, wide_send, wide_recv, share_send, share_recv, own_sem,
 ):
     pipe = lax.axis_index("pipe")
     dp = lax.axis_index("dp")
@@ -853,13 +844,13 @@
     def send(source, target, s, r, to):
         return pltpu.make_async_remote_copy(source, target, s, r, device_id=to, device_id_type=MESH)
 
-    def add(target, rows, others, lanes=lanes_of[0]):
+    def add(rows, others, lanes=lanes_of[0]):
         def body(i, carry):
             span = pl.ds(pl.multiple_of(rows.start + i * 16, 16), 16)
             value = own[span, lanes].astype(jnp.float32)
             for ref in others:
                 value = value + ref[pl.ds(pl.multiple_of(i * 16, 16), 16), lanes].astype(jnp.float32)
-            target[span, lanes] = value.astype(jnp.bfloat16)
+            own[span, lanes] = value.astype(jnp.bfloat16)
             return carry
 
         lax.fori_loop(0, rows.size // 16, body, 0)
@@ -928,13 +919,16 @@
 
     def back_copy(p, d, rel=0, on=0):
         at = (p, slot[d], on)
-        ref = total.at[unit(p, 0, rel), lanes_of[0 if not on else 1 if d == 1 else 2]]
-        return send(ref, ref, back_send.at[at], back_recv.at[at], second[p](d))
+        lanes = lanes_of[0 if not on else 1 if d == 1 else 2]
+        ref = total.at[unit(p, 0, rel), lanes]
+        source = own.at[unit(p, 0, rel), lanes] if rel == 0 else ref
+        return send(source, ref, back_send.at[at], back_recv.at[at], second[p](d))
 
     def wide_copy(p, d, rel, block=0, on=0):
         at = (p, slot[d], rel + 4 * on)
         ref = total.at[unit(p, block, rel)]
-        return send(ref, ref, wide_send.at[at], wide_recv.at[at], first[p](d))
+        source = own.at[unit(p, block, rel)] if block == 0 and rel == 0 else ref
+        return send(source, ref, wide_send.at[at], wide_recv.at[at], first[p](d))
 
     def start_near(parts):
         for k in range(2):
@@ -953,13 +947,13 @@
             for p in parts:
                 for d in (1, -1):
                     near_copy(p, d, k).wait_recv()
-                    add(own, unit(p, d, side[d][k]), [near.at[p, slot[d], k]])
+                    add(unit(p, d, side[d][k]), [near.at[p, slot[d], k]])
                     go(far_copy(p, d, 2 + k))
 
     def collect(p, rel):
         for d in (1, -1):
             far_copy(p, d, (side[-d] + side[d]).index(rel), 0).wait_recv()
-        add(own, unit(p, 0, rel), [far.at[p, 0, rel], far.at[p, 1, rel]])
+        add(unit(p, 0, rel), [far.at[p, 0, rel], far.at[p, 1, rel]])
 
     def start_second(parts):
         for p in parts:
@@ -977,15 +971,19 @@
         for d in (1, -1):
             for p in parts:
                 part_copy(p, d).wait_recv()
-                add(own, unit(p, 0, d), [part.at[p, slot[d]]], lanes_of[1 if d == 1 else 2])
+                add(unit(p, 0, d), [part.at[p, slot[d]]], lanes_of[1 if d == 1 else 2])
                 go(last_copy(p, d, 1))
 
-    def finish_second(parts, target):
+    def finish_second(parts):
         for p in parts:
             for d in (1, -1):
                 for k in range(2):
                     last_copy(p, d, k).wait_recv()
-            add(target, unit(p, 0, 0), [part.at[p, 2], part.at[p, 3]])
+            add(unit(p, 0, 0), [part.at[p, 2], part.at[p, 3]])
+
+    def keep_copy(p):
+        rows = unit(p, 0, 0)
+        return pltpu.make_async_copy(own.at[rows], total.at[rows], own_sem.at[p])
 
     def start_back(parts):
         for p in parts:
@@ -993,6 +991,7 @@
                 go(back_copy(p, d))
             for d in (1, -1):
                 go(wide_copy(p, d, 0))
+            keep_copy(p).start()
 
     def pass_back(parts):
         for d in (1, -1):
@@ -1044,32 +1043,36 @@
     for i in range(4):
         share_copy(i).wait_recv()
         rows = pl.ds(pl.multiple_of(THIRD + z * SHARE + i * UNIT, UNIT), UNIT)
-        add(own, rows, [share.at[pl.ds(i * UNIT, UNIT)]])
+        add(rows, [share.at[pl.ds(i * UNIT, UNIT)]])
     start_near(small)
     start_far(small)
     start_second(big)
     finish_near(small)
     finish_part(big)
     start_second(small)
-    finish_second(big, own)
+    finish_second(big)
     for p in big:
-        go(cross_copy(p))
+        cross_copy(p).start()
     finish_part(small)
-    finish_second(small, total)
+    finish_second(small)
     start_back(small)
     pass_back(small)
     for p in big:
-        cross_copy(p).wait_recv()
-        add(total, unit(p, 0, 0), [cross.at[p]])
+        cross_copy(p).wait()
+        add(unit(p, 0, 0), [cross.at[p]])
     start_back(big)
     finish_back(small)
     pass_wide(small)
     pass_back(big)
     finish_wide(small)
+    for p in small:
+        keep_copy(p).wait()
     go(share_back(z))
     finish_back(big)
     pass_wide(big)
     finish_wide(big)
+    for p in big:
+        keep_copy(p).wait()
     share_back(1 - z).wait_recv()
     for copy in started:
         copy.wait_send()
@@ -1083,7 +1086,7 @@
         reduce_kernel,
         out_shape=jax.ShapeDtypeStruct((UNITS * UNIT, WIDE), half),
         in_specs=[whole] * 2,
-        out_specs=whole,
+        out_specs=pl.BlockSpec(memory_space=pl.ANY),
         scratch_shapes=[
             pltpu.VMEM((UNITS * UNIT, WIDE), half),
             pltpu.VMEM((4, 2, 2, BIG, WIDE), half),
@@ -1093,7 +1096,7 @@
             pltpu.VMEM((SHARE, WIDE), half),
             dma((4, 2, 2)), dma((4, 2, 2)), dma((4, 2, 4)), dma((4, 2, 4)), dma((4, 2)), dma((4, 2)),
             dma((4, 2, 2)), dma((4, 2, 2)), dma((2,)), dma((2,)), dma((4, 2, 2)), dma((4, 2, 2)),
-            dma((4, 2, 8)), dma((4, 2, 8)), dma((5,)), dma((5,)),
+            dma((4, 2, 8)), dma((4, 2, 8)), dma((5,)), dma((5,)), dma((4,)),
         ],
         compiler_params=pltpu.CompilerParams(
             vmem_limit_bytes=60 << 20, collective_id=1, has_side_effects=True
@@ -1117,11 +1120,11 @@
 
     @pl.when(step == D_IN // SLAB)
     def _():
-        o_bias_one[...] = wide(source)[D_IN % SLAB : D_IN % SLAB + 1]
+        o_bias_one[...] = wide(source)[D_IN % SLAB]
 
     @pl.when(step == HID // SLAB)
     def _():
-        o_bias_two[...] = wide(u_two)[HID % SLAB : HID % SLAB + 1]
+        o_bias_two[...] = wide(u_two)[HID % SLAB]
 
 
 def finish(total, drop_one, drop_two):
@@ -1131,9 +1134,9 @@
     def rows(last):
         return pl.BlockSpec((SLAB, HID), lambda i: (jnp.minimum(i, last), 0))
 
-    one = pl.BlockSpec((1, HID), lambda i: (0, 0))
+    one = pl.BlockSpec((HID,), lambda i: (0,))
     count, short = WIDE // SLAB - 1, D_IN // SLAB
-    square, line = jax.ShapeDtypeStruct((HID, HID), jnp.float32), jax.ShapeDtypeStruct((1, HID), jnp.float32)
+    square, line = jax.ShapeDtypeStruct((HID, HID), jnp.float32), jax.ShapeDtypeStruct((HID,), jnp.float32)
     return pl.pallas_call(
         finish_kernel,
         grid=(count + 1,),
@@ -1153,7 +1156,8 @@
     w_ih_one, w_hh_one, bias_one, drop_one, w_ih_two, w_hh_two, bias_two, drop_two, cotangent,
 ):
     pipe = lax.axis_index("pipe")
-    bias = jnp.stack([bias_one, bias_two])
+    w_one = jnp.concatenate([w_ih_one, bias_one[None]], 0)
+    w_one = jnp.pad(w_one, ((0, D_WIDE - D_IN - 1), (0, WIDE - HID)))
     last = WIDE - UNIT
     tails = jnp.stack([
         jnp.pad(w_hh_one[last:] * drop_one[last:].astype(jnp.bfloat16) * weight_scale, ((0, 2), (0, 2))),
@@ -1161,7 +1165,7 @@
         jnp.pad(jnp.concatenate([w_ih_two[last:], bias_two[None]], 0), ((0, 1), (0, 2))),
     ])
     left, out_two, dz, dx, _, _ = relay(
-        w_ih_one, bias, tails, w_hh_one, drop_one, w_hh_two, drop_two, w_ih_two,
+        w_one, tails, w_hh_one, drop_one, w_hh_two, drop_two, w_ih_two,
         inputs, in_mask, mid_mask, out_mask, cotangent, resets,
     )
     left = left.reshape(STEPS * ROWS, UNITS * UNIT)
@@ -1177,7 +1181,7 @@
     grad_input = grad_input * keep_part[:, :, None, :]
 
     in_one, rec_one, bias_one, in_two, rec_two, bias_two = finish(total, drop_one, drop_two)
-    return (layer_outputs, grad_input, in_one, rec_one, bias_one[0], in_two, rec_two, bias_two[0])
+    return (layer_outputs, grad_input, in_one, rec_one, bias_one, in_two, rec_two, bias_two)
 
 
 def solution(mesh):

time: 466 us -> 461 us (0.989)
  no operation moved by 1% of the time
where the time goes in v6:
time: 461 us
  Pallas kernels  449 us (97%)
  other arithmetic  7.64 us (2%)
    pallas_call x1, Pallas kernels, relay(): pl.pallas_call(relay_kernel, out_shape=shapes, in_specs=[whole] * 2 + [aw...  330 us
    pallas_call x1, Pallas kernels, reduce_over_dp(): pl.pallas_call(reduce_kernel, out_shape=jax.ShapeDtypeStruct((UNITS * UNI...  105 us
    pallas_call x1, Pallas kernels, finish(): pl.pallas_call(finish_kernel, grid=(count + 1,), in_specs=[units(HP_ONE /...  14.3 us

profile of v6, /device:TPU:32, one launch (start us, length us, event | category | flops | bytes accessed | tf_op | source)
XLA Modules:
  0.0 460.7 jit_solution(5929396076124663929)
XLA Ops:
  0.6 0.0 slice-start
  0.7 0.8 fusion.19
  1.5 0.7 broadcast_in_dim.10
  2.2 0.7 broadcast_in_dim.11
  2.9 1.2 fusion.15
  4.1 0.0 copy-start
  4.1 1.3 fusion.17
  5.4 0.0 slice-done
  5.4 0.1 fusion.13
  5.5 1.0 pad_maximum_fusion.tails
  6.5 0.0 copy-done
  6.5 1.0 fusion.5.plain_in
  7.5 329.7 %relay.1 = (bf16[44,8,4096]{2,1,0:T(8,128)(2,1)}, bf16[44,8,1152]{2,1,0:T(8,128)(2,1)}, bf16[2,44,8,1152]{3,2,1,0:T(8,128)(2,1)}, f32[352,128]{1,0:T(8,128)}, bf...) custom-call(bf16[416,1152]{1,0:T(8,128)(2,1)} %fusion.5.plain_in, bf16[3,128,1152]{2,1,0:T(8,128)(2,1)} %pad_maximum_fusion.tails, ...), custom_call_target="tpu_custom_call" | custom-call | tf_op jit(solution)/shard_map/relay/pallas_call | solution.py:769
  337.3 0.0 copy-start.1
  337.3 1.5 fusion.6
  338.8 0.3 reshape.34
  339.1 0.3 constant_dynamic-slice_fusion
  339.4 0.8 copy.29
  340.2 0.0 copy-done.1
  340.2 0.7 fusion.18
  340.9 105.2 %reduce.1.hp_one.source.u_two.hp_two = bf16[4096,1152]{1,0:T(8,128)(2,1)} custom-call(bf16[352,4096]{1,0:T(8,128)(2,1)} %bitcast.25, bf16[2,352,1152]{2,1,0:T(8,128)(2,1)} %bitcast.27), custom_call_target="tpu_custom_call" | custom-call | tf_op jit(solution)/shard_map/reduce/pallas_call | solution.py:1085
  446.2 14.3 %finish.1 = (f32[400,1150]{1,0:T(8,128)}, f32[1150,1150]{1,0:T(8,128)}, f32[1150]{0:T(1024)}, f32[1150,1150]{1,0:T(8,128)}, f32[1150,1150]{1,0:T(8,128)}, /*index=5*/f32[1150]{0:T(1024)}) custom-call(bf16[4096,1152]{1,0:T(8,128)(2,1)} %reduce.1.hp_one.source.u_two.hp_two, bf16[4096,1152]{1,0:T(8,128)(2,1)} %reduce.1.hp_one.source.u_two.hp_two, ...), custom_call_target="tpu_custom_call" | custom-call | tf_op jit(solution)/shard_map/finish/pallas_call | solution.py:1140
  (1 shorter events, 0.0 us)
Async XLA Ops:
  0.6 4.8 %slice-start = ((bf16[1150,1150]{1,0:T(8,128)(2,1)}), bf16[126,1150]{1,0:T(8,128)(2,1)S(1)}, s32[]{:S(2)}) async-start(bf16[1150,1150]{1,0:T(8,128)(2,1)} %w_two.1), calls=%async_computation | async-start | bytes 589824 | tf_op jit(solution)/shard_map/slice | solution.py:1165
  4.1 2.4 copy-start
  337.3 2.9 copy-start.1

commit v7 on v6

--- a/solution.py
+++ b/solution.py
@@ -1099,7 +1099,7 @@
             dma((4, 2, 8)), dma((4, 2, 8)), dma((5,)), dma((5,)), dma((4,)),
         ],
         compiler_params=pltpu.CompilerParams(
-            vmem_limit_bytes=60 << 20, collective_id=1, has_side_effects=True
+            vmem_limit_bytes=32 << 20, collective_id=1, has_side_effects=True
         ),
         name="reduce",
     )(left, dz)
@@ -1146,7 +1146,7 @@
         ],
         out_specs=[rows(short), rows(count), one, rows(count), rows(count), one],
         out_shape=[jax.ShapeDtypeStruct((D_IN, HID), jnp.float32), square, line, square, square, line],
-        compiler_params=pltpu.CompilerParams(vmem_limit_bytes=60 << 20),
+        compiler_params=pltpu.CompilerParams(vmem_limit_bytes=30 << 20),
         name="finish",
     )(total, total, total, total, drop_one, drop_two)
 

time: 461 us -> 455 us (0.987)
  Pallas kernels: 449 us -> 439 us
    pallas_call x1, Pallas kernels: 14.3 us -> 6.94 us  [finish(): pl.pallas_call(finish_kernel, grid=(count + 1,), in_specs=[units(HP_ONE /...]
where the time goes in v7:
time: 455 us
  Pallas kernels  439 us (96%)
  other arithmetic  8.64 us (2%)
  local copies, waits for them, and re-layouts  6.54 us (1%)
    pallas_call x1, Pallas kernels, relay(): pl.pallas_call(relay_kernel, out_shape=shapes, in_specs=[whole] * 2 + [aw...  330 us
    pallas_call x1, Pallas kernels, reduce_over_dp(): pl.pallas_call(reduce_kernel, out_shape=jax.ShapeDtypeStruct((UNITS * UNI...  102 us

profile of v7, /device:TPU:32, one launch (start us, length us, event | category | flops | bytes accessed | tf_op | source)
XLA Modules:
  0.0 455.0 jit_solution(5374307294280400823)
XLA Ops:
  0.6 0.0 slice-start.4
  0.7 0.8 fusion.19
  1.5 0.7 broadcast_in_dim.10
  2.2 0.7 broadcast_in_dim.11
  2.9 1.2 fusion.15
  4.1 0.0 copy-start.2
  4.1 1.3 fusion.17
  5.4 0.0 slice-done.4
  5.4 0.1 fusion.13
  5.5 1.0 pad_maximum_fusion.tails
  6.5 0.0 copy-done.2
  6.5 1.0 fusion.5.plain_in
  7.5 329.7 %relay.1 = (bf16[44,8,4096]{2,1,0:T(8,128)(2,1)}, bf16[44,8,1152]{2,1,0:T(8,128)(2,1)}, bf16[2,44,8,1152]{3,2,1,0:T(8,128)(2,1)}, f32[352,128]{1,0:T(8,128)}, bf...) custom-call(bf16[416,1152]{1,0:T(8,128)(2,1)} %fusion.5.plain_in, bf16[3,128,1152]{2,1,0:T(8,128)(2,1)} %pad_maximum_fusion.tails, ...), custom_call_target="tpu_custom_call" | custom-call | tf_op jit(solution)/shard_map/relay/pallas_call | solution.py:769
  337.3 0.0 copy-start.3
  337.3 0.0 copy-start
  337.3 2.5 fusion.6
  339.8 2.9 reshape.34
  342.7 0.0 copy-start.1
  342.7 1.4 constant_dynamic-slice_fusion
  344.1 0.0 slice-start
  344.1 0.0 slice-start.2
  344.1 0.8 copy.29
  344.9 0.0 copy-done.3
  344.9 0.7 fusion.18
  345.6 0.0 copy-done
  345.6 0.0 copy-done.1
  345.6 0.0 slice-start.1
  345.6 0.0 slice-start.3
  345.6 102.2 %reduce.1.hp_one.source.u_two.hp_two = bf16[4096,1152]{1,0:T(8,128)(2,1)S(1)} custom-call(bf16[352,4096]{1,0:T(8,128)(2,1)S(1)} %bitcast.29, bf16[2,352,1152]{2,1,0:T(8,128)(2,1)S(1)} %bitcast.30), custom_call_target="tpu_custom_call" | custom-call | tf_op jit(solution)/shard_map/reduce/pallas_call | solution.py:1085
  447.9 0.0 slice-done
  447.9 0.0 slice-done.2
  447.9 0.0 slice-done.1
  447.9 0.0 slice-done.3
  447.9 6.9 %finish.1 = (f32[400,1150]{1,0:T(8,128)}, f32[1150,1150]{1,0:T(8,128)}, f32[1150]{0:T(1024)}, f32[1150,1150]{1,0:T(8,128)}, f32[1150,1150]{1,0:T(8,128)}, /*index=5*/f32[1150]{0:T(1024)}) custom-call(bf16[4096,1152]{1,0:T(8,128)(2,1)S(1)} %reduce.1.hp_one.source.u_two.hp_two, bf16[4096,1152]{1,0:T(8,128)(2,1)S(1)} %reduce.1.hp_one.source.u_two.hp_two, ...), custom_call_target="tpu_custom_call" | custom-call | tf_op jit(solution)/shard_map/finish/pallas_call | solution.py:1140
  (3 shorter events, 0.0 us)
Async XLA Ops:
  0.6 4.8 %slice-start.4 = ((bf16[1150,1150]{1,0:T(8,128)(2,1)}), bf16[126,1150]{1,0:T(8,128)(2,1)S(1)}, s32[]{:S(2)}) async-start(bf16[1150,1150]{1,0:T(8,128)(2,1)} %w_two.1), calls=%async_computation.4 | async-start | bytes 589824 | tf_op jit(solution)/shard_map/slice | solution.py:1165
  4.1 2.4 copy-start.2
  337.3 7.7 %copy-start.3 = (f32[352,128]{1,0:T(8,128)S(1)}, f32[352,128]{1,0:T(8,128)}, u32[]{:S(2)}) copy-start(f32[352,128]{1,0:T(8,128)} %get-tuple-element.20) | copy-start | bytes 540676
  337.3 8.3 %copy-start = (bf16[44,8,4096]{2,1,0:T(8,128)(2,1)S(1)}, bf16[44,8,4096]{2,1,0:T(8,128)(2,1)}, u32[]{:S(2)}) copy-start(bf16[44,8,4096]{2,1,0:T(8,128)(2,1)} %get-tuple-element.18) | copy-start | bytes 8650756
  342.7 2.9 copy-start.1
  344.1 103.8 %slice-start = ((s8[5308416]{0:T(1024)(128)(4,1)}), s8[4194304]{0:T(1024)(128)(4,1)S(1)}, s32[]{:S(2)}) async-start(s8[5308416]{0:T(1024)(128)(4,1)} %bitcast.24), calls=%async_computation | async-start | bytes 8388608
  344.1 103.8 %slice-start.2 = ((s8[5308416]{0:T(1024)(128)(4,1)}), s8[4194304]{0:T(1024)(128)(4,1)S(1)}, s32[]{:S(2)}) async-start(s8[5308416]{0:T(1024)(128)(4,1)} %bitcast.26), calls=%async_computation.2 | async-start | bytes 8388608
  345.6 102.3 %slice-start.1 = ((s8[5308416]{0:T(1024)(128)(4,1)}), s8[1114112]{0:T(1024)(128)(4,1)S(1)}, s32[]{:S(2)}) async-start(s8[5308416]{0:T(1024)(128)(4,1)} %bitcast.24), calls=%async_computation.1 | async-start | bytes 2228224
  345.6 102.3 %slice-start.3 = ((s8[5308416]{0:T(1024)(128)(4,1)}), s8[1114112]{0:T(1024)(128)(4,1)S(1)}, s32[]{:S(2)}) async-start(s8[5308416]{0:T(1024)(128)(4,1)} %bitcast.26), calls=%async_computation.3 | async-start | bytes 2228224

commit v8 on v7

--- a/solution.py
+++ b/solution.py
@@ -521,6 +521,7 @@
         def ahead(c, carry):
             forward_pair(c, layer_keep[0], True, o_hp_one, o_u)
             copy_u(c).start()
+            o_out[c] = stage_b[...].astype(jnp.bfloat16)
 
             @pl.when((c >= LATER) & (c < LATER + TURNS))
             def _():
@@ -714,6 +715,10 @@
 
         lax.fori_loop(0, TURNS, pass_on, 0)
         start_near(me)
+        copy_bulk(me, o_u, 0, 0).wait_recv()
+        mine = pltpu.make_async_copy(o_u, o_out, local_sem.at[0])
+        mine.start()
+        mine.wait()
         await_blocks(W_ONE_T)
 
         def behind(i, carry):
@@ -746,7 +751,6 @@
         own.wait()
         own_dx.wait()
 
-        copy_bulk(me, o_u, 0, 0).wait_recv()
         copy_bulk(me, o_hp_one, 0, 1).wait_recv()
         copy_bulk(me, o_hp_two, 0, 2).wait_recv()
         for group in range(groups):
@@ -1164,15 +1168,14 @@
         jnp.pad(w_hh_two[last:] * drop_two[last:].astype(jnp.bfloat16) * weight_scale, ((0, 2), (0, 2))),
         jnp.pad(jnp.concatenate([w_ih_two[last:], bias_two[None]], 0), ((0, 1), (0, 2))),
     ])
-    left, out_two, dz, dx, _, _ = relay(
+    left, layer, dz, dx, _, _ = relay(
         w_one, tails, w_hh_one, drop_one, w_hh_two, drop_two, w_ih_two,
         inputs, in_mask, mid_mask, out_mask, cotangent, resets,
     )
     left = left.reshape(STEPS * ROWS, UNITS * UNIT)
     total = reduce_over_dp(left, dz.reshape(2, STEPS * ROWS, WIDE))
 
-    u_two = left[:, U_TWO : U_TWO + WIDE].reshape(out_two.shape)
-    layer = jnp.where(pipe < 2, u_two, out_two).reshape(STEPS, 2, 2, WIDE)[..., :HID]
+    layer = layer.reshape(STEPS, 2, 2, WIDE)[..., :HID]
     layer = lax.dynamic_index_in_dim(layer, pipe % 2, 1, keepdims=False)
     layer_outputs = jnp.swapaxes(layer, 0, 1)[None]
     grad_input = jnp.transpose(dx.reshape(STEPS, 2, 2, 128)[..., :100], (1, 2, 0, 3))

time: 455 us -> 456 us (level)
  no operation moved by 1% of the time
where the time goes in v8:
time: 456 us; the launch traced here: 455 us
  Pallas kernels  439 us (96%)
  local copies, waits for them, and re-layouts  8 us (2%)
  other arithmetic  7.58 us (2%)
    pallas_call x1, Pallas kernels, relay(): pl.pallas_call(relay_kernel, out_shape=shapes, in_specs=[whole] * 2 + [aw...  330 us
    pallas_call x1, Pallas kernels, reduce_over_dp(): pl.pallas_call(reduce_kernel, out_shape=jax.ShapeDtypeStruct((UNITS * UNI...  102 us

profile of v8, /device:TPU:32, one launch (start us, length us, event | category | flops | bytes accessed | tf_op | source)
XLA Modules:
  0.0 455.2 jit_solution(5955252886996634298)
XLA Ops:
  0.6 0.0 slice-start.4
  0.7 0.8 fusion.18
  1.5 0.7 broadcast_in_dim.10
  2.2 0.7 broadcast_in_dim.11
  2.9 1.2 fusion.14
  4.1 0.0 copy-start.2
  4.1 1.3 fusion.16
  5.4 0.0 slice-done.4
  5.4 0.1 fusion.12
  5.5 1.0 pad_maximum_fusion.tails
  6.5 0.0 copy-done.2
  6.5 1.0 fusion.5.plain_in
  7.5 329.7 %relay.1 = (bf16[44,8,4096]{2,1,0:T(8,128)(2,1)}, bf16[44,8,1152]{2,1,0:T(8,128)(2,1)}, bf16[2,44,8,1152]{3,2,1,0:T(8,128)(2,1)}, f32[352,128]{1,0:T(8,128)}, bf...) custom-call(bf16[416,1152]{1,0:T(8,128)(2,1)} %fusion.5.plain_in, bf16[3,128,1152]{2,1,0:T(8,128)(2,1)} %pad_maximum_fusion.tails, ...), custom_call_target="tpu_custom_call" | custom-call | tf_op jit(solution)/shard_map/relay/pallas_call | solution.py:773
  337.3 0.0 copy-start
  337.3 3.0 reshape.29
  340.3 1.3 constant_dynamic-slice_fusion
  341.6 0.0 slice-start
  341.6 0.0 slice-start.2
  341.6 0.8 copy.29
  342.4 2.2 fusion.17
  344.6 0.0 copy-done
  344.6 0.0 copy-start.1
  344.6 1.4 copy-done.1
  346.0 0.0 slice-start.1
  346.0 0.0 slice-start.3
  346.0 102.1 %reduce.1.hp_one.source.u_two.hp_two = bf16[4096,1152]{1,0:T(8,128)(2,1)S(1)} custom-call(bf16[352,4096]{1,0:T(8,128)(2,1)S(1)} %bitcast.24, bf16[2,352,1152]{2,1,0:T(8,128)(2,1)S(1)} %bitcast.25), custom_call_target="tpu_custom_call" | custom-call | tf_op jit(solution)/shard_map/reduce/pallas_call | solution.py:1089
  448.1 0.0 slice-done
  448.1 0.0 slice-done.2
  448.1 0.0 slice-done.1
  448.1 0.0 slice-done.3
  448.2 6.9 %finish.1 = (f32[400,1150]{1,0:T(8,128)}, f32[1150,1150]{1,0:T(8,128)}, f32[1150]{0:T(1024)}, f32[1150,1150]{1,0:T(8,128)}, f32[1150,1150]{1,0:T(8,128)}, /*index=5*/f32[1150]{0:T(1024)}) custom-call(bf16[4096,1152]{1,0:T(8,128)(2,1)S(1)} %reduce.1.hp_one.source.u_two.hp_two, bf16[4096,1152]{1,0:T(8,128)(2,1)S(1)} %reduce.1.hp_one.source.u_two.hp_two, ...), custom_call_target="tpu_custom_call" | custom-call | tf_op jit(solution)/shard_map/finish/pallas_call | solution.py:1144
  (3 shorter events, 0.0 us)
Async XLA Ops:
  0.6 4.8 %slice-start.4 = ((bf16[1150,1150]{1,0:T(8,128)(2,1)}), bf16[126,1150]{1,0:T(8,128)(2,1)S(1)}, s32[]{:S(2)}) async-start(bf16[1150,1150]{1,0:T(8,128)(2,1)} %w_two.1), calls=%async_computation.4 | async-start | bytes 589824 | tf_op jit(solution)/shard_map/slice | solution.py:1169
  4.1 2.4 copy-start.2
  337.3 7.3 %copy-start = (bf16[44,8,4096]{2,1,0:T(8,128)(2,1)S(1)}, bf16[44,8,4096]{2,1,0:T(8,128)(2,1)}, u32[]{:S(2)}) copy-start(bf16[44,8,4096]{2,1,0:T(8,128)(2,1)} %get-tuple-element.20) | copy-start | bytes 8650756
  341.6 106.5 %slice-start = ((s8[5308416]{0:T(1024)(128)(4,1)}), s8[4194304]{0:T(1024)(128)(4,1)S(1)}, s32[]{:S(2)}) async-start(s8[5308416]{0:T(1024)(128)(4,1)} %bitcast.20), calls=%async_computation | async-start | bytes 8388608
  341.6 106.5 %slice-start.2 = ((s8[5308416]{0:T(1024)(128)(4,1)}), s8[4194304]{0:T(1024)(128)(4,1)S(1)}, s32[]{:S(2)}) async-start(s8[5308416]{0:T(1024)(128)(4,1)} %bitcast.22), calls=%async_computation.2 | async-start | bytes 8388608
  344.6 1.4 copy-start.1
  346.0 102.1 %slice-start.1 = ((s8[5308416]{0:T(1024)(128)(4,1)}), s8[1114112]{0:T(1024)(128)(4,1)S(1)}, s32[]{:S(2)}) async-start(s8[5308416]{0:T(1024)(128)(4,1)} %bitcast.20), calls=%async_computation.1 | async-start | bytes 2228224
  346.0 102.1 %slice-start.3 = ((s8[5308416]{0:T(1024)(128)(4,1)}), s8[1114112]{0:T(1024)(128)(4,1)S(1)}, s32[]{:S(2)}) async-start(s8[5308416]{0:T(1024)(128)(4,1)} %bitcast.22), calls=%async_computation.3 | async-start | bytes 2228224
